TPU v7x, 256 devices: a whole 4x4x8 slice. The times are simulated.
256 devices in a mesh: mem: 8 (over x, core), state: 32 (over y, z).
Axes of the slice: x: 4, y: 4, z: 8, core: 2. Of those that a mesh axis runs over, the one named last changes fastest.
Arguments:
- prior_realizations: bfloat16 [64, 4, 2048, 512], P('mem', None, 'state'), may hold values from -6 to 6
- latent_stencil_weights: bfloat16 [128, 36], replicated, may hold values from -1 to 1
- latent_offset: float32 [128], replicated, may hold values from -3 to 3
- output_mixing_matrix: bfloat16 [4, 128], replicated, may hold values from -0.5 to 0.5
- transform: float32 [64, 64], replicated, may hold values from -0.35 to 1.35
- mean_weights: float32 [64], replicated, may hold values from -0.3 to 0.3
- obs_index: int32 [32, 8, 16], P('state', 'mem'), may hold values from 0 to 127, as said below
- obs_values: float32 [32, 8, 16, 128], P('state', 'mem'), may hold values from -6 to 6
- obs_precision: float32 [32, 8, 16, 128], P('state', 'mem'), may hold values from 0.083333333 to 3
Outputs:
- analysis: bfloat16 [64, 4, 2048, 512], P('mem', None, 'state')
- gram: float32 [64, 64], replicated
- proj: float32 [64], replicated
Inputs may be any that keep to these rules, and one draw needn't show every extreme that they name: `obs_index`: in each device's list, entry j lies from j * 8 to (j + 1) * 8 - 1.
All inputs are finite; a program needn't handle non-finite values.
Results may differ from a plain program's by a relative error of at most 0.0053.
Values may be sent and summed in bfloat16 or wider, within the bound.
No kernel may reach another device: no remote copies, remote signals or barrier semaphores. Data moves between devices by JAX's collectives and lax.ppermute only.
A program may use at most 64 MiB of HBM per device.

v0:
```python
import math

import jax
import jax.numpy as jnp
from jax import lax
from jax.sharding import PartitionSpec as P


def padded(block, sides, width):
    for axis, dim in sides:
        count = lax.axis_size(axis)
        forward = [(i, i + 1) for i in range(count - 1)]
        backward = [(target, source) for source, target in forward]
        low = lax.ppermute(
            lax.slice_in_dim(block, block.shape[dim] - width, None, axis=dim), axis, forward
        )
        high = lax.ppermute(lax.slice_in_dim(block, 0, width, axis=dim), axis, backward)
        block = jnp.concatenate([low, block, high], axis=dim)
    return block


def ensemble_sums(observed_rows, values, precision_rows):
    member_count = observed_rows.shape[0]
    observed = observed_rows.reshape(member_count, -1).astype(jnp.float32)
    obs_mean = jnp.mean(observed, axis=0)
    spread = observed - obs_mean
    weights_flat = precision_rows.reshape(-1)
    gram_part = jnp.dot(spread * weights_flat, spread.T, precision=lax.Precision.HIGHEST)
    innovation = weights_flat * (values.reshape(-1) - obs_mean)
    proj_part = jnp.dot(spread, innovation, precision=lax.Precision.HIGHEST)
    return lax.psum((gram_part, proj_part), ("mem", "state"))


def observed_states(realization_vectors, obs_index):
    member_count = realization_vectors.shape[0]
    blocked = realization_vectors.reshape(member_count, -1, 128)
    return jnp.take(blocked, obs_index[0, 0], axis=1)


def shards(
    prior_realizations,
    latent_stencil_weights,
    latent_offset,
    output_mixing_matrix,
    transform,
    mean_weights,
    obs_index,
    obs_values,
    obs_precision,
):
    local_members, fields, row_count, col_count = prior_realizations.shape
    groups = lax.axis_size("mem")
    member_total = local_members * groups
    bordered_vector = padded(prior_realizations, (("state", 2),), 1)
    bordered_vector = jnp.pad(bordered_vector, ((0, 0), (0, 0), (0, 0), (1, 1)))

    def propagate_realizations(member_pair):
        framed, realization_vector = member_pair
        patches = jnp.concatenate(
            [
                framed[:, row_off : row_off + row_count, col_off : col_off + col_count]
                for row_off in range(3)
                for col_off in range(3)
            ],
            axis=0,
        )
        patches = patches.reshape(9 * fields, row_count * col_count)
        before = (
            jnp.dot(latent_stencil_weights, patches, preferred_element_type=jnp.float32)
            + latent_offset[:, None]
        )
        hidden = jax.nn.gelu(before, approximate=True).astype(jnp.bfloat16)
        increment = jnp.dot(output_mixing_matrix, hidden, preferred_element_type=jnp.float32)
        return (
            realization_vector.astype(jnp.float32) + increment.reshape(realization_vector.shape)
        ).astype(jnp.bfloat16)

    predicted_realizations = lax.map(propagate_realizations, (bordered_vector, prior_realizations))
    combined = transform + mean_weights[:, None]
    realization_vectors = lax.all_to_all(
        predicted_realizations, "mem", split_axis=2, concat_axis=0, tiled=True
    )
    observed_rows = observed_states(realization_vectors, obs_index)
    flat_states = realization_vectors.reshape(member_total, -1).astype(jnp.float32)
    state_mean = jnp.mean(flat_states, axis=0)
    moved = state_mean + jnp.dot(
        combined.T, flat_states - state_mean, precision=lax.Precision.HIGHEST
    )
    moved = moved.astype(jnp.bfloat16).reshape(realization_vectors.shape)
    analysis = lax.all_to_all(moved, "mem", split_axis=0, concat_axis=2, tiled=True)
    gram_sum, proj_sum = ensemble_sums(observed_rows, obs_values, obs_precision)
    obs_count = obs_values.size * groups * lax.axis_size("state")
    gram = gram_sum / obs_count
    proj = proj_sum / math.sqrt(obs_count)
    return (analysis, gram, proj)


def solution(mesh):
    return jax.shard_map(
        shards,
        mesh=mesh,
        in_specs=(
            P("mem", None, "state", None),
            P(),
            P(),
            P(),
            P(),
            P(),
            P("state", "mem", None),
            P("state", "mem", None, None),
            P("state", "mem", None, None),
        ),
        out_specs=(P("mem", None, "state", None), P(), P()),
        check_vma=False,
    )
```

profile of v0, /device:TPU:24, one launch (start us, length us, event | category | flops | bytes accessed | tf_op | source)
XLA Modules:
  0.0 273.9 jit_solution(16982058579253469306)
XLA Ops:
  1.8 4.0 %collective-permute-start = (bf16[8,4,1,512]{3,2,1,0:T(2,128)(2,1)S(1)}, bf16[8,4,1,512]{3,2,1,0:T(2,128)(2,1)S(1)}, u32[]{:S(2)}, u32[]{:S(2)}) collective-permute-start(bf16[8,4,1,512]{3,2,1,0:T(2,128)(2,1)S(1)} %get-tuple-element.59), channel_id=1, source_target_pairs={{0,1},{1,2},{2,3},{3,4},{4,5},{5,6},{6,7},{7,8},{8,9},{9,10},{10,1... | collective-permute-start | bytes 98312 | tf_op jit(solution)/shard_map/ppermute | solution.py:14
  5.8 6.0 %collective-permute-start.1 = (bf16[8,4,1,512]{3,2,1,0:T(2,128)(2,1)S(1)}, bf16[8,4,1,512]{3,2,1,0:T(2,128)(2,1)S(1)}, u32[]{:S(2)}, u32[]{:S(2)}) collective-permute-start(bf16[8,4,1,512]{3,2,1,0:T(2,128)(2,1)S(1)} %get-tuple-element.60), channel_id=1, source_target_pairs={{1,0},{2,1},{3,2},{4,3},{5,4},{6,5},{7,6},{8,7},{9,8},{10,9},{11,1... | collective-permute-start | bytes 98312 | tf_op jit(solution)/shard_map/ppermute | solution.py:17
  12.1 1.6 collective-permute-done.1
  13.7 5.3 %fusion.22 = bf16[8,4,66,514]{3,2,1,0:T(8,128)(2,1)} fusion(bf16[8,4,1,512]{3,2,1,0:T(2,128)(2,1)S(1)} %collective-permute-done.1, bf16[8,4,64,512]{3,2,1,0:T(8,128)(2,1)} %param.11, bf16[8,4,1,512]{3,2,1,0:T(2,128)(2,1)S(1)} %collective-permute-done), kind=kLoop, calls=%fused_computation.40 | loop fusion | flops 13026816 | bytes 4333824 | tf_op jit(solution)/shard_map/concatenate | solution.py:18
  19.0 102.0 %while.10 = (s32[]{:T(128)}, bf16[8,4,64,512]{3,1,0,2:T(4,128)(2,1)}, bf16[8,4,64,512]{3,2,1,0:T(8,128)(2,1)}, bf16[8,4,66,514]{3,2,1,0:T(8,128)(2,1)}, bf16[128...) while((s32[]{:T(128)}, ...), condition=%wide.region_1.2_spmd, body=%wide.region_0.1_spmd.sunk | while | flops 377880576 | bytes 19952308 | solution.py:78
  21.5 1.5 copy.49
  23.1 6.7 %fusion.50 = f32[32768,4]{0,1:T(4,128)S(1)} fusion(bf16[4,128]{1,0:T(4,128)(2,1)S(1)} %get-tuple-element.128, bf16[36,32768]{1,0:T(8,128)(2,1)S(1)} %bitcast.101, bf16[128,36]{0,1:T(8,128)(2,1)S(1)} %get-tuple-element.126, f32[128]{0:T(128)S(1)} %get-tuple-element.127), kind=kOutput, calls=%fused_computation.12.clone.1 | convolution fusion | flops 377487360 | bytes 2894336 | tf_op jit(solution)/shard_map/while/body/eval_jaxpr/dot_general | solution.py:73
  34.3 1.5 copy.49
  35.8 6.7 %fusion.50 = f32[32768,4]{0,1:T(4,128)S(1)} fusion(bf16[4,128]{1,0:T(4,128)(2,1)S(1)} %get-tuple-element.128, bf16[36,32768]{1,0:T(8,128)(2,1)S(1)} %bitcast.101, bf16[128,36]{0,1:T(8,128)(2,1)S(1)} %get-tuple-element.126, f32[128]{0:T(128)S(1)} %get-tuple-element.127), kind=kOutput, calls=%fused_computation.12.clone.1 | convolution fusion | flops 377487360 | bytes 2894336 | tf_op jit(solution)/shard_map/while/body/eval_jaxpr/dot_general | solution.py:73
  47.0 1.5 copy.49
  48.6 6.7 %fusion.50 = f32[32768,4]{0,1:T(4,128)S(1)} fusion(bf16[4,128]{1,0:T(4,128)(2,1)S(1)} %get-tuple-element.128, bf16[36,32768]{1,0:T(8,128)(2,1)S(1)} %bitcast.101, bf16[128,36]{0,1:T(8,128)(2,1)S(1)} %get-tuple-element.126, f32[128]{0:T(128)S(1)} %get-tuple-element.127), kind=kOutput, calls=%fused_computation.12.clone.1 | convolution fusion | flops 377487360 | bytes 2894336 | tf_op jit(solution)/shard_map/while/body/eval_jaxpr/dot_general | solution.py:73
  59.8 1.5 copy.49
  61.3 6.7 %fusion.50 = f32[32768,4]{0,1:T(4,128)S(1)} fusion(bf16[4,128]{1,0:T(4,128)(2,1)S(1)} %get-tuple-element.128, bf16[36,32768]{1,0:T(8,128)(2,1)S(1)} %bitcast.101, bf16[128,36]{0,1:T(8,128)(2,1)S(1)} %get-tuple-element.126, f32[128]{0:T(128)S(1)} %get-tuple-element.127), kind=kOutput, calls=%fused_computation.12.clone.1 | convolution fusion | flops 377487360 | bytes 2894336 | tf_op jit(solution)/shard_map/while/body/eval_jaxpr/dot_general | solution.py:73
  72.5 1.5 copy.49
  74.1 6.7 %fusion.50 = f32[32768,4]{0,1:T(4,128)S(1)} fusion(bf16[4,128]{1,0:T(4,128)(2,1)S(1)} %get-tuple-element.128, bf16[36,32768]{1,0:T(8,128)(2,1)S(1)} %bitcast.101, bf16[128,36]{0,1:T(8,128)(2,1)S(1)} %get-tuple-element.126, f32[128]{0:T(128)S(1)} %get-tuple-element.127), kind=kOutput, calls=%fused_computation.12.clone.1 | convolution fusion | flops 377487360 | bytes 2894336 | tf_op jit(solution)/shard_map/while/body/eval_jaxpr/dot_general | solution.py:73
  85.3 1.5 copy.49
  86.8 6.7 %fusion.50 = f32[32768,4]{0,1:T(4,128)S(1)} fusion(bf16[4,128]{1,0:T(4,128)(2,1)S(1)} %get-tuple-element.128, bf16[36,32768]{1,0:T(8,128)(2,1)S(1)} %bitcast.101, bf16[128,36]{0,1:T(8,128)(2,1)S(1)} %get-tuple-element.126, f32[128]{0:T(128)S(1)} %get-tuple-element.127), kind=kOutput, calls=%fused_computation.12.clone.1 | convolution fusion | flops 377487360 | bytes 2894336 | tf_op jit(solution)/shard_map/while/body/eval_jaxpr/dot_general | solution.py:73
  99.6 6.7 %fusion.50 = f32[32768,4]{0,1:T(4,128)S(1)} fusion(bf16[4,128]{1,0:T(4,128)(2,1)S(1)} %get-tuple-element.128, bf16[36,32768]{1,0:T(8,128)(2,1)S(1)} %bitcast.101, bf16[128,36]{0,1:T(8,128)(2,1)S(1)} %get-tuple-element.126, f32[128]{0:T(128)S(1)} %get-tuple-element.127), kind=kOutput, calls=%fused_computation.12.clone.1 | convolution fusion | flops 377487360 | bytes 2894336 | tf_op jit(solution)/shard_map/while/body/eval_jaxpr/dot_general | solution.py:73
  110.8 1.5 copy.49
  112.3 6.7 %fusion.50 = f32[32768,4]{0,1:T(4,128)S(1)} fusion(bf16[4,128]{1,0:T(4,128)(2,1)S(1)} %get-tuple-element.128, bf16[36,32768]{1,0:T(8,128)(2,1)S(1)} %bitcast.101, bf16[128,36]{0,1:T(8,128)(2,1)S(1)} %get-tuple-element.126, f32[128]{0:T(128)S(1)} %get-tuple-element.127), kind=kOutput, calls=%fused_computation.12.clone.1 | convolution fusion | flops 377487360 | bytes 2894336 | tf_op jit(solution)/shard_map/while/body/eval_jaxpr/dot_general | solution.py:73
  121.0 31.8 %all_to_all.33 = bf16[8,4,64,512]{3,1,0,2:T(4,128)(2,1)S(1)} all-to-all(bf16[8,4,64,512]{3,1,0,2:T(4,128)(2,1)} %get-tuple-element.40), channel_id=1, replica_groups=mesh['mem'=8,'state'=32] {'mem'}, dimensions={2} | all-to-all | bytes 4194304 | tf_op jit(solution)/shard_map/all_to_all | solution.py:80
  152.8 2.5 convert_reduce_fusion
  155.3 5.3 %copy_bitcast_fusion.1 = (bf16[8,8,4,8,512]{4,3,2,1,0:T(8,128)(2,1)}, f32[8,8,4,8,512]{4,3,2,1,0:T(8,128)}) fusion(bf16[8,4,8,8,512]{4,1,0,3,2:T(4,128)(2,1)S(1)} %bitcast.103), kind=kLoop, calls=%fused_computation.42 | loop fusion | flops 1048576 | bytes 8388608 | tf_op jit(solution)/shard_map/all_to_all | solution.py:80
  160.7 5.0 %reshape.178 = f32[64,16384]{1,0:T(8,128)} reshape(f32[8,8,4,8,512]{4,3,2,1,0:T(8,128)} %get-tuple-element.58) | data formatting | bytes 8388608 | tf_op jit(solution)/shard_map/convert_element_type | solution.py:84
  165.7 6.3 %fusion.15 = bf16[64,16384]{1,0:T(8,128)(2,1)S(1)} fusion(f32[64,16384]{1,0:T(8,128)} %reshape.178, f32[16384]{0:T(1024)S(1)} %bitcast.109, f32[64,64]{1,0:T(8,128)S(1)} %copy-done, f32[64]{0:T(128)S(1)} %copy-done.3), kind=kOutput, calls=%fused_computation.31 | convolution fusion | flops 808456192 | bytes 6373632 | tf_op jit(solution)/shard_map/dot_general | solution.py:86
  171.9 2.1 copy.30
  174.1 4.0 %all-to-all-start.1 = ((bf16[64,4,8,512]{3,2,1,0:T(8,128)(2,1)}), bf16[64,4,8,512]{3,2,1,0:T(8,128)(2,1)S(1)}, u32[]{:S(2)}, u32[]{:S(2)}) async-start(bf16[64,4,8,512]{3,2,1,0:T(8,128)(2,1)} %bitcast.107), calls=%async_computation.1 | async-start | bytes 4194304 | tf_op jit(solution)/shard_map/all_to_all | solution.py:90
  178.1 4.3 %reshape.177 = bf16[64,128,128]{2,1,0:T(8,128)(2,1)} reshape(bf16[8,8,4,8,512]{4,3,2,1,0:T(8,128)(2,1)} %get-tuple-element.57) | data formatting | bytes 4194304 | tf_op jit(solution)/shard_map/reshape | solution.py:36
  182.4 4.3 %copy.21 = bf16[64,128,128]{2,0,1:T(8,128)(2,1)} copy(bf16[64,128,128]{2,1,0:T(8,128)(2,1)} %reshape.177) | data formatting | bytes 4194304 | tf_op jit(solution)/shard_map/reshape | solution.py:36
  186.7 2.2 gather_fusion
  190.5 80.7 %all-reduce.1 = (f32[64,64]{1,0:T(8,128)S(1)}, f32[64]{0:T(128)S(1)}) all-reduce(f32[64,64]{1,0:T(8,128)S(1)} %convolution_bitcast_fusion, f32[64]{0:T(128)S(1)} %convolution_bitcast_fusion.1), channel_id=1, replica_groups=mesh['mem'=8,'state'=32] {'mem','state'}, use_global_device_ids=true, to_apply=%region_4.5 | all-reduce | flops 4160 | bytes 33280 | tf_op jit(solution)/shard_map/psum | solution.py:31
  272.3 1.6 copy.43
  (137 shorter events, 41.7 us)
Async XLA Ops:
  1.8 17.2 %copy-start.4 = (bf16[128,36]{0,1:T(8,128)(2,1)S(1)}, bf16[128,36]{0,1:T(8,128)(2,1)}, u32[]{:S(2)}) copy-start(bf16[128,36]{0,1:T(8,128)(2,1)} %param.12) | copy-start | bytes 27652
  1.8 17.2 %copy-start.5 = (bf16[4,128]{1,0:T(4,128)(2,1)S(1)}, bf16[4,128]{1,0:T(4,128)(2,1)}, u32[]{:S(2)}) copy-start(bf16[4,128]{1,0:T(4,128)(2,1)} %param.14) | copy-start | bytes 3076
  1.8 17.2 %copy-start.6 = (f32[128]{0:T(128)S(1)}, f32[128]{0:T(128)}, u32[]{:S(2)}) copy-start(f32[128]{0:T(128)} %param.13) | copy-start | bytes 1540
  1.8 10.3 %collective-permute-start = (bf16[8,4,1,512]{3,2,1,0:T(2,128)(2,1)S(1)}, bf16[8,4,1,512]{3,2,1,0:T(2,128)(2,1)S(1)}, u32[]{:S(2)}, u32[]{:S(2)}) collective-permute-start(bf16[8,4,1,512]{3,2,1,0:T(2,128)(2,1)S(1)} %get-tuple-element.59), channel_id=1, source_target_pairs={{0,1},{1,2},{2,3},{3,4},{4,5},{5,6},{6,7},{7,8},{8,9},{9,10},{10,1... | collective-permute-start | bytes 98312 | tf_op jit(solution)/shard_map/ppermute | solution.py:14
  5.8 7.9 %collective-permute-start.1 = (bf16[8,4,1,512]{3,2,1,0:T(2,128)(2,1)S(1)}, bf16[8,4,1,512]{3,2,1,0:T(2,128)(2,1)S(1)}, u32[]{:S(2)}, u32[]{:S(2)}) collective-permute-start(bf16[8,4,1,512]{3,2,1,0:T(2,128)(2,1)S(1)} %get-tuple-element.60), channel_id=1, source_target_pairs={{1,0},{2,1},{3,2},{4,3},{5,4},{6,5},{7,6},{8,7},{9,8},{10,9},{11,1... | collective-permute-start | bytes 98312 | tf_op jit(solution)/shard_map/ppermute | solution.py:17
  160.7 5.0 %copy-start = (f32[64,64]{1,0:T(8,128)S(1)}, f32[64,64]{1,0:T(8,128)}, u32[]{:S(2)}) copy-start(f32[64,64]{1,0:T(8,128)} %param.15) | copy-start | bytes 49156
  160.7 5.0 %copy-start.3 = (f32[64]{0:T(128)S(1)}, f32[64]{0:T(128)}, u32[]{:S(2)}) copy-start(f32[64]{0:T(128)} %param.16) | copy-start | bytes 772
  174.1 4.0 %copy-start.7 = (s32[1,1,16]{2,1,0:T(1,128)S(1)}, s32[1,1,16]{2,1,0:T(1,128)}, u32[]{:S(2)}) copy-start(s32[1,1,16]{2,1,0:T(1,128)} %param.17) | copy-start | bytes 196
  174.1 98.2 %all-to-all-start.1 = ((bf16[64,4,8,512]{3,2,1,0:T(8,128)(2,1)}), bf16[64,4,8,512]{3,2,1,0:T(8,128)(2,1)S(1)}, u32[]{:S(2)}, u32[]{:S(2)}) async-start(bf16[64,4,8,512]{3,2,1,0:T(8,128)(2,1)} %bitcast.107), calls=%async_computation.1 | async-start | bytes 4194304 | tf_op jit(solution)/shard_map/all_to_all | solution.py:90
  182.4 6.6 %copy-start.1 = (f32[1,1,16,128]{3,2,1,0:T(8,128)S(1)}, f32[1,1,16,128]{3,2,1,0:T(8,128)}, u32[]{:S(2)}) copy-start(f32[1,1,16,128]{3,2,1,0:T(8,128)} %param.18) | copy-start | bytes 24580
  182.4 6.7 %copy-start.2 = (f32[1,1,16,128]{3,2,1,0:T(8,128)S(1)}, f32[1,1,16,128]{3,2,1,0:T(8,128)}, u32[]{:S(2)}) copy-start(f32[1,1,16,128]{3,2,1,0:T(8,128)} %param.19) | copy-start | bytes 24580
where the time goes:
time: 277 us; the launch traced here: 274 us
  blocking collectives  112 us (40%)
  matrix products  60.9 us (22%)
  local copies, waits for them, and re-layouts  59.7 us (22%)
  other arithmetic  23.5 us (8%)
  starting transfers between devices  14 us (5%)
    psum x1, blocking collectives, ensemble_sums(): return lax.psum((gram_part, proj_part), ('mem', 'state'))  80.7 us
    dot_general x8, matrix products, propagate_realizations(): jnp.dot(output_mixing_matrix, hidden, preferred_element_type=jnp.float32)  53.3 us
    all_to_all x1, blocking collectives, shards(): lax.all_to_all(predicted_realizations, 'mem', split_axis=2, concat_axis=0...  31.8 us
    while x80, local copies, waits for them, and re-layouts  22.1 us
    convert_element_type x8, other arithmetic, propagate_realizations(): return (realization_vector.astype(jnp.float32) + increment.reshape(realiz...  9.07 us
    reshape x2, local copies, waits for them, and re-layouts, observed_states(): blocked = realization_vectors.reshape(member_count, -1, 128)  8.62 us
    squeeze x8, local copies, waits for them, and re-layouts, shards(): lax.map(propagate_realizations, (bordered_vector, prior_realizations))  8.16 us
    dynamic_update_slice x8, local copies, waits for them, and re-layouts, shards(): lax.map(propagate_realizations, (bordered_vector, prior_realizations))  7.31 us
  transfers between devices with their start and end apart: 3, of which 2 were waited for; matrix products, arithmetic and copies ran while one was open for 5% of the time, Pallas kernels for 0%

commit v1 on v0

v1 whole, which is shorter than its diff:
```python
import functools
import math

import jax
import jax.numpy as jnp
import numpy as np
from jax import lax
from jax.experimental import pallas as pl
from jax.experimental.pallas import tpu as pltpu
from jax.sharding import PartitionSpec as P

BF = jnp.bfloat16
F32 = jnp.float32
VM = pltpu.VMEM
LIMIT = pltpu.CompilerParams(vmem_limit_bytes=56 * 1024 * 1024)

MEMBERS = 8
FIELDS = 4
ROWS = 64
COLS = 512
HID = 128
GROUP = 16
GROUPS = ROWS // GROUP
DEPTH = 224
CHUNKS = 4
LANES = 128
TILE = 256
GELU_A = math.sqrt(2.0 / math.pi)
GELU_B = GELU_A * 0.044715


def selection():
    chosen = np.zeros((DEPTH, GROUP, 39), np.float32)
    for b in range(3):
        for f in range(4):
            for row in range(GROUP):
                for a in (-1, 0, 1):
                    if 0 <= row + a < GROUP:
                        chosen[(b * 4 + f) * GROUP + row + a, row, (3 * (a + 1) + b) * 4 + f] = 1
            chosen[192 + b * 8 + f, 0, b * 4 + f] = 1
            chosen[196 + b * 8 + f, GROUP - 1, (6 + b) * 4 + f] = 1
    chosen[216:219, :, 36:] = np.eye(3)[:, None, :]
    return chosen.reshape(DEPTH * GROUP, 39)


def stencil_matrix(stencil, offset):
    half = 0.5 * offset
    cut = functools.partial(lax.reduce_precision, exponent_bits=8, mantissa_bits=7)
    first = cut(half)
    second = cut(half - first)
    third = half - first - second
    parts = jnp.stack([first, second, third], axis=1).astype(BF)
    rows = jnp.concatenate([(0.5 * stencil.astype(F32)).astype(BF), parts], axis=1)
    chosen = jnp.asarray(selection(), BF)
    spread = lax.dot_general(chosen, rows, (((1,), (1,)), ((), ())), preferred_element_type=F32)
    return spread.astype(BF).reshape(DEPTH, GROUP * HID)


def mixing_matrix(mixing):
    same = jnp.eye(GROUP, dtype=BF)
    return (mixing.T[None, :, :, None] * same[:, None, None, :]).reshape(GROUP * HID, 64)


def halved_gelu(half):
    return half + half * jnp.tanh(half * (8 * GELU_B * (half * half) + 2 * GELU_A))


def forecast_body(c, x_ref, edge_ref, w_ref, mix_ref, o_ref, p_ref, va, vb, ha, hb):
    lane = lax.broadcasted_iota(jnp.int32, (1, LANES), 1)
    row8 = lax.broadcasted_iota(jnp.int32, (8, LANES), 0)
    ones = jnp.where(row8 < 3, 1.0, 0.0).astype(F32)

    def three(read):
        mid = read(c)
        left = read(c - 1) if c > 0 else jnp.zeros_like(mid)
        right = read(c + 1) if c < CHUNKS - 1 else jnp.zeros_like(mid)
        return (
            jnp.where(lane == 0, pltpu.roll(left, 1, 1), pltpu.roll(mid, 1, 1)),
            mid,
            jnp.where(lane == LANES - 1, pltpu.roll(right, LANES - 1, 1), pltpu.roll(mid, LANES - 1, 1)),
        )

    def block(k, f, g, cc):
        return x_ref[k, f, g * 16 : (g + 1) * 16, cc * 128 : (cc + 1) * 128].astype(F32)

    def border(k, g, cc):
        edge = edge_ref[k, :, cc * 128 : (cc + 1) * 128]
        out = edge
        for f in range(FIELDS):
            if g > 0:
                out = jnp.where(row8 == f, pltpu.roll(block(k, f, g - 1, cc)[8:], (f + 1) % 8, 0), out)
            if g < GROUPS - 1:
                out = jnp.where(row8 == 4 + f, pltpu.roll(block(k, f, g + 1, cc)[:8], 4 + f, 0), out)
        return out

    def member(k, _):
        at = pl.ds(pl.multiple_of(k * LANES, LANES), LANES)
        for g in range(GROUPS):
            for f in range(FIELDS):
                for b, v in enumerate(three(lambda cc: block(k, f, g, cc))):
                    p_ref[g, (b * 4 + f) * 16 : (b * 4 + f + 1) * 16, at] = v.astype(BF)
            sides = three(lambda cc: border(k, g, cc))
            p_ref[g, 192:224, at] = jnp.concatenate([*sides, ones], axis=0).astype(BF)
        return 0

    lax.fori_loop(0, MEMBERS, member, 0)

    tiles = GROUP * HID // TILE
    held_v, held_h = (va, vb), (ha, hb)

    def group(g, _):
        patches = p_ref[g].T

        def before(n):
            held_v[n % 2][...] = jnp.dot(
                patches, w_ref[:, n * TILE : (n + 1) * TILE], preferred_element_type=F32
            )

        total = None
        before(0)
        for n in range(tiles + 1):
            if n + 1 < tiles:
                before(n + 1)
            if n < tiles:
                held_h[n % 2][...] = halved_gelu(held_v[n % 2][...]).astype(BF)
            if n >= 1:
                part = jnp.dot(
                    held_h[(n - 1) % 2][...],
                    mix_ref[(n - 1) * TILE : n * TILE, :],
                    preferred_element_type=F32,
                )
                total = part if total is None else total + part
        moved = total.T
        rows = pl.ds(pl.multiple_of(g * GROUP, GROUP), GROUP)
        for k in range(MEMBERS):
            new = [
                x_ref[k, f, rows, c * 128 : (c + 1) * 128].astype(F32)
                + moved[f * 16 : (f + 1) * 16, k * 128 : (k + 1) * 128]
                for f in range(FIELDS)
            ]
            for part in range(2):
                for pair in range(2):
                    both = [new[2 * pair + i][part * 8 : part * 8 + 8] for i in range(2)]
                    o_ref[2 * g + part, k, pair * 16 : pair * 16 + 16, :] = jnp.concatenate(
                        both, axis=0
                    ).astype(BF)
        return 0

    lax.fori_loop(0, GROUPS, group, 0)


def forecast_chunk(c, x, edges, weights, mix):
    cells = MEMBERS * LANES
    return pl.pallas_call(
        functools.partial(forecast_body, c),
        out_shape=jax.ShapeDtypeStruct((8, MEMBERS, 32, LANES), BF),
        in_specs=[pl.BlockSpec(memory_space=VM)] * 4,
        out_specs=pl.BlockSpec(memory_space=VM),
        scratch_shapes=[
            VM((GROUPS, DEPTH, cells), BF),
            VM((cells, TILE), F32),
            VM((cells, TILE), F32),
            VM((cells, TILE), BF),
            VM((cells, TILE), BF),
        ],
        compiler_params=LIMIT,
        name=f"forecast_{c}",
    )(x, edges, weights, mix)


def analysis_body(a_ref, f_ref, o_ref, s_ref, t_ref):
    s_ref[...] = f_ref[...].astype(F32).reshape(2048, LANES)
    for q in range(4):
        at = [pl.ds(q * 8 + i, 64, stride=32) for i in range(8)]
        states = jnp.concatenate([s_ref[i, :] for i in at], axis=1).astype(BF)
        both = jnp.dot(a_ref[...], states, preferred_element_type=F32)
        total = both[:64] + both[64:]
        for i in range(8):
            t_ref[at[i], :] = total[:, i * LANES : (i + 1) * LANES]
    o_ref[...] = t_ref[...].reshape(64, 32, LANES).astype(BF)


def analysis_chunk(update, states):
    return pl.pallas_call(
        analysis_body,
        out_shape=jax.ShapeDtypeStruct((64, 32, LANES), BF),
        in_specs=[pl.BlockSpec(memory_space=VM)] * 2,
        out_specs=pl.BlockSpec(memory_space=VM),
        scratch_shapes=[VM((2048, LANES), F32), VM((2048, LANES), F32)],
        compiler_params=LIMIT,
        name="analysis",
    )(update, states)


def gram_body(index_ref, values_ref, precision_ref, f0, f1, f2, f3, o_ref, s_ref, g_ref):
    for c, ref in enumerate((f0, f1, f2, f3)):
        s_ref[c * 2048 : (c + 1) * 2048, :] = ref[...].astype(F32).reshape(2048, LANES)
    for j in range(16):
        place = index_ref[j]
        start = lax.rem(place, 4) * 2048 + lax.div(place, 4)
        g_ref[:, j * LANES : (j + 1) * LANES] = s_ref[pl.ds(start, 64, stride=32), :]
    observed = g_ref[...]
    mean = jnp.sum(observed, axis=0, keepdims=True) * (1.0 / 64)
    spread = observed - mean
    weight = jnp.concatenate([precision_ref[j : j + 1, :] for j in range(16)], axis=1)
    value = jnp.concatenate([values_ref[j : j + 1, :] for j in range(16)], axis=1)
    weighted = spread * weight
    gram = lax.dot_general(
        spread,
        weighted,
        (((1,), (1,)), ((), ())),
        precision=lax.Precision.HIGHEST,
        preferred_element_type=F32,
    )
    proj = jnp.sum(weighted * (value - mean), axis=1, keepdims=True)
    o_ref[:, 0:64] = gram
    o_ref[:, 64:128] = jnp.broadcast_to(proj, (64, 64))


def gram_part(index, values, precision, chunks):
    return pl.pallas_call(
        gram_body,
        out_shape=jax.ShapeDtypeStruct((64, LANES), F32),
        in_specs=[pl.BlockSpec(memory_space=pltpu.SMEM)] + [pl.BlockSpec(memory_space=VM)] * 6,
        out_specs=pl.BlockSpec(memory_space=VM),
        scratch_shapes=[VM((4 * 2048, LANES), F32), VM((64, 2048), F32)],
        compiler_params=LIMIT,
        name="gram",
    )(index, values, precision, *chunks)


def place_body(c, *refs):
    b_ref, o_ref = refs[0], refs[-1]
    for k in range(MEMBERS):
        for pair in range(2):
            for half in range(4):
                low = b_ref[2 * half, k, pair * 16 : pair * 16 + 16, :].astype(F32)
                high = b_ref[2 * half + 1, k, pair * 16 : pair * 16 + 16, :].astype(F32)
                for i in range(2):
                    o_ref[k, 2 * pair + i, half * 16 : half * 16 + 16, :] = jnp.concatenate(
                        [low[i * 8 : i * 8 + 8], high[i * 8 : i * 8 + 8]], axis=0
                    ).astype(BF)


def place_chunk(c, back, so_far):
    first = so_far is None
    return pl.pallas_call(
        functools.partial(place_body, c),
        grid=(1,),
        out_shape=jax.ShapeDtypeStruct((MEMBERS, FIELDS, ROWS, COLS), BF),
        in_specs=[pl.BlockSpec((8, MEMBERS, 32, LANES), lambda i: (0, 0, 0, 0))]
        + ([] if first else [pl.BlockSpec(memory_space=pl.ANY)]),
        out_specs=pl.BlockSpec((MEMBERS, FIELDS, ROWS, LANES), lambda i: (0, 0, 0, c)),
        input_output_aliases={} if first else {1: 0},
        compiler_params=LIMIT,
        name=f"place_{c}",
    )(*([back] if first else [back, so_far]))


def sum_over(part, axis, groups=None):
    count = len(groups[0]) if groups else lax.axis_size(axis)
    copies = jnp.broadcast_to(part[None], (count, *part.shape))
    got = lax.all_to_all(
        copies, axis, split_axis=0, concat_axis=0, tiled=True, axis_index_groups=groups
    )
    return jnp.sum(got, axis=0)


def shards(
    prior_realizations,
    latent_stencil_weights,
    latent_offset,
    output_mixing_matrix,
    transform,
    mean_weights,
    obs_index,
    obs_values,
    obs_precision,
):
    count = lax.axis_size("state")
    forward = [(i, i + 1) for i in range(count - 1)]
    backward = [(i + 1, i) for i in range(count - 1)]
    low = lax.ppermute(prior_realizations[:, :, ROWS - 1, :], "state", forward)
    high = lax.ppermute(prior_realizations[:, :, 0, :], "state", backward)
    edges = jnp.concatenate([low, high], axis=1).astype(F32)

    weights = stencil_matrix(latent_stencil_weights, latent_offset)
    mix = mixing_matrix(output_mixing_matrix)
    combined = transform + mean_weights[:, None]
    update = (combined + (1.0 - jnp.sum(combined, axis=0)) / 64).T
    coarse = lax.reduce_precision(update, 8, 7)
    update = jnp.concatenate([coarse, update - coarse], axis=0).astype(BF)

    exchange = functools.partial(
        lax.all_to_all, axis_name="mem", split_axis=0, concat_axis=0, tiled=True
    )
    there = [
        exchange(forecast_chunk(c, prior_realizations, edges, weights, mix)) for c in range(CHUNKS)
    ]
    there = [piece.reshape(64, 32, LANES) for piece in there]
    back = [
        exchange(analysis_chunk(update, piece).reshape(8, MEMBERS, 32, LANES)) for piece in there
    ]
    part = gram_part(obs_index[0, 0], obs_values[0, 0], obs_precision[0, 0], there)
    total = sum_over(part, "mem")
    total = sum_over(total, "state", [[y * 8 + z for z in range(8)] for y in range(4)])
    total = sum_over(total, "state", [[y * 8 + z for y in range(4)] for z in range(8)])
    analysis = None
    for c in range(CHUNKS):
        analysis = place_chunk(c, back[c], analysis)
    gram = total[:, :64] / 524288
    proj = total[:, 64] / math.sqrt(524288)
    return (analysis, gram, proj)


def solution(mesh):
    return jax.shard_map(
        shards,
        mesh=mesh,
        in_specs=(
            P("mem", None, "state", None),
            P(),
            P(),
            P(),
            P(),
            P(),
            P("state", "mem", None),
            P("state", "mem", None, None),
            P("state", "mem", None, None),
        ),
        out_specs=(P("mem", None, "state", None), P(), P()),
        check_vma=False,
    )
```

time: 277 us -> 213 us (0.77)
  blocking collectives: 112 us -> 0 us
  Pallas kernels: 0 us -> 84.2 us
  matrix products: 60.9 us -> 1.81 us
  waiting for transfers between devices: 1.88 us -> 56.9 us
  local copies, waits for them, and re-layouts: 59.7 us -> 8.05 us
  starting transfers between devices: 14 us -> 55.5 us
  other arithmetic: 23.5 us -> 3.64 us
    pallas_call x0 -> x13, Pallas kernels: none -> 84.2 us  [the longest x4 60 us: forecast_chunk(): pl.pallas_call(functools.partial(forecast_body, c), out_shape=jax.ShapeDt...]
    psum x1 -> x0, blocking collectives: 80.7 us -> none  [ensemble_sums(): return lax.psum((gram_part, proj_part), ('mem', 'state'))]
    dot_general x11 -> x1, matrix products: 60.9 us -> 1.81 us  [stencil_matrix(): lax.dot_general(chosen, rows, (((1,), (1,)), ((), ())), preferred_element...]
    all_to_all x1 -> x11, waiting for transfers between devices: 0.01 us -> 56.5 us  [the longest x4 34.5 us: shards(): exchange(analysis_chunk(update, piece).reshape(8, MEMBERS, 32, LANES))]
    all_to_all x1 -> x11, starting transfers between devices: 3.95 us -> 45.7 us  [the longest x4 18.7 us: shards(): exchange(forecast_chunk(c, prior_realizations, edges, weights, mix))]
    all_to_all x1 -> x0, blocking collectives: 31.8 us -> none  [shards(): lax.all_to_all(predicted_realizations, 'mem', split_axis=2, concat_axis=0...]
    while x80 -> x0, local copies, waits for them, and re-layouts: 22.1 us -> none
    convert_element_type x8 -> x2, other arithmetic: 9.07 us -> 0.69 us  [the longest x1 0.69 us: shards(): edges = jnp.concatenate([low, high], axis=1).astype(F32)]
  transfers between devices with their start and end apart: 3 -> 13, of which waited for: 2 -> 8; matrix products, arithmetic and copies ran while one was open for 5% -> 3% of each run, Pallas kernels for 0% -> 31%
where the time goes in v1:
time: 213 us; the launch traced here: 211 us
  Pallas kernels  84.2 us (40%)
  waiting for transfers between devices  56.9 us (27%)
  starting transfers between devices  55.5 us (26%)
  local copies, waits for them, and re-layouts  8.05 us (4%)
  other arithmetic  3.64 us (2%)
    pallas_call x4, Pallas kernels, forecast_chunk(): pl.pallas_call(functools.partial(forecast_body, c), out_shape=jax.ShapeDt...  60 us
    all_to_all x4, waiting for transfers between devices, shards(): exchange(analysis_chunk(update, piece).reshape(8, MEMBERS, 32, LANES))  34.5 us
    all_to_all x4, starting transfers between devices, shards(): exchange(forecast_chunk(c, prior_realizations, edges, weights, mix))  18.7 us
    all_to_all x4, starting transfers between devices, shards(): exchange(analysis_chunk(update, piece).reshape(8, MEMBERS, 32, LANES))  14 us
    pallas_call x4, Pallas kernels, analysis_chunk(): pl.pallas_call(analysis_body, out_shape=jax.ShapeDtypeStruct((64, 32, LAN...  13 us
    all_to_all x3, starting transfers between devices, sum_over(): lax.all_to_all(copies, axis, split_axis=0, concat_axis=0, tiled=True, axi...  13 us
    all_to_all x3, waiting for transfers between devices, sum_over(): lax.all_to_all(copies, axis, split_axis=0, concat_axis=0, tiled=True, axi...  11.9 us
    all_to_all x4, waiting for transfers between devices, shards(): exchange(forecast_chunk(c, prior_realizations, edges, weights, mix))  10.1 us
  transfers between devices with their start and end apart: 13, of which 8 were waited for; matrix products, arithmetic and copies ran while one was open for 3% of the time, Pallas kernels for 31%

profile of v1, /device:TPU:24, one launch (start us, length us, event | category | flops | bytes accessed | tf_op | source)
XLA Modules:
  0.0 211.0 jit_solution(3653072760285970712)
XLA Ops:
  1.8 7.9 %collective-permute-start.1 = (bf16[8,4,512]{2,1,0:T(4,128)(2,1)S(1)}, bf16[8,4,512]{2,1,0:T(4,128)(2,1)S(1)}, u32[]{:S(2)}, u32[]{:S(2)}) collective-permute-start(bf16[8,4,512]{2,1,0:T(4,128)(2,1)S(1)} %bitcast.45), channel_id=1, source_target_pairs={{1,0},{2,1},{3,2},{4,3},{5,4},{6,5},{7,6},{8,7},{9,8},{10,9},{11,1... | collective-permute-start | bytes 98312 | tf_op jit(solution)/shard_map/ppermute | solution.py:284
  18.4 14.9 %forecast_0.1 = bf16[8,8,32,128]{3,2,1,0:T(8,128)(2,1)} custom-call(bf16[8,4,64,512]{3,2,1,0:T(8,128)(2,1)} %x_ref.7, f32[8,8,512]{2,1,0:T(8,128)} %maximum_convert_fusion.edge_ref, bf16[224,2048]{1,0:T(8,128)(2,1)} %reshape.56.w_ref, bf16[2048,64]{1,0:T(8,128)(2,1)} %copy.33.mix_ref), custom_call_target="tpu_custom_call" | custom-call | tf_op jit(solution)/shard_map/forecast_0/pallas_call | solution.py:154
  33.3 4.3 %all-to-all-start.6 = ((bf16[8,8,32,128]{3,2,1,0:T(8,128)(2,1)}), bf16[8,8,32,128]{3,2,1,0:T(8,128)(2,1)S(1)}, u32[]{:S(2)}, u32[]{:S(2)}) async-start(bf16[8,8,32,128]{3,2,1,0:T(8,128)(2,1)} %forecast_0.1), calls=%async_computation.6 | async-start | bytes 1048576 | tf_op jit(solution)/shard_map/all_to_all | solution.py:298
  37.6 15.1 %forecast_1.1 = bf16[8,8,32,128]{3,2,1,0:T(8,128)(2,1)} custom-call(bf16[8,4,64,512]{3,2,1,0:T(8,128)(2,1)} %x_ref.7, f32[8,8,512]{2,1,0:T(8,128)} %maximum_convert_fusion.edge_ref, bf16[224,2048]{1,0:T(8,128)(2,1)} %reshape.56.w_ref, bf16[2048,64]{1,0:T(8,128)(2,1)} %copy.33.mix_ref), custom_call_target="tpu_custom_call" | custom-call | tf_op jit(solution)/shard_map/forecast_1/pallas_call | solution.py:154
  52.7 4.8 %all-to-all-start.4 = ((bf16[8,8,32,128]{3,2,1,0:T(8,128)(2,1)}), bf16[8,8,32,128]{3,2,1,0:T(8,128)(2,1)S(1)}, u32[]{:S(2)}, u32[]{:S(2)}) async-start(bf16[8,8,32,128]{3,2,1,0:T(8,128)(2,1)} %forecast_1.1), calls=%async_computation.4 | async-start | bytes 1048576 | tf_op jit(solution)/shard_map/all_to_all | solution.py:298
  57.5 14.9 %forecast_3.1 = bf16[8,8,32,128]{3,2,1,0:T(8,128)(2,1)} custom-call(bf16[8,4,64,512]{3,2,1,0:T(8,128)(2,1)} %x_ref.7, f32[8,8,512]{2,1,0:T(8,128)} %maximum_convert_fusion.edge_ref, bf16[224,2048]{1,0:T(8,128)(2,1)} %reshape.56.w_ref, bf16[2048,64]{1,0:T(8,128)(2,1)} %copy.33.mix_ref), custom_call_target="tpu_custom_call" | custom-call | tf_op jit(solution)/shard_map/forecast_3/pallas_call | solution.py:154
  72.5 4.8 %all-to-all-start = ((bf16[8,8,32,128]{3,2,1,0:T(8,128)(2,1)}), bf16[8,8,32,128]{3,2,1,0:T(8,128)(2,1)S(1)}, u32[]{:S(2)}, u32[]{:S(2)}) async-start(bf16[8,8,32,128]{3,2,1,0:T(8,128)(2,1)} %forecast_3.1), calls=%async_computation | async-start | bytes 1048576 | tf_op jit(solution)/shard_map/all_to_all | solution.py:298
  77.3 15.1 %forecast_2.1 = bf16[8,8,32,128]{3,2,1,0:T(8,128)(2,1)} custom-call(bf16[8,4,64,512]{3,2,1,0:T(8,128)(2,1)} %x_ref.7, f32[8,8,512]{2,1,0:T(8,128)} %maximum_convert_fusion.edge_ref, bf16[224,2048]{1,0:T(8,128)(2,1)} %reshape.56.w_ref, bf16[2048,64]{1,0:T(8,128)(2,1)} %copy.33.mix_ref), custom_call_target="tpu_custom_call" | custom-call | tf_op jit(solution)/shard_map/forecast_2/pallas_call | solution.py:154
  92.4 4.8 %all-to-all-start.2 = ((bf16[8,8,32,128]{3,2,1,0:T(8,128)(2,1)}), bf16[8,8,32,128]{3,2,1,0:T(8,128)(2,1)S(1)}, u32[]{:S(2)}, u32[]{:S(2)}) async-start(bf16[8,8,32,128]{3,2,1,0:T(8,128)(2,1)} %forecast_2.1), calls=%async_computation.2 | async-start | bytes 1048576 | tf_op jit(solution)/shard_map/all_to_all | solution.py:298
  97.4 10.1 %all-to-all-done.2 = bf16[8,8,32,128]{3,2,1,0:T(8,128)(2,1)S(1)} async-done(((bf16[8,8,32,128]{3,2,1,0:T(8,128)(2,1)}), bf16[8,8,32,128]{3,2,1,0:T(8,128)(2,1)S(1)}, u32[]{:S(2)}, u32[]{:S(2)}) %all-to-all-start.2) | async-done | bytes 524320 | tf_op jit(solution)/shard_map/all_to_all | solution.py:298
  108.3 3.5 %gram.1 = f32[64,128]{1,0:T(8,128)} custom-call(s32[16]{0:T(128)} %bitcast.50, f32[16,128]{1,0:T(8,128)} %bitcast.47, f32[16,128]{1,0:T(8,128)} %bitcast.48, bf16[64,32,128]{2,1,0:T(8,128)(2,1)} %bitcast.37, bf16[64,32,128]{2,1,0:T(8,128)(2,1)} %bitcast.35, bf16[64,32,128]{2,1,0:T(8,128)(2,1)} %bitcast.31, bf16[64,32,128]{2,1,0:T(8,128)(2,1)} %bitcast.33), custom_call_target="tpu_custom_call" | custom-call | tf_op jit(solution)/shard_map/gram/pallas_call | solution.py:221
  113.3 3.4 %all-to-all-start.8 = ((f32[8,64,128]{2,1,0:T(8,128)}), f32[8,64,128]{2,1,0:T(8,128)S(1)}, u32[]{:S(2)}, u32[]{:S(2)}) async-start(f32[8,64,128]{2,1,0:T(8,128)} %broadcast_in_dim.6), calls=%async_computation.8 | async-start | bytes 524288 | tf_op jit(solution)/shard_map/all_to_all | solution.py:263
  117.4 3.3 %analysis.7 = bf16[64,32,128]{2,1,0:T(8,128)(2,1)} custom-call(bf16[128,64]{1,0:T(8,128)(2,1)} %pad_maximum_fusion.a_ref, bf16[64,32,128]{2,1,0:T(8,128)(2,1)} %bitcast.38), custom_call_target="tpu_custom_call" | custom-call | tf_op jit(solution)/shard_map/analysis/pallas_call | solution.py:184
  120.7 3.5 %all-to-all-done.8 = f32[8,64,128]{2,1,0:T(8,128)S(1)} async-done(((f32[8,64,128]{2,1,0:T(8,128)}), f32[8,64,128]{2,1,0:T(8,128)S(1)}, u32[]{:S(2)}, u32[]{:S(2)}) %all-to-all-start.8) | async-done | bytes 262176 | tf_op jit(solution)/shard_map/all_to_all | solution.py:263
  124.2 3.5 %all-to-all-start.7 = ((bf16[8,8,32,128]{3,2,1,0:T(8,128)(2,1)}), bf16[8,8,32,128]{3,2,1,0:T(8,128)(2,1)S(1)}, u32[]{:S(2)}, u32[]{:S(2)}) async-start(bf16[8,8,32,128]{3,2,1,0:T(8,128)(2,1)} %bitcast.40), calls=%async_computation.7 | async-start | bytes 1048576 | tf_op jit(solution)/shard_map/all_to_all | solution.py:302
  127.7 3.3 %analysis.6 = bf16[64,32,128]{2,1,0:T(8,128)(2,1)} custom-call(bf16[128,64]{1,0:T(8,128)(2,1)} %pad_maximum_fusion.a_ref, bf16[64,32,128]{2,1,0:T(8,128)(2,1)} %bitcast.36), custom_call_target="tpu_custom_call" | custom-call | tf_op jit(solution)/shard_map/analysis/pallas_call | solution.py:184
  130.9 7.0 %all-to-all-done.7.refs_0_ = bf16[8,8,32,128]{3,2,1,0:T(8,128)(2,1)S(1)} async-done(((bf16[8,8,32,128]{3,2,1,0:T(8,128)(2,1)}), bf16[8,8,32,128]{3,2,1,0:T(8,128)(2,1)S(1)}, u32[]{:S(2)}, u32[]{:S(2)}) %all-to-all-start.7) | async-done | bytes 524320 | tf_op jit(solution)/shard_map/all_to_all | solution.py:302
  137.9 3.5 %all-to-all-start.5 = ((bf16[8,8,32,128]{3,2,1,0:T(8,128)(2,1)}), bf16[8,8,32,128]{3,2,1,0:T(8,128)(2,1)S(1)}, u32[]{:S(2)}, u32[]{:S(2)}) async-start(bf16[8,8,32,128]{3,2,1,0:T(8,128)(2,1)} %bitcast.41), calls=%async_computation.5 | async-start | bytes 1048576 | tf_op jit(solution)/shard_map/all_to_all | solution.py:302
  141.4 3.2 %analysis.4 = bf16[64,32,128]{2,1,0:T(8,128)(2,1)} custom-call(bf16[128,64]{1,0:T(8,128)(2,1)} %pad_maximum_fusion.a_ref, bf16[64,32,128]{2,1,0:T(8,128)(2,1)} %bitcast.34), custom_call_target="tpu_custom_call" | custom-call | tf_op jit(solution)/shard_map/analysis/pallas_call | solution.py:184
  144.7 7.0 %all-to-all-done.5.refs_0_ = bf16[8,8,32,128]{3,2,1,0:T(8,128)(2,1)S(1)} async-done(((bf16[8,8,32,128]{3,2,1,0:T(8,128)(2,1)}), bf16[8,8,32,128]{3,2,1,0:T(8,128)(2,1)S(1)}, u32[]{:S(2)}, u32[]{:S(2)}) %all-to-all-start.5) | async-done | bytes 524320 | tf_op jit(solution)/shard_map/all_to_all | solution.py:302
  151.7 3.5 %all-to-all-start.1 = ((bf16[8,8,32,128]{3,2,1,0:T(8,128)(2,1)}), bf16[8,8,32,128]{3,2,1,0:T(8,128)(2,1)S(1)}, u32[]{:S(2)}, u32[]{:S(2)}) async-start(bf16[8,8,32,128]{3,2,1,0:T(8,128)(2,1)} %bitcast.42), calls=%async_computation.1 | async-start | bytes 1048576 | tf_op jit(solution)/shard_map/all_to_all | solution.py:302
  155.2 10.2 %all-to-all-done.1.refs_0_ = bf16[8,8,32,128]{3,2,1,0:T(8,128)(2,1)S(1)} async-done(((bf16[8,8,32,128]{3,2,1,0:T(8,128)(2,1)}), bf16[8,8,32,128]{3,2,1,0:T(8,128)(2,1)S(1)}, u32[]{:S(2)}, u32[]{:S(2)}) %all-to-all-start.1) | async-done | bytes 524320 | tf_op jit(solution)/shard_map/all_to_all | solution.py:302
  166.2 4.1 %all-to-all-start.9 = ((f32[8,64,128]{2,1,0:T(8,128)}), f32[8,64,128]{2,1,0:T(8,128)S(1)}, u32[]{:S(2)}, u32[]{:S(2)}) async-start(f32[8,64,128]{2,1,0:T(8,128)} %broadcast_in_dim.7), calls=%async_computation.9 | async-start | bytes 524288 | tf_op jit(solution)/shard_map/all_to_all | solution.py:263
  170.3 3.3 %analysis.5 = bf16[64,32,128]{2,1,0:T(8,128)(2,1)} custom-call(bf16[128,64]{1,0:T(8,128)(2,1)} %pad_maximum_fusion.a_ref, bf16[64,32,128]{2,1,0:T(8,128)(2,1)} %bitcast.32), custom_call_target="tpu_custom_call" | custom-call | tf_op jit(solution)/shard_map/analysis/pallas_call | solution.py:184
  173.6 8.4 %all-to-all-done.9 = f32[8,64,128]{2,1,0:T(8,128)S(1)} async-done(((f32[8,64,128]{2,1,0:T(8,128)}), f32[8,64,128]{2,1,0:T(8,128)S(1)}, u32[]{:S(2)}, u32[]{:S(2)}) %all-to-all-start.9) | async-done | bytes 262176 | tf_op jit(solution)/shard_map/all_to_all | solution.py:263
  182.0 3.5 %all-to-all-start.3 = ((bf16[8,8,32,128]{3,2,1,0:T(8,128)(2,1)}), bf16[8,8,32,128]{3,2,1,0:T(8,128)(2,1)S(1)}, u32[]{:S(2)}, u32[]{:S(2)}) async-start(bf16[8,8,32,128]{3,2,1,0:T(8,128)(2,1)} %bitcast.39), calls=%async_computation.3 | async-start | bytes 1048576 | tf_op jit(solution)/shard_map/all_to_all | solution.py:302
  185.6 10.2 %all-to-all-done.3.refs_0_ = bf16[8,8,32,128]{3,2,1,0:T(8,128)(2,1)S(1)} async-done(((bf16[8,8,32,128]{3,2,1,0:T(8,128)(2,1)}), bf16[8,8,32,128]{3,2,1,0:T(8,128)(2,1)S(1)}, u32[]{:S(2)}, u32[]{:S(2)}) %all-to-all-start.3) | async-done | bytes 524320 | tf_op jit(solution)/shard_map/all_to_all | solution.py:302
  196.5 5.5 %all-to-all-start.10 = ((f32[4,64,128]{2,1,0:T(8,128)}), f32[4,64,128]{2,1,0:T(8,128)S(1)}, u32[]{:S(2)}, u32[]{:S(2)}) async-start(f32[4,64,128]{2,1,0:T(8,128)} %broadcast_in_dim.8), calls=%async_computation.10 | async-start | bytes 262144 | tf_op jit(solution)/shard_map/all_to_all | solution.py:263
  202.0 1.9 place_0.1.refs_1_
  203.9 1.9 place_1.1.refs_1_
  205.8 1.9 place_2.1.refs_1_
  207.7 1.9 place_3.1
  (54 shorter events, 15.8 us)
Async XLA Ops:
  0.6 13.6 %copy-start.10 = (bf16[4,128]{1,0:T(4,128)(2,1)S(1)}, bf16[4,128]{1,0:T(4,128)(2,1)}, u32[]{:S(2)}) copy-start(bf16[4,128]{1,0:T(4,128)(2,1)} %param.13) | copy-start | bytes 3076
  1.8 15.5 %collective-permute-start.1 = (bf16[8,4,512]{2,1,0:T(4,128)(2,1)S(1)}, bf16[8,4,512]{2,1,0:T(4,128)(2,1)S(1)}, u32[]{:S(2)}, u32[]{:S(2)}) collective-permute-start(bf16[8,4,512]{2,1,0:T(4,128)(2,1)S(1)} %bitcast.45), channel_id=1, source_target_pairs={{1,0},{2,1},{3,2},{4,3},{5,4},{6,5},{7,6},{8,7},{9,8},{10,9},{11,1... | collective-permute-start | bytes 98312 | tf_op jit(solution)/shard_map/ppermute | solution.py:284
  9.8 7.9 %collective-permute-start = (bf16[8,4,512]{2,1,0:T(4,128)(2,1)S(1)}, bf16[8,4,512]{2,1,0:T(4,128)(2,1)S(1)}, u32[]{:S(2)}, u32[]{:S(2)}) collective-permute-start(bf16[8,4,512]{2,1,0:T(4,128)(2,1)S(1)} %bitcast.46), channel_id=1, source_target_pairs={{0,1},{1,2},{2,3},{3,4},{4,5},{5,6},{6,7},{7,8},{8,9},{9,10},{10,1... | collective-permute-start | bytes 98312 | tf_op jit(solution)/shard_map/ppermute | solution.py:283
  33.3 19.4 %all-to-all-start.6 = ((bf16[8,8,32,128]{3,2,1,0:T(8,128)(2,1)}), bf16[8,8,32,128]{3,2,1,0:T(8,128)(2,1)S(1)}, u32[]{:S(2)}, u32[]{:S(2)}) async-start(bf16[8,8,32,128]{3,2,1,0:T(8,128)(2,1)} %forecast_0.1), calls=%async_computation.6 | async-start | bytes 1048576 | tf_op jit(solution)/shard_map/all_to_all | solution.py:298
  52.7 19.8 %copy-start.3 = (bf16[8,8,32,128]{3,2,1,0:T(8,128)(2,1)}, bf16[8,8,32,128]{3,2,1,0:T(8,128)(2,1)S(1)}, u32[]{:S(2)}) copy-start(bf16[8,8,32,128]{3,2,1,0:T(8,128)(2,1)S(1)} %all-to-all-done.6) | copy-start | bytes 1572868
  52.7 19.8 %all-to-all-start.4 = ((bf16[8,8,32,128]{3,2,1,0:T(8,128)(2,1)}), bf16[8,8,32,128]{3,2,1,0:T(8,128)(2,1)S(1)}, u32[]{:S(2)}, u32[]{:S(2)}) async-start(bf16[8,8,32,128]{3,2,1,0:T(8,128)(2,1)} %forecast_1.1), calls=%async_computation.4 | async-start | bytes 1048576 | tf_op jit(solution)/shard_map/all_to_all | solution.py:298
  72.4 19.9 %copy-start.2 = (bf16[8,8,32,128]{3,2,1,0:T(8,128)(2,1)}, bf16[8,8,32,128]{3,2,1,0:T(8,128)(2,1)S(1)}, u32[]{:S(2)}) copy-start(bf16[8,8,32,128]{3,2,1,0:T(8,128)(2,1)S(1)} %all-to-all-done.4) | copy-start | bytes 1572868
  72.5 19.9 %all-to-all-start = ((bf16[8,8,32,128]{3,2,1,0:T(8,128)(2,1)}), bf16[8,8,32,128]{3,2,1,0:T(8,128)(2,1)S(1)}, u32[]{:S(2)}, u32[]{:S(2)}) async-start(bf16[8,8,32,128]{3,2,1,0:T(8,128)(2,1)} %forecast_3.1), calls=%async_computation | async-start | bytes 1048576 | tf_op jit(solution)/shard_map/all_to_all | solution.py:298
  77.3 19.9 %copy-start.8 = (f32[64,64]{1,0:T(8,128)S(1)}, f32[64,64]{1,0:T(8,128)}, u32[]{:S(2)}) copy-start(f32[64,64]{1,0:T(8,128)} %param.14) | copy-start | bytes 49156
  77.3 20.0 %copy-start.9 = (f32[64]{0:T(128)S(1)}, f32[64]{0:T(128)}, u32[]{:S(2)}) copy-start(f32[64]{0:T(128)} %param.15) | copy-start | bytes 772
  92.4 15.2 %copy-start.1 = (bf16[8,8,32,128]{3,2,1,0:T(8,128)(2,1)}, bf16[8,8,32,128]{3,2,1,0:T(8,128)(2,1)S(1)}, u32[]{:S(2)}) copy-start(bf16[8,8,32,128]{3,2,1,0:T(8,128)(2,1)S(1)} %all-to-all-done) | copy-start | bytes 1572868
  92.4 15.1 %all-to-all-start.2 = ((bf16[8,8,32,128]{3,2,1,0:T(8,128)(2,1)}), bf16[8,8,32,128]{3,2,1,0:T(8,128)(2,1)S(1)}, u32[]{:S(2)}, u32[]{:S(2)}) async-start(bf16[8,8,32,128]{3,2,1,0:T(8,128)(2,1)} %forecast_2.1), calls=%async_computation.2 | async-start | bytes 1048576 | tf_op jit(solution)/shard_map/all_to_all | solution.py:298
  107.5 0.8 copy-start
  113.3 10.9 %all-to-all-start.8 = ((f32[8,64,128]{2,1,0:T(8,128)}), f32[8,64,128]{2,1,0:T(8,128)S(1)}, u32[]{:S(2)}, u32[]{:S(2)}) async-start(f32[8,64,128]{2,1,0:T(8,128)} %broadcast_in_dim.6), calls=%async_computation.8 | async-start | bytes 524288 | tf_op jit(solution)/shard_map/all_to_all | solution.py:263
  124.2 13.8 %all-to-all-start.7 = ((bf16[8,8,32,128]{3,2,1,0:T(8,128)(2,1)}), bf16[8,8,32,128]{3,2,1,0:T(8,128)(2,1)S(1)}, u32[]{:S(2)}, u32[]{:S(2)}) async-start(bf16[8,8,32,128]{3,2,1,0:T(8,128)(2,1)} %bitcast.40), calls=%async_computation.7 | async-start | bytes 1048576 | tf_op jit(solution)/shard_map/all_to_all | solution.py:302
  137.9 28.3 %copy-start.4 = (bf16[8,8,32,128]{3,2,1,0:T(8,128)(2,1)}, bf16[8,8,32,128]{3,2,1,0:T(8,128)(2,1)S(1)}, u32[]{:S(2)}) copy-start(bf16[8,8,32,128]{3,2,1,0:T(8,128)(2,1)S(1)} %all-to-all-done.7.refs_0_) | copy-start | bytes 1572868
  137.9 13.8 %all-to-all-start.5 = ((bf16[8,8,32,128]{3,2,1,0:T(8,128)(2,1)}), bf16[8,8,32,128]{3,2,1,0:T(8,128)(2,1)S(1)}, u32[]{:S(2)}, u32[]{:S(2)}) async-start(bf16[8,8,32,128]{3,2,1,0:T(8,128)(2,1)} %bitcast.41), calls=%async_computation.5 | async-start | bytes 1048576 | tf_op jit(solution)/shard_map/all_to_all | solution.py:302
  151.7 30.3 %copy-start.5 = (bf16[8,8,32,128]{3,2,1,0:T(8,128)(2,1)}, bf16[8,8,32,128]{3,2,1,0:T(8,128)(2,1)S(1)}, u32[]{:S(2)}) copy-start(bf16[8,8,32,128]{3,2,1,0:T(8,128)(2,1)S(1)} %all-to-all-done.5.refs_0_) | copy-start | bytes 1572868
  151.7 13.8 %all-to-all-start.1 = ((bf16[8,8,32,128]{3,2,1,0:T(8,128)(2,1)}), bf16[8,8,32,128]{3,2,1,0:T(8,128)(2,1)S(1)}, u32[]{:S(2)}, u32[]{:S(2)}) async-start(bf16[8,8,32,128]{3,2,1,0:T(8,128)(2,1)} %bitcast.42), calls=%async_computation.1 | async-start | bytes 1048576 | tf_op jit(solution)/shard_map/all_to_all | solution.py:302
  165.5 31.0 %copy-start.6 = (bf16[8,8,32,128]{3,2,1,0:T(8,128)(2,1)}, bf16[8,8,32,128]{3,2,1,0:T(8,128)(2,1)S(1)}, u32[]{:S(2)}) copy-start(bf16[8,8,32,128]{3,2,1,0:T(8,128)(2,1)S(1)} %all-to-all-done.1.refs_0_) | copy-start | bytes 1572868
  166.2 15.8 %all-to-all-start.9 = ((f32[8,64,128]{2,1,0:T(8,128)}), f32[8,64,128]{2,1,0:T(8,128)S(1)}, u32[]{:S(2)}, u32[]{:S(2)}) async-start(f32[8,64,128]{2,1,0:T(8,128)} %broadcast_in_dim.7), calls=%async_computation.9 | async-start | bytes 524288 | tf_op jit(solution)/shard_map/all_to_all | solution.py:263
  182.0 13.8 %all-to-all-start.3 = ((bf16[8,8,32,128]{3,2,1,0:T(8,128)(2,1)}), bf16[8,8,32,128]{3,2,1,0:T(8,128)(2,1)S(1)}, u32[]{:S(2)}, u32[]{:S(2)}) async-start(bf16[8,8,32,128]{3,2,1,0:T(8,128)(2,1)} %bitcast.39), calls=%async_computation.3 | async-start | bytes 1048576 | tf_op jit(solution)/shard_map/all_to_all | solution.py:302
  195.8 10.0 %copy-start.7 = (bf16[8,8,32,128]{3,2,1,0:T(8,128)(2,1)}, bf16[8,8,32,128]{3,2,1,0:T(8,128)(2,1)S(1)}, u32[]{:S(2)}) copy-start(bf16[8,8,32,128]{3,2,1,0:T(8,128)(2,1)S(1)} %all-to-all-done.3.refs_0_) | copy-start | bytes 1572868
  196.5 13.2 %all-to-all-start.10 = ((f32[4,64,128]{2,1,0:T(8,128)}), f32[4,64,128]{2,1,0:T(8,128)S(1)}, u32[]{:S(2)}, u32[]{:S(2)}) async-start(f32[4,64,128]{2,1,0:T(8,128)} %broadcast_in_dim.8), calls=%async_computation.10 | async-start | bytes 262144 | tf_op jit(solution)/shard_map/all_to_all | solution.py:263

commit v2 on v1

v2 whole, which is shorter than its diff:
```python
import functools
import math

import jax
import jax.numpy as jnp
from jax import lax
from jax.experimental import pallas as pl
from jax.experimental.pallas import tpu as pltpu
from jax.sharding import PartitionSpec as P

BF = jnp.bfloat16
F32 = jnp.float32
VM = pltpu.VMEM
LIMIT = pltpu.CompilerParams(vmem_limit_bytes=24 * 1024 * 1024)

MEMBERS = 8
FIELDS = 4
ROWS = 64
COLS = 512
HID = 128
GROUP = 16
GROUPS = ROWS // GROUP
DEPTH = 224
CHUNKS = 4
LANES = 128
TILE = 256
GELU_A = math.sqrt(2.0 / math.pi)
GELU_B = GELU_A * 0.044715


def held(x):
    return pltpu.with_memory_space_constraint(x, pltpu.VMEM)


def stored(x):
    return pltpu.with_memory_space_constraint(x, pltpu.HBM)


WHOLE = pl.BlockSpec(memory_space=VM)


def weights_body(rows_ref, mix_ref, w_ref, m_ref):
    k = lax.broadcasted_iota(jnp.int32, (DEPTH, LANES), 0)
    j = lax.broadcasted_iota(jnp.int32, (DEPTH, LANES), 1)
    b, f, row = k // 64, (k // 16) % 4, k % 16
    edge = k - 192
    edge_b, below, edge_f = edge // 8, (edge // 4) % 2, edge % 4
    lanes = lax.broadcasted_iota(jnp.int32, (HID, LANES), 1)
    linear = jnp.zeros((DEPTH, LANES), F32)
    for r in range(GROUP):
        inside = jnp.where(jnp.abs(row - r) <= 1, (3 * (row - r + 1) + b) * 4 + f, -1)
        border = (below * 6 + edge_b) * 4 + edge_f
        border = jnp.where(below * (GROUP - 1) == r, border, -1)
        want = jnp.where(k < 192, inside, jnp.where(k < 216, border, k - 180))
        chosen = jnp.where(j == want, 1.0, 0.0).astype(BF)
        part = jnp.dot(chosen, rows_ref[...], preferred_element_type=F32).astype(BF)
        w_ref[:, r * HID : (r + 1) * HID] = part
        spread = jnp.zeros((HID, LANES), F32)
        for field in range(FIELDS):
            spread = jnp.where(lanes == field * GROUP + r, mix_ref[:, field : field + 1], spread)
        spread = spread.astype(BF)
        m_ref[r * HID : (r + 1) * HID, :] = spread[:, :64]
        linear = linear + jnp.dot(part, spread, preferred_element_type=F32)
    linear = linear[:, :64]
    coarse = linear.astype(BF)
    w_ref[:, GROUP * HID :] = jnp.concatenate(
        [coarse, (linear - coarse.astype(F32)).astype(BF)], axis=1
    )


def product_weights(stencil, offset, mixing):
    half = 0.5 * offset
    cut = functools.partial(lax.reduce_precision, exponent_bits=8, mantissa_bits=7)
    first = cut(half)
    second = cut(half - first)
    third = half - first - second
    rows = jnp.concatenate(
        [0.5 * stencil.astype(F32).T, jnp.stack([first, second, third]), jnp.zeros((89, HID), F32)]
    ).astype(BF)
    return pl.pallas_call(
        weights_body,
        out_shape=(
            pltpu.HBM((DEPTH, GROUP * HID + LANES), BF),
            pltpu.HBM((GROUP * HID, 64), BF),
        ),
        in_specs=[WHOLE] * 2,
        out_specs=(WHOLE, WHOLE),
        compiler_params=LIMIT,
        name="weights",
    )(rows, mixing.astype(F32).T)


def forecast_body(chunks, columns, edge_ref, w_ref, mix_ref, *refs):
    windows, (o_ref, pa, pb, va, vb, ha, hb, s_ref) = refs[: len(columns)], refs[len(columns) :]
    windows = dict(zip(columns, windows))
    for slot, c in enumerate(chunks):
        forecast_block(
            c, slot, windows, edge_ref, w_ref, mix_ref, o_ref, pa, pb, va, vb, ha, hb, s_ref
        )


def forecast_block(
    c, slot, windows, edge_ref, w_ref, mix_ref, o_ref, pa, pb, va, vb, ha, hb, s_ref
):
    lane = lax.broadcasted_iota(jnp.int32, (1, LANES), 1)
    row8 = lax.broadcasted_iota(jnp.int32, (8, LANES), 0)
    ones = jnp.where(row8 < 3, 1.0, 0.0).astype(F32)

    def three(read):
        mid = read(c)
        left = read(c - 1) if c > 0 else jnp.zeros_like(mid)
        right = read(c + 1) if c < CHUNKS - 1 else jnp.zeros_like(mid)
        last = LANES - 1
        return (
            jnp.where(lane == 0, pltpu.roll(left, 1, 1), pltpu.roll(mid, 1, 1)),
            mid,
            jnp.where(lane == last, pltpu.roll(right, last, 1), pltpu.roll(mid, last, 1)),
        )

    def block(k, f, g, cc):
        rows = pl.ds(pl.multiple_of(g * GROUP, GROUP), GROUP)
        return windows[cc][k, f, rows, :].astype(F32)

    def border(k, g, cc):
        out = edge_ref[k, :, cc * LANES : (cc + 1) * LANES]
        above, below = jnp.maximum(g - 1, 0), jnp.minimum(g + 1, GROUPS - 1)
        for f in range(FIELDS):
            up = pltpu.roll(block(k, f, above, cc)[8:], (f + 1) % 8, 0)
            down = pltpu.roll(block(k, f, below, cc)[:8], 4 + f, 0)
            out = jnp.where((row8 == f) & (g > 0), up, out)
            out = jnp.where((row8 == 4 + f) & (g < GROUPS - 1), down, out)
        return out

    def build(g, k, to):
        inner = [three(lambda cc: block(k, f, g, cc)) for f in range(FIELDS)]
        parts = [inner[f][b] for b in range(3) for f in range(FIELDS)]
        parts += [*three(lambda cc: border(k, g, cc)), ones]
        to[k * LANES : (k + 1) * LANES, :] = jnp.concatenate(parts, axis=0).astype(BF).T

    tiles = GROUP * HID // TILE
    held_v, held_h = (va, vb), (ha, hb)

    def group(g, patches, following, to):
        def before(n):
            held_v[n % 2][...] = jnp.dot(
                patches[...], w_ref[:, n * TILE : (n + 1) * TILE], preferred_element_type=F32
            ).astype(BF)

        linear = jnp.dot(patches[...], w_ref[:, GROUP * HID :], preferred_element_type=F32)
        total = linear[:, :64] + linear[:, 64:]
        before(0)
        for n in range(tiles + 1):
            if n + 1 < tiles:
                before(n + 1)
            if n < tiles:
                h = held_v[n % 2][...]
                bend = jnp.tanh(h * (h * h * BF(8 * GELU_B) + BF(2 * GELU_A)))
                held_h[n % 2][...] = h * bend
                build(following, n, to)
            if n >= 1:
                total = total + jnp.dot(
                    held_h[(n - 1) % 2][...],
                    mix_ref[(n - 1) * TILE : n * TILE, :],
                    preferred_element_type=F32,
                )
        moved = total.T
        rows = pl.ds(pl.multiple_of(g * GROUP, GROUP), GROUP)
        for k in range(MEMBERS):
            new = [
                windows[c][k, f, rows, :].astype(F32)
                + moved[f * GROUP : (f + 1) * GROUP, k * LANES : (k + 1) * LANES]
                for f in range(FIELDS)
            ]
            for f in range(FIELDS):
                for part in range(2):
                    at = pl.ds(f * 64 + k, 8, stride=8)
                    s_ref[part, at, :] = new[f][part * 8 : part * 8 + 8]
        for part in range(2):
            o_ref[2 * g + part, slot] = s_ref[part].astype(BF)

    for k in range(MEMBERS):
        build(0, k, pa)

    def step(i, _):
        group(2 * i, pa, 2 * i + 1, pb)
        group(2 * i + 1, pb, jnp.minimum(2 * i + 2, GROUPS - 1), pa)
        return 0

    lax.fori_loop(0, GROUPS // 2, step, 0)


def forecast_chunks(chunks, x, edges, weights, mix):
    cells = MEMBERS * LANES
    count = len(chunks)
    columns = [c for c in range(CHUNKS) if chunks[0] - 1 <= c <= chunks[-1] + 1]
    shape = (MEMBERS, FIELDS, ROWS, LANES)
    return pl.pallas_call(
        functools.partial(forecast_body, chunks, columns),
        grid=(1,),
        out_shape=jax.ShapeDtypeStruct((8, count, 256, LANES), BF),
        in_specs=[WHOLE] * 3 + [pl.BlockSpec(shape, lambda i, c=c: (0, 0, 0, c)) for c in columns],
        out_specs=pl.BlockSpec((8, count, 256, LANES), lambda i: (0, 0, 0, 0)),
        scratch_shapes=[VM((cells, DEPTH), BF)] * 2
        + [VM((cells, TILE), BF)] * 4
        + [VM((2, 256, LANES), F32)],
        cost_estimate=pl.CostEstimate(
            flops=count * 10_000_000_000, bytes_accessed=4_000_000, transcendentals=0
        ),
        compiler_params=LIMIT,
        name=f"forecast_{chunks[0]}",
    )(edges, stored(weights), stored(mix), *[stored(x)] * len(columns))


def analysis_body(count, slots, a_ref, *refs):
    o_ref = refs[-1]
    for n in range(count):
        f_ref, slot = refs[n], slots[n]
        for q in range(4):
            spans = [slice((q * 8 + 2 * i) * 8, (q * 8 + 2 * i) * 8 + 16) for i in range(4)]
            got = [[f_ref[m, slot, span, :].astype(F32) for m in range(8)] for span in spans]
            rows = [
                jnp.concatenate([v[h * 8 : h * 8 + 8] for v in got[i]], axis=0)
                for i in range(4)
                for h in range(2)
            ]
            states = jnp.concatenate(rows, axis=1).astype(BF)
            both = jnp.dot(a_ref[...], states, preferred_element_type=F32)
            total = both[:64] + both[64:]
            for i, span in enumerate(spans):
                for m in range(8):
                    pair = [
                        total[m * 8 : m * 8 + 8, (2 * i + h) * LANES : (2 * i + h + 1) * LANES]
                        for h in range(2)
                    ]
                    o_ref[m, n, span, :] = jnp.concatenate(pair, axis=0).astype(BF)


def analysis_chunks(update, states, slots, buffer, to, total):
    count = len(slots)
    given = [update, *[held(s) for s in states]]
    alias = {}
    if buffer is not None:
        alias = {len(given): 0}
        given.append(buffer)
    return pl.pallas_call(
        functools.partial(analysis_body, count, slots),
        grid=(1,),
        out_shape=jax.ShapeDtypeStruct((8, total, 256, LANES), BF),
        in_specs=[WHOLE] * (1 + count) + [pl.BlockSpec(memory_space=pl.ANY)] * len(alias),
        out_specs=pl.BlockSpec((8, count, 256, LANES), lambda i: (0, to // count, 0, 0)),
        input_output_aliases=alias,
        compiler_params=LIMIT,
        name=f"analysis_{to}",
    )(*given)


def observed_rows(index_ref, chunks, g_ref):
    for j in range(16):
        place = index_ref[j]
        p = lax.div(place, 4)
        rows = pl.ds(pl.multiple_of(lax.div(p, 2) * 16, 16), 16)
        odd = lax.rem(p, 2) == 1
        for c, (ref, slot) in chunks.items():

            @pl.when(lax.rem(place, 4) == c)
            def _():
                for m in range(8):
                    two = ref[m, slot, rows, :].astype(F32)
                    g_ref[m * 8 : m * 8 + 8, j * LANES : (j + 1) * LANES] = jnp.where(
                        odd, two[8:], two[:8]
                    )


def gather_body(where, index_ref, *refs):
    o_ref = refs[-1]
    observed_rows(index_ref, {c: (refs[i], slot) for c, i, slot in where}, o_ref)


def gather_part(index, where, sources):
    return pl.pallas_call(
        functools.partial(gather_body, where),
        out_shape=jax.ShapeDtypeStruct((64, 2048), F32),
        in_specs=[pl.BlockSpec(memory_space=pltpu.SMEM)] + [WHOLE] * len(sources),
        out_specs=WHOLE,
        compiler_params=LIMIT,
        name="gather",
    )(index, *[held(s) for s in sources])


def gram_body(where, index_ref, values_ref, precision_ref, so_far_ref, f_ref, o_ref, g_ref):
    g_ref[...] = so_far_ref[...]
    observed_rows(index_ref, {c: (f_ref, slot) for c, slot in where}, g_ref)
    observed = g_ref[...]
    mean = jnp.sum(observed, axis=0, keepdims=True) * (1.0 / 64)
    spread = observed - mean
    weight = jnp.concatenate([precision_ref[j : j + 1, :] for j in range(16)], axis=1)
    value = jnp.concatenate([values_ref[j : j + 1, :] for j in range(16)], axis=1)
    dot = functools.partial(
        lax.dot_general,
        dimension_numbers=(((1,), (1,)), ((), ())),
        precision=lax.Precision.HIGHEST,
        preferred_element_type=F32,
    )
    gram = dot(spread * weight, spread)
    proj = dot(jnp.broadcast_to(weight * (value - mean), (8, 2048)), spread)
    o_ref[0:32, 0:64] = gram[:32]
    o_ref[0:32, 64:128] = gram[32:]
    o_ref[32:40, 0:64] = proj
    o_ref[32:40, 64:128] = proj


def gram_part(index, values, precision, so_far, where, states):
    return pl.pallas_call(
        functools.partial(gram_body, where),
        out_shape=jax.ShapeDtypeStruct((40, LANES), F32),
        in_specs=[pl.BlockSpec(memory_space=pltpu.SMEM)] + [WHOLE] * 4,
        out_specs=WHOLE,
        scratch_shapes=[VM((64, 2048), F32)],
        compiler_params=LIMIT,
        name="gram",
    )(index, values, precision, so_far, held(states))


def place_body(slots, *refs):
    o_ref, s_ref = refs[-2:]
    for i, (which, slot) in enumerate(slots):
        for m in range(8):
            s_ref[m] = refs[which][m, slot].astype(F32)
        for k in range(MEMBERS):
            for f in range(FIELDS):
                at = pl.ds(f * 64 + k, 8, stride=8)
                for half in range(4):
                    o_ref[
                        k, f, half * 16 : half * 16 + 16, i * LANES : (i + 1) * LANES
                    ] = jnp.concatenate(
                        [s_ref[2 * half, at, :], s_ref[2 * half + 1, at, :]], axis=0
                    ).astype(BF)


def place_chunks(at, sources, slots, so_far):
    given = [held(s) for s in sources]
    alias = {}
    if so_far is not None:
        alias[len(given)] = 0
        given.append(so_far)
    wide = len(slots) * LANES
    return pl.pallas_call(
        functools.partial(place_body, slots),
        grid=(1,),
        out_shape=jax.ShapeDtypeStruct((MEMBERS, FIELDS, ROWS, COLS), BF),
        in_specs=[WHOLE] * len(sources) + [pl.BlockSpec(memory_space=pl.ANY)] * len(alias),
        out_specs=pl.BlockSpec((MEMBERS, FIELDS, ROWS, wide), lambda i: (0, 0, 0, at)),
        scratch_shapes=[VM((8, 256, LANES), F32)],
        input_output_aliases=alias,
        compiler_params=LIMIT,
        name=f"place_{at}",
    )(*given)


def sum_over(part, axis, steps):
    size = lax.axis_size(axis)
    got = [lax.ppermute(part, axis, [(i, step(i)) for i in range(size)]) for step in steps]
    return functools.reduce(lambda a, b: a + b, got, part)


def shards(
    prior_realizations,
    latent_stencil_weights,
    latent_offset,
    output_mixing_matrix,
    transform,
    mean_weights,
    obs_index,
    obs_values,
    obs_precision,
):
    count = lax.axis_size("state")
    forward = [(i, i + 1) for i in range(count - 1)]
    backward = [(i + 1, i) for i in range(count - 1)]
    low = lax.ppermute(prior_realizations[:, :, ROWS - 1, :], "state", forward)
    high = lax.ppermute(prior_realizations[:, :, 0, :], "state", backward)
    edges = jnp.concatenate([low, high], axis=1).astype(F32)

    weights, mix = product_weights(latent_stencil_weights, latent_offset, output_mixing_matrix)
    combined = transform + mean_weights[:, None]
    update = (combined + (1.0 - jnp.sum(combined, axis=0)) / 64).T
    coarse = lax.reduce_precision(update, 8, 7)
    update = jnp.concatenate([coarse, update - coarse], axis=0).astype(BF)
    index = obs_index[0, 0]

    exchange = functools.partial(
        lax.all_to_all, axis_name="mem", split_axis=0, concat_axis=0, tiled=True
    )

    def forecast(chunks, edges):
        return forecast_chunks(chunks, prior_realizations, edges, weights, mix)

    x0 = exchange(forecast((0,), edges))
    x1 = exchange(forecast((1, 2), edges))
    x2 = exchange(forecast((3,), edges))
    held4 = analysis_chunks(update, [x0], [0], None, 0, 4)
    held4 = analysis_chunks(update, [x1], [0], held4, 1, 4)
    held4 = analysis_chunks(update, [x1], [1], held4, 2, 4)
    seen = gather_part(index, [(0, 0, 0), (1, 1, 0), (2, 1, 1)], [x0, x1])
    part = gram_part(index, obs_values[0, 0], obs_precision[0, 0], seen, [(3, 0)], x2)
    held4 = analysis_chunks(update, [x2], [0], held4, 3, 4)
    held4, total = lax.optimization_barrier((held4, part))
    x4 = exchange(held4)
    for n in (1, 2, 4):
        total = sum_over(total, "state", [lambda i: i ^ n])
    total = sum_over(total, "state", [lambda i, n=n: (i + 8 * n) % 32 for n in range(1, 4)])
    x4, total = lax.optimization_barrier((x4, total))
    total = jnp.sum(exchange(jnp.broadcast_to(total[None], (8, *total.shape))), axis=0)
    analysis = place_chunks(0, [x4], [(0, 0), (0, 1), (0, 2), (0, 3)], None)
    gram = jnp.concatenate([total[:32, :64], total[:32, 64:]], axis=0) / 524288
    proj = total[32, :64] / math.sqrt(524288)
    return (analysis, gram, proj)


def solution(mesh):
    return jax.shard_map(
        shards,
        mesh=mesh,
        in_specs=(
            P("mem", None, "state", None),
            P(),
            P(),
            P(),
            P(),
            P(),
            P("state", "mem", None),
            P("state", "mem", None, None),
            P("state", "mem", None, None),
        ),
        out_specs=(P("mem", None, "state", None), P(), P()),
        check_vma=False,
    )
```

time: 213 us -> 140 us (0.66)
  waiting for transfers between devices: 56.9 us -> 32.3 us
  Pallas kernels: 84.2 us -> 62.6 us
  starting transfers between devices: 55.5 us -> 36.7 us
  local copies, waits for them, and re-layouts: 8.05 us -> 3.84 us
    all_to_all x11 -> x5, waiting for transfers between devices: 56.5 us -> 17.2 us  [the longest x1 5.53 us: shards(): x2 = exchange(forecast((3,), edges))]
    all_to_all x11 -> x5, starting transfers between devices: 45.7 us -> 19.6 us  [the longest x1 4.81 us: shards(): x1 = exchange(forecast((1, 2), edges))]
    pallas_call x13 -> x11, Pallas kernels: 84.2 us -> 62.6 us  [the longest x3 50.4 us: forecast_chunks(): pl.pallas_call(functools.partial(forecast_body, chunks, columns), grid=(1...]
    ppermute x0 -> x6, waiting for transfers between devices: none -> 15.1 us  [sum_over(): lax.ppermute(part, axis, [(i, step(i)) for i in range(size)])]
    ppermute x0 -> x6, starting transfers between devices: none -> 7.19 us  [sum_over(): lax.ppermute(part, axis, [(i, step(i)) for i in range(size)])]
    broadcast_in_dim x3 -> x2, local copies, waits for them, and re-layouts: 2.96 us -> 0.68 us  [the longest x1 0.67 us: shards(): jnp.broadcast_to(total[None], (8, *total.shape))]
  transfers between devices with their start and end apart: 13 -> 13, of which waited for: 8 -> 10; matrix products, arithmetic and copies ran while one was open for 3% -> 3% of each run, Pallas kernels for 31% -> 33%
where the time goes in v2:
time: 140 us
  Pallas kernels  62.6 us (45%)
  starting transfers between devices  36.7 us (26%)
  waiting for transfers between devices  32.3 us (23%)
  local copies, waits for them, and re-layouts  3.84 us (3%)
  other arithmetic  3.44 us (2%)
    pallas_call x3, Pallas kernels, forecast_chunks(): pl.pallas_call(functools.partial(forecast_body, chunks, columns), grid=(1...  50.4 us
    ppermute x6, waiting for transfers between devices, sum_over(): lax.ppermute(part, axis, [(i, step(i)) for i in range(size)])  15.1 us
    ppermute x1, starting transfers between devices, shards(): high = lax.ppermute(prior_realizations[:, :, 0, :], 'state', backward)  7.94 us
    ppermute x6, starting transfers between devices, sum_over(): lax.ppermute(part, axis, [(i, step(i)) for i in range(size)])  7.19 us
    all_to_all x1, waiting for transfers between devices, shards(): x2 = exchange(forecast((3,), edges))  5.53 us
    pallas_call x4, Pallas kernels, analysis_chunks(): pl.pallas_call(functools.partial(analysis_body, count, slots), grid=(1,),...  4.84 us
    all_to_all x1, starting transfers between devices, shards(): x1 = exchange(forecast((1, 2), edges))  4.81 us
    all_to_all x1, waiting for transfers between devices, shards(): x4 = exchange(held4)  4.78 us
  transfers between devices with their start and end apart: 13, of which 10 were waited for; matrix products, arithmetic and copies ran while one was open for 3% of the time, Pallas kernels for 33%

profile of v2, /device:TPU:24, one launch (start us, length us, event | category | flops | bytes accessed | tf_op | source)
XLA Modules:
  0.0 139.7 jit_solution(5397927821064898132)
XLA Ops:
  0.6 1.1 fusion.7
  1.8 7.9 %collective-permute-start.1 = (bf16[8,4,512]{2,1,0:T(4,128)(2,1)S(1)}, bf16[8,4,512]{2,1,0:T(4,128)(2,1)S(1)}, u32[]{:S(2)}, u32[]{:S(2)}) collective-permute-start(bf16[8,4,512]{2,1,0:T(4,128)(2,1)S(1)} %bitcast.28), channel_id=1, source_target_pairs={{1,0},{2,1},{3,2},{4,3},{5,4},{6,5},{7,6},{8,7},{9,8},{10,9},{11,1... | collective-permute-start | bytes 98312 | tf_op jit(solution)/shard_map/ppermute | solution.py:381
  9.8 1.9 %collective-permute-start = (bf16[8,4,512]{2,1,0:T(4,128)(2,1)S(1)}, bf16[8,4,512]{2,1,0:T(4,128)(2,1)S(1)}, u32[]{:S(2)}, u32[]{:S(2)}) collective-permute-start(bf16[8,4,512]{2,1,0:T(4,128)(2,1)S(1)} %bitcast.29), channel_id=1, source_target_pairs={{0,1},{1,2},{2,3},{3,4},{4,5},{5,6},{6,7},{7,8},{8,9},{9,10},{10,1... | collective-permute-start | bytes 98312 | tf_op jit(solution)/shard_map/ppermute | solution.py:380
  13.1 0.8 copy.19
  13.9 0.8 add_reduce_fusion
  14.7 0.8 copy.22
  15.8 2.2 %weights.1 = (bf16[224,2176]{1,0:T(8,128)(2,1)}, bf16[2048,64]{1,0:T(8,128)(2,1)}) custom-call(bf16[128,128]{1,0:T(8,128)(2,1)S(1)} %concatenate.16.rows_ref, f32[128,4]{1,0:T(8,128)S(1)} %bitcast.23), custom_call_target="tpu_custom_call" | custom-call | tf_op jit(solution)/shard_map/weights/pallas_call | solution.py:80
  18.0 13.1 %forecast_0.1 = bf16[8,1,256,128]{3,2,1,0:T(8,128)(2,1)} custom-call(f32[8,8,512]{2,1,0:T(8,128)S(1)} %maximum_convert_fusion.edge_ref, bf16[224,2176]{1,0:T(8,128)(2,1)} %get-tuple-element.9.w_ref, bf16[2048,64]{1,0:T(8,128)(2,1)} %get-tuple-element.10.mix_ref, bf16[8,4,64,512]{3,2,1,0:T(8,128)(2,1)} %refs_1_.5, bf16[8,4,64,512]{3,2,1,0:T(8,128)(2,1)} %refs_1_.5), custom_call_target="tpu_custom_call" | custom-call | flops 10000000000 | bytes 4000000 | tf_op jit(solution)/shard_map/forecast_0/pallas_call | solution.py:197
  31.1 4.3 %all-to-all-start.2 = ((bf16[8,1,256,128]{3,2,1,0:T(8,128)(2,1)}), bf16[8,1,256,128]{3,2,1,0:T(8,128)(2,1)S(1)}, u32[]{:S(2)}, u32[]{:S(2)}) async-start(bf16[8,1,256,128]{3,2,1,0:T(8,128)(2,1)} %forecast_0.1), calls=%async_computation.2 | async-start | bytes 1048576 | tf_op jit(solution)/shard_map/all_to_all | solution.py:398
  35.4 24.3 %forecast_1.1 = bf16[8,2,256,128]{3,2,1,0:T(8,128)(2,1)} custom-call(f32[8,8,512]{2,1,0:T(8,128)S(1)} %maximum_convert_fusion.edge_ref, bf16[224,2176]{1,0:T(8,128)(2,1)} %get-tuple-element.9.w_ref, bf16[2048,64]{1,0:T(8,128)(2,1)} %get-tuple-element.10.mix_ref, bf16[8,4,64,512]{3,2,1,0:T(8,128)(2,1)} %refs_1_.5, bf16[8,4,64,512]{3,2,1,0:T(8,128)(2,1)} %refs_1_.5, ...), custom_call_target="tpu_custom_call" | custom-call | flops 20000000000 | bytes 4000000 | tf_op jit(solution)/shard_map/forecast_1/pallas_call | solution.py:197
  59.7 4.8 %all-to-all-start.1 = ((bf16[8,2,256,128]{3,2,1,0:T(8,128)(2,1)}), bf16[8,2,256,128]{3,2,1,0:T(8,128)(2,1)S(1)}, u32[]{:S(2)}, u32[]{:S(2)}) async-start(bf16[8,2,256,128]{3,2,1,0:T(8,128)(2,1)} %forecast_1.1), calls=%async_computation.1 | async-start | bytes 2097152 | tf_op jit(solution)/shard_map/all_to_all | solution.py:399
  64.5 13.1 %forecast_3.1 = bf16[8,1,256,128]{3,2,1,0:T(8,128)(2,1)} custom-call(f32[8,8,512]{2,1,0:T(8,128)S(1)} %maximum_convert_fusion.edge_ref, bf16[224,2176]{1,0:T(8,128)(2,1)} %get-tuple-element.9.w_ref, bf16[2048,64]{1,0:T(8,128)(2,1)} %get-tuple-element.10.mix_ref, bf16[8,4,64,512]{3,2,1,0:T(8,128)(2,1)} %refs_1_.5, bf16[8,4,64,512]{3,2,1,0:T(8,128)(2,1)} %refs_1_.5), custom_call_target="tpu_custom_call" | custom-call | flops 10000000000 | bytes 4000000 | tf_op jit(solution)/shard_map/forecast_3/pallas_call | solution.py:197
  77.6 2.9 %all-to-all-done.1.refs_0_.refs_1_ = bf16[8,2,256,128]{3,2,1,0:T(8,128)(2,1)S(1)} async-done(((bf16[8,2,256,128]{3,2,1,0:T(8,128)(2,1)}), bf16[8,2,256,128]{3,2,1,0:T(8,128)(2,1)S(1)}, u32[]{:S(2)}, u32[]{:S(2)}) %all-to-all-start.1) | async-done | bytes 1048608 | tf_op jit(solution)/shard_map/all_to_all | solution.py:399
  80.4 3.5 %all-to-all-start = ((bf16[8,1,256,128]{3,2,1,0:T(8,128)(2,1)}), bf16[8,1,256,128]{3,2,1,0:T(8,128)(2,1)S(1)}, u32[]{:S(2)}, u32[]{:S(2)}) async-start(bf16[8,1,256,128]{3,2,1,0:T(8,128)(2,1)} %forecast_3.1), calls=%async_computation | async-start | bytes 1048576 | tf_op jit(solution)/shard_map/all_to_all | solution.py:400
  84.1 1.2 analysis_0.1.refs_1_
  85.3 1.0 gather.1.so_far_ref
  86.3 1.2 analysis_1.1.refs_1_
  87.5 1.2 analysis_2.1.refs_1_
  88.7 5.5 %all-to-all-done.refs_0_.f_ref = bf16[8,1,256,128]{3,2,1,0:T(8,128)(2,1)S(1)} async-done(((bf16[8,1,256,128]{3,2,1,0:T(8,128)(2,1)}), bf16[8,1,256,128]{3,2,1,0:T(8,128)(2,1)S(1)}, u32[]{:S(2)}, u32[]{:S(2)}) %all-to-all-start) | async-done | bytes 524320 | tf_op jit(solution)/shard_map/all_to_all | solution.py:400
  94.2 1.2 analysis_3.1
  95.4 1.8 %gram.1 = f32[40,128]{1,0:T(8,128)S(1)} custom-call(s32[16]{0:T(128)S(1)} %bitcast.27, f32[16,128]{1,0:T(8,128)S(1)} %bitcast.24, f32[16,128]{1,0:T(8,128)S(1)} %bitcast.25, f32[64,2048]{1,0:T(8,128)S(1)} %gather.1.so_far_ref, bf16[8,1,256,128]{3,2,1,0:T(8,128)(2,1)S(1)} %all-to-all-done.refs_0_.f_ref), custom_call_target="tpu_custom_call" | custom-call | tf_op jit(solution)/shard_map/gram/pallas_call | solution.py:313
  97.2 3.6 %all-to-all-start.3 = ((bf16[8,4,256,128]{3,2,1,0:T(8,128)(2,1)}), bf16[8,4,256,128]{3,2,1,0:T(8,128)(2,1)S(1)}, u32[]{:S(2)}, u32[]{:S(2)}) async-start(bf16[8,4,256,128]{3,2,1,0:T(8,128)(2,1)} %analysis_3.1), calls=%async_computation.3 | async-start | bytes 4194304 | tf_op jit(solution)/shard_map/all_to_all | solution.py:408
  100.9 3.8 %collective-permute-done.2 = f32[40,128]{1,0:T(8,128)S(1)} collective-permute-done((f32[40,128]{1,0:T(8,128)S(1)}, f32[40,128]{1,0:T(8,128)S(1)}, u32[]{:S(2)}, u32[]{:S(2)}) %collective-permute-start.2) | collective-permute-done | bytes 20512 | tf_op jit(solution)/shard_map/ppermute | solution.py:362
  105.1 4.3 %collective-permute-done.3 = f32[40,128]{1,0:T(8,128)S(1)} collective-permute-done((f32[40,128]{1,0:T(8,128)S(1)}, f32[40,128]{1,0:T(8,128)S(1)}, u32[]{:S(2)}, u32[]{:S(2)}) %collective-permute-start.3) | collective-permute-done | bytes 20512 | tf_op jit(solution)/shard_map/ppermute | solution.py:362
  109.4 3.2 %collective-permute-start.4 = (f32[40,128]{1,0:T(8,128)S(1)}, f32[40,128]{1,0:T(8,128)S(1)}, u32[]{:S(2)}, u32[]{:S(2)}) collective-permute-start(f32[40,128]{1,0:T(8,128)S(1)} %add.39), channel_id=1, source_target_pairs={{0,4},{1,5},{2,6},{3,7},{4,0},{5,1},{6,2},{7,3},{8,12},{9,13},{10,... | collective-permute-start | bytes 61448 | tf_op jit(solution)/shard_map/ppermute | solution.py:362
  112.6 4.5 %collective-permute-done.4 = f32[40,128]{1,0:T(8,128)S(1)} collective-permute-done((f32[40,128]{1,0:T(8,128)S(1)}, f32[40,128]{1,0:T(8,128)S(1)}, u32[]{:S(2)}, u32[]{:S(2)}) %collective-permute-start.4) | collective-permute-done | bytes 20512 | tf_op jit(solution)/shard_map/ppermute | solution.py:362
  118.1 2.5 %collective-permute-start.5 = (f32[40,128]{1,0:T(8,128)S(1)}, f32[40,128]{1,0:T(8,128)S(1)}, u32[]{:S(2)}, u32[]{:S(2)}) collective-permute-start(f32[40,128]{1,0:T(8,128)S(1)} %add.40), channel_id=1, source_target_pairs={{0,8},{1,9},{2,10},{3,11},{4,12},{5,13},{6,14},{7,15},{8,16},{9,17... | collective-permute-start | bytes 61448 | tf_op jit(solution)/shard_map/ppermute | solution.py:362
  120.7 1.4 %collective-permute-done.7 = f32[40,128]{1,0:T(8,128)S(1)} collective-permute-done((f32[40,128]{1,0:T(8,128)S(1)}, f32[40,128]{1,0:T(8,128)S(1)}, u32[]{:S(2)}, u32[]{:S(2)}) %collective-permute-start.7) | collective-permute-done | bytes 20512 | tf_op jit(solution)/shard_map/ppermute | solution.py:362
  123.2 4.8 %all-to-all-done.3.refs_0_ = bf16[8,4,256,128]{3,2,1,0:T(8,128)(2,1)S(1)} async-done(((bf16[8,4,256,128]{3,2,1,0:T(8,128)(2,1)}), bf16[8,4,256,128]{3,2,1,0:T(8,128)(2,1)S(1)}, u32[]{:S(2)}, u32[]{:S(2)}) %all-to-all-start.3) | async-done | bytes 2097184 | tf_op jit(solution)/shard_map/all_to_all | solution.py:408
  128.6 3.4 %all-to-all-start.4 = ((f32[8,40,128]{2,1,0:T(8,128)}), f32[8,40,128]{2,1,0:T(8,128)S(1)}, u32[]{:S(2)}, u32[]{:S(2)}) async-start(f32[8,40,128]{2,1,0:T(8,128)} %broadcast_in_dim.5), calls=%async_computation.4 | async-start | bytes 327680 | tf_op jit(solution)/shard_map/all_to_all | solution.py:413
  132.0 2.4 %place_0.1 = bf16[8,4,64,512]{3,2,1,0:T(8,128)(2,1)} custom-call(bf16[8,4,256,128]{3,2,1,0:T(8,128)(2,1)S(1)} %all-to-all-done.3.refs_0_), custom_call_target="tpu_custom_call" | custom-call | tf_op jit(solution)/shard_map/place_0/pallas_call | solution.py:347
  134.5 4.0 %all-to-all-done.4 = f32[8,40,128]{2,1,0:T(8,128)S(1)} async-done(((f32[8,40,128]{2,1,0:T(8,128)}), f32[8,40,128]{2,1,0:T(8,128)S(1)}, u32[]{:S(2)}, u32[]{:S(2)}) %all-to-all-start.4) | async-done | bytes 163872 | tf_op jit(solution)/shard_map/all_to_all | solution.py:413
  (36 shorter events, 6.3 us)
Async XLA Ops:
  1.8 16.2 %collective-permute-start.1 = (bf16[8,4,512]{2,1,0:T(4,128)(2,1)S(1)}, bf16[8,4,512]{2,1,0:T(4,128)(2,1)S(1)}, u32[]{:S(2)}, u32[]{:S(2)}) collective-permute-start(bf16[8,4,512]{2,1,0:T(4,128)(2,1)S(1)} %bitcast.28), channel_id=1, source_target_pairs={{1,0},{2,1},{3,2},{4,3},{5,4},{6,5},{7,6},{8,7},{9,8},{10,9},{11,1... | collective-permute-start | bytes 98312 | tf_op jit(solution)/shard_map/ppermute | solution.py:381
  9.8 8.2 %collective-permute-start = (bf16[8,4,512]{2,1,0:T(4,128)(2,1)S(1)}, bf16[8,4,512]{2,1,0:T(4,128)(2,1)S(1)}, u32[]{:S(2)}, u32[]{:S(2)}) collective-permute-start(bf16[8,4,512]{2,1,0:T(4,128)(2,1)S(1)} %bitcast.29), channel_id=1, source_target_pairs={{0,1},{1,2},{2,3},{3,4},{4,5},{5,6},{6,7},{7,8},{8,9},{9,10},{10,1... | collective-permute-start | bytes 98312 | tf_op jit(solution)/shard_map/ppermute | solution.py:380
  31.1 28.6 %all-to-all-start.2 = ((bf16[8,1,256,128]{3,2,1,0:T(8,128)(2,1)}), bf16[8,1,256,128]{3,2,1,0:T(8,128)(2,1)S(1)}, u32[]{:S(2)}, u32[]{:S(2)}) async-start(bf16[8,1,256,128]{3,2,1,0:T(8,128)(2,1)} %forecast_0.1), calls=%async_computation.2 | async-start | bytes 1048576 | tf_op jit(solution)/shard_map/all_to_all | solution.py:398
  59.7 20.8 %all-to-all-start.1 = ((bf16[8,2,256,128]{3,2,1,0:T(8,128)(2,1)}), bf16[8,2,256,128]{3,2,1,0:T(8,128)(2,1)S(1)}, u32[]{:S(2)}, u32[]{:S(2)}) async-start(bf16[8,2,256,128]{3,2,1,0:T(8,128)(2,1)} %forecast_1.1), calls=%async_computation.1 | async-start | bytes 2097152 | tf_op jit(solution)/shard_map/all_to_all | solution.py:399
  64.5 19.5 %copy-start.3 = (f32[64]{0:T(128)S(1)}, f32[64]{0:T(128)}, u32[]{:S(2)}) copy-start(f32[64]{0:T(128)} %param.14) | copy-start | bytes 772
  77.6 7.7 %copy-start.2 = (s32[1,1,16]{2,1,0:T(1,128)S(1)}, s32[1,1,16]{2,1,0:T(1,128)}, u32[]{:S(2)}) copy-start(s32[1,1,16]{2,1,0:T(1,128)} %param.15) | copy-start | bytes 196
  80.4 13.8 %all-to-all-start = ((bf16[8,1,256,128]{3,2,1,0:T(8,128)(2,1)}), bf16[8,1,256,128]{3,2,1,0:T(8,128)(2,1)S(1)}, u32[]{:S(2)}, u32[]{:S(2)}) async-start(bf16[8,1,256,128]{3,2,1,0:T(8,128)(2,1)} %forecast_3.1), calls=%async_computation | async-start | bytes 1048576 | tf_op jit(solution)/shard_map/all_to_all | solution.py:400
  88.7 6.7 %copy-start = (f32[1,1,16,128]{3,2,1,0:T(8,128)S(1)}, f32[1,1,16,128]{3,2,1,0:T(8,128)}, u32[]{:S(2)}) copy-start(f32[1,1,16,128]{3,2,1,0:T(8,128)} %param.16) | copy-start | bytes 24580
  88.7 6.7 %copy-start.1 = (f32[1,1,16,128]{3,2,1,0:T(8,128)S(1)}, f32[1,1,16,128]{3,2,1,0:T(8,128)}, u32[]{:S(2)}) copy-start(f32[1,1,16,128]{3,2,1,0:T(8,128)} %param.17) | copy-start | bytes 24580
  97.2 30.8 %all-to-all-start.3 = ((bf16[8,4,256,128]{3,2,1,0:T(8,128)(2,1)}), bf16[8,4,256,128]{3,2,1,0:T(8,128)(2,1)S(1)}, u32[]{:S(2)}, u32[]{:S(2)}) async-start(bf16[8,4,256,128]{3,2,1,0:T(8,128)(2,1)} %analysis_3.1), calls=%async_computation.3 | async-start | bytes 4194304 | tf_op jit(solution)/shard_map/all_to_all | solution.py:408
  100.8 3.9 %collective-permute-start.2 = (f32[40,128]{1,0:T(8,128)S(1)}, f32[40,128]{1,0:T(8,128)S(1)}, u32[]{:S(2)}, u32[]{:S(2)}) collective-permute-start(f32[40,128]{1,0:T(8,128)S(1)} %gram.1), channel_id=1, source_target_pairs={{0,1},{1,0},{2,3},{3,2},{4,5},{5,4},{6,7},{7,6},{8,9},{9,8},{10,11... | collective-permute-start | bytes 61448 | tf_op jit(solution)/shard_map/ppermute | solution.py:362
  104.7 4.7 %collective-permute-start.3 = (f32[40,128]{1,0:T(8,128)S(1)}, f32[40,128]{1,0:T(8,128)S(1)}, u32[]{:S(2)}, u32[]{:S(2)}) collective-permute-start(f32[40,128]{1,0:T(8,128)S(1)} %add.38), channel_id=1, source_target_pairs={{0,2},{1,3},{2,0},{3,1},{4,6},{5,7},{6,4},{7,5},{8,10},{9,11},{10,... | collective-permute-start | bytes 61448 | tf_op jit(solution)/shard_map/ppermute | solution.py:362
  109.4 7.7 %collective-permute-start.4 = (f32[40,128]{1,0:T(8,128)S(1)}, f32[40,128]{1,0:T(8,128)S(1)}, u32[]{:S(2)}, u32[]{:S(2)}) collective-permute-start(f32[40,128]{1,0:T(8,128)S(1)} %add.39), channel_id=1, source_target_pairs={{0,4},{1,5},{2,6},{3,7},{4,0},{5,1},{6,2},{7,3},{8,12},{9,13},{10,... | collective-permute-start | bytes 61448 | tf_op jit(solution)/shard_map/ppermute | solution.py:362
  117.1 5.0 %collective-permute-start.7 = (f32[40,128]{1,0:T(8,128)S(1)}, f32[40,128]{1,0:T(8,128)S(1)}, u32[]{:S(2)}, u32[]{:S(2)}) collective-permute-start(f32[40,128]{1,0:T(8,128)S(1)} %add.40), channel_id=1, source_target_pairs={{0,24},{1,25},{2,26},{3,27},{4,28},{5,29},{6,30},{7,31},{8,0},{9,1... | collective-permute-start | bytes 61448 | tf_op jit(solution)/shard_map/ppermute | solution.py:362
  117.6 5.3 %collective-permute-start.6 = (f32[40,128]{1,0:T(8,128)S(1)}, f32[40,128]{1,0:T(8,128)S(1)}, u32[]{:S(2)}, u32[]{:S(2)}) collective-permute-start(f32[40,128]{1,0:T(8,128)S(1)} %add.40), channel_id=1, source_target_pairs={{0,16},{1,17},{2,18},{3,19},{4,20},{5,21},{6,22},{7,23},{8,24},{9,... | collective-permute-start | bytes 61448 | tf_op jit(solution)/shard_map/ppermute | solution.py:362
  118.1 5.0 %collective-permute-start.5 = (f32[40,128]{1,0:T(8,128)S(1)}, f32[40,128]{1,0:T(8,128)S(1)}, u32[]{:S(2)}, u32[]{:S(2)}) collective-permute-start(f32[40,128]{1,0:T(8,128)S(1)} %add.40), channel_id=1, source_target_pairs={{0,8},{1,9},{2,10},{3,11},{4,12},{5,13},{6,14},{7,15},{8,16},{9,17... | collective-permute-start | bytes 61448 | tf_op jit(solution)/shard_map/ppermute | solution.py:362
  128.6 9.8 %all-to-all-start.4 = ((f32[8,40,128]{2,1,0:T(8,128)}), f32[8,40,128]{2,1,0:T(8,128)S(1)}, u32[]{:S(2)}, u32[]{:S(2)}) async-start(f32[8,40,128]{2,1,0:T(8,128)} %broadcast_in_dim.5), calls=%async_computation.4 | async-start | bytes 327680 | tf_op jit(solution)/shard_map/all_to_all | solution.py:413

commit v3 on v2

--- a/solution.py
+++ b/solution.py
@@ -21,7 +21,9 @@
 GROUP = 16
 GROUPS = ROWS // GROUP
 DEPTH = 224
+HOME_DEPTH = 128
 CHUNKS = 4
+RAW = 48
 LANES = 128
 TILE = 256
 GELU_A = math.sqrt(2.0 / math.pi)
@@ -39,68 +41,87 @@
 WHOLE = pl.BlockSpec(memory_space=VM)
 
 
-def weights_body(rows_ref, mix_ref, w_ref, m_ref):
-    k = lax.broadcasted_iota(jnp.int32, (DEPTH, LANES), 0)
-    j = lax.broadcasted_iota(jnp.int32, (DEPTH, LANES), 1)
-    b, f, row = k // 64, (k // 16) % 4, k % 16
-    edge = k - 192
+def product_weights(height, rows, mixing, w_ref, m_ref):
+    inner, depth = 12 * height, 12 * height + 32
+    k = lax.broadcasted_iota(jnp.int32, (depth, LANES), 0)
+    j = lax.broadcasted_iota(jnp.int32, (depth, LANES), 1)
+    b, f, row = k // (4 * height), (k // height) % 4, k % height
+    edge = k - inner
     edge_b, below, edge_f = edge // 8, (edge // 4) % 2, edge % 4
     lanes = lax.broadcasted_iota(jnp.int32, (HID, LANES), 1)
-    linear = jnp.zeros((DEPTH, LANES), F32)
-    for r in range(GROUP):
+    linear = jnp.zeros((depth, LANES), F32)
+    width = FIELDS * height
+    for r in range(height):
         inside = jnp.where(jnp.abs(row - r) <= 1, (3 * (row - r + 1) + b) * 4 + f, -1)
         border = (below * 6 + edge_b) * 4 + edge_f
-        border = jnp.where(below * (GROUP - 1) == r, border, -1)
-        want = jnp.where(k < 192, inside, jnp.where(k < 216, border, k - 180))
+        border = jnp.where(below * (height - 1) == r, border, -1)
+        want = jnp.where(k < inner, inside, jnp.where(edge < 24, border, edge + 12))
         chosen = jnp.where(j == want, 1.0, 0.0).astype(BF)
-        part = jnp.dot(chosen, rows_ref[...], preferred_element_type=F32).astype(BF)
+        part = jnp.dot(chosen, rows, preferred_element_type=F32).astype(BF)
         w_ref[:, r * HID : (r + 1) * HID] = part
         spread = jnp.zeros((HID, LANES), F32)
         for field in range(FIELDS):
-            spread = jnp.where(lanes == field * GROUP + r, mix_ref[:, field : field + 1], spread)
+            spread = jnp.where(lanes == field * height + r, mixing[:, field : field + 1], spread)
         spread = spread.astype(BF)
-        m_ref[r * HID : (r + 1) * HID, :] = spread[:, :64]
+        m_ref[r * HID : (r + 1) * HID, :] = spread[:, :width]
         linear = linear + jnp.dot(part, spread, preferred_element_type=F32)
-    linear = linear[:, :64]
+    linear = linear[:, :width]
     coarse = linear.astype(BF)
-    w_ref[:, GROUP * HID :] = jnp.concatenate(
-        [coarse, (linear - coarse.astype(F32)).astype(BF)], axis=1
-    )
-
-
-def product_weights(stencil, offset, mixing):
-    half = 0.5 * offset
-    cut = functools.partial(lax.reduce_precision, exponent_bits=8, mantissa_bits=7)
-    first = cut(half)
-    second = cut(half - first)
-    third = half - first - second
-    rows = jnp.concatenate(
-        [0.5 * stencil.astype(F32).T, jnp.stack([first, second, third]), jnp.zeros((89, HID), F32)]
-    ).astype(BF)
+    fine = (linear - coarse.astype(F32)).astype(BF)
+    w_ref[:, height * HID : height * HID + 2 * width] = jnp.concatenate([coarse, fine], axis=1)
+
+
+def weights_body(
+    stencil_ref, offset_ref, mixing_ref, transform_ref, mean_ref, w_ref, m_ref, hw_ref, hm_ref, u_ref
+):
+    stencil = 0.5 * stencil_ref[...].astype(F32)
+    rows = jnp.concatenate([stencil, jnp.zeros((HID, LANES - 36), F32)], axis=1).T
+    rest = 0.5 * offset_ref[...]
+    for i in range(3):
+        cut = rest.astype(BF).astype(F32)
+        rest = rest - cut
+        rows = jnp.where(lax.broadcasted_iota(jnp.int32, rows.shape, 0) == 36 + i, cut, rows)
+    mixing = mixing_ref[...].astype(F32)
+    mixing = jnp.concatenate([mixing, jnp.zeros((LANES - FIELDS, HID), F32)], axis=0).T
+    product_weights(GROUP, rows.astype(BF), mixing, w_ref, m_ref)
+    product_weights(8, rows.astype(BF), mixing, hw_ref, hm_ref)
+    wide = jnp.concatenate([transform_ref[...], jnp.zeros((64, 64), F32)], axis=1)
+    turned = jnp.concatenate([wide, jnp.zeros((64, LANES), F32)], axis=0).T[:64, :64]
+    update = turned + mean_ref[...]
+    update = update + (1.0 - jnp.sum(update, axis=1, keepdims=True)) * (1.0 / 64)
+    coarse = update.astype(BF)
+    u_ref[:64, :] = coarse
+    u_ref[64:, :] = (update - coarse.astype(F32)).astype(BF)
+
+
+def all_weights(stencil, offset, mixing, transform, mean_weights):
     return pl.pallas_call(
         weights_body,
         out_shape=(
             pltpu.HBM((DEPTH, GROUP * HID + LANES), BF),
             pltpu.HBM((GROUP * HID, 64), BF),
+            pltpu.HBM((HOME_DEPTH, 8 * HID + LANES), BF),
+            pltpu.HBM((8 * HID, 32), BF),
+            pltpu.HBM((LANES, 64), BF),
         ),
-        in_specs=[WHOLE] * 2,
-        out_specs=(WHOLE, WHOLE),
+        in_specs=[WHOLE] * 5,
+        out_specs=(WHOLE,) * 5,
         compiler_params=LIMIT,
         name="weights",
-    )(rows, mixing.astype(F32).T)
-
-
-def forecast_body(chunks, columns, edge_ref, w_ref, mix_ref, *refs):
+    )(*map(stored, (stencil, offset[None], mixing, transform, mean_weights[None])))
+
+
+def forecast_body(chunks, columns, raw, edge_ref, w_ref, mix_ref, *refs):
     windows, (o_ref, pa, pb, va, vb, ha, hb, s_ref) = refs[: len(columns)], refs[len(columns) :]
     windows = dict(zip(columns, windows))
     for slot, c in enumerate(chunks):
         forecast_block(
-            c, slot, windows, edge_ref, w_ref, mix_ref, o_ref, pa, pb, va, vb, ha, hb, s_ref
+            c, slot, windows, raw, edge_ref, w_ref, mix_ref, o_ref, pa, pb, va, vb, ha, hb, s_ref
         )
 
 
 def forecast_block(
-    c, slot, windows, edge_ref, w_ref, mix_ref, o_ref, pa, pb, va, vb, ha, hb, s_ref
+    c, slot, windows, raw, edge_ref, w_ref, mix_ref, o_ref, pa, pb, va, vb, ha, hb, s_ref
 ):
     lane = lax.broadcasted_iota(jnp.int32, (1, LANES), 1)
     row8 = lax.broadcasted_iota(jnp.int32, (8, LANES), 0)
@@ -136,6 +157,33 @@
         parts = [inner[f][b] for b in range(3) for f in range(FIELDS)]
         parts += [*three(lambda cc: border(k, g, cc)), ones]
         to[k * LANES : (k + 1) * LANES, :] = jnp.concatenate(parts, axis=0).astype(BF).T
+
+    def pack(g, k, part):
+        last = CHUNKS - 1
+        here = slice(part * 8, part * 8 + 8)
+        above, below = jnp.maximum(g - 1, 0), jnp.minimum(g + 1, GROUPS - 1)
+
+        def outer(cc):
+            out = edge_ref[k, :, cc * LANES : (cc + 1) * LANES]
+            for f in range(FIELDS):
+                inner = block(k, f, g, cc)
+                up = inner[:8] if part else block(k, f, above, cc)[8:]
+                down = block(k, f, below, cc)[:8] if part else inner[8:]
+                out = jnp.where((row8 == f) & (part + g > 0), pltpu.roll(up, (f + 1) % 8, 0), out)
+                use = (row8 == 4 + f) & (g + part < GROUPS)
+                out = jnp.where(use, pltpu.roll(down, 4 + f, 0), out)
+            return out
+
+        main = [block(k, f, g, last)[here] for f in range(FIELDS)]
+        left = [block(k, f, g, last - 1)[here] for f in range(FIELDS)] + [outer(last - 1)]
+        column = jnp.zeros((8, LANES), F32)
+        for n, v in enumerate(left):
+            column = jnp.where(lane == n, pltpu.roll(v, n + 1, 1), column)
+        main += [outer(last), column]
+        for i in range(3):
+            o_ref[2 * g + part, 256 + k * RAW + i * 16 : 272 + k * RAW + i * 16, :] = (
+                jnp.concatenate(main[2 * i : 2 * i + 2], axis=0).astype(BF)
+            )
 
     tiles = GROUP * HID // TILE
     held_v, held_h = (va, vb), (ha, hb)
@@ -157,6 +205,9 @@
                 bend = jnp.tanh(h * (h * h * BF(8 * GELU_B) + BF(2 * GELU_A)))
                 held_h[n % 2][...] = h * bend
                 build(following, n, to)
+                if raw:
+                    pack(g, n, 0)
+                    pack(g, n, 1)
             if n >= 1:
                 total = total + jnp.dot(
                     held_h[(n - 1) % 2][...],
@@ -176,7 +227,7 @@
                     at = pl.ds(f * 64 + k, 8, stride=8)
                     s_ref[part, at, :] = new[f][part * 8 : part * 8 + 8]
         for part in range(2):
-            o_ref[2 * g + part, slot] = s_ref[part].astype(BF)
+            o_ref[2 * g + part, slot * 256 : slot * 256 + 256, :] = s_ref[part].astype(BF)
 
     for k in range(MEMBERS):
         build(0, k, pa)
@@ -189,17 +240,19 @@
     lax.fori_loop(0, GROUPS // 2, step, 0)
 
 
-def forecast_chunks(chunks, x, edges, weights, mix):
+def forecast_chunks(chunks, raw, x, edges, weights, mix):
     cells = MEMBERS * LANES
     count = len(chunks)
-    columns = [c for c in range(CHUNKS) if chunks[0] - 1 <= c <= chunks[-1] + 1]
-    shape = (MEMBERS, FIELDS, ROWS, LANES)
+    low, high = chunks[0] - 1, CHUNKS - 1 if raw else chunks[-1] + 1
+    columns = [c for c in range(CHUNKS) if low <= c <= high]
+    window = (MEMBERS, FIELDS, ROWS, LANES)
+    shape = (8, count * 256 + raw * MEMBERS * RAW, LANES)
     return pl.pallas_call(
-        functools.partial(forecast_body, chunks, columns),
+        functools.partial(forecast_body, chunks, columns, raw),
         grid=(1,),
-        out_shape=jax.ShapeDtypeStruct((8, count, 256, LANES), BF),
-        in_specs=[WHOLE] * 3 + [pl.BlockSpec(shape, lambda i, c=c: (0, 0, 0, c)) for c in columns],
-        out_specs=pl.BlockSpec((8, count, 256, LANES), lambda i: (0, 0, 0, 0)),
+        out_shape=jax.ShapeDtypeStruct(shape, BF),
+        in_specs=[WHOLE] * 3 + [pl.BlockSpec(window, lambda i, c=c: (0, 0, 0, c)) for c in columns],
+        out_specs=pl.BlockSpec(shape, lambda i: (0, 0, 0)),
         scratch_shapes=[VM((cells, DEPTH), BF)] * 2
         + [VM((cells, TILE), BF)] * 4
         + [VM((2, 256, LANES), F32)],
@@ -211,13 +264,109 @@
     )(edges, stored(weights), stored(mix), *[stored(x)] * len(columns))
 
 
+def home_body(x_ref, w_ref, mix_ref, o_ref, pa, pb, va, vb, ha, hb, s_ref):
+    lane = lax.broadcasted_iota(jnp.int32, (1, LANES), 1)
+    row8 = lax.broadcasted_iota(jnp.int32, (8, LANES), 0)
+    ones = jnp.where(row8 < 3, 1.0, 0.0).astype(F32)
+    last = LANES - 1
+
+    def raw(m, k):
+        got = [x_ref[m, 256 + k * RAW + i * 16 : 272 + k * RAW + i * 16, :] for i in range(3)]
+        got = [v.astype(F32) for v in got]
+        return [got[i // 2][i % 2 * 8 : i % 2 * 8 + 8] for i in range(6)]
+
+    def build(m, k, to):
+        *blocks, column = raw(m, k)
+        three = []
+        for n, mid in enumerate(blocks):
+            first = pltpu.roll(column, (LANES - n) % LANES, 1)
+            three.append(
+                (
+                    jnp.where(lane == 0, first, pltpu.roll(mid, 1, 1)),
+                    mid,
+                    jnp.where(lane == last, 0.0, pltpu.roll(mid, last, 1)),
+                )
+            )
+        parts = [three[f][b] for b in range(3) for f in range(FIELDS)]
+        parts += [*three[FIELDS], ones]
+        to[k * LANES : (k + 1) * LANES, :] = jnp.concatenate(parts, axis=0).astype(BF).T
+
+    tiles = 8 * HID // TILE
+    held_v, held_h = (va, vb), (ha, hb)
+
+    def group(m, patches, following, to):
+        def before(n):
+            held_v[n % 2][...] = jnp.dot(
+                patches[...], w_ref[:, n * TILE : (n + 1) * TILE], preferred_element_type=F32
+            ).astype(BF)
+
+        linear = jnp.dot(patches[...], w_ref[:, 8 * HID :], preferred_element_type=F32)
+        total = linear[:, :32] + linear[:, 32:64]
+        before(0)
+        for n in range(tiles + 1):
+            if n + 1 < tiles:
+                before(n + 1)
+            if n < tiles:
+                h = held_v[n % 2][...]
+                bend = jnp.tanh(h * (h * h * BF(8 * GELU_B) + BF(2 * GELU_A)))
+                held_h[n % 2][...] = h * bend
+                build(following, 2 * n, to)
+                build(following, 2 * n + 1, to)
+            if n >= 1:
+                total = total + jnp.dot(
+                    held_h[(n - 1) % 2][...],
+                    mix_ref[(n - 1) * TILE : n * TILE, :],
+                    preferred_element_type=F32,
+                )
+        moved = total.T
+        for k in range(MEMBERS):
+            main = raw(m, k)
+            for f in range(FIELDS):
+                s_ref[pl.ds(f * 64 + k, 8, stride=8), :] = (
+                    main[f] + moved[f * 8 : f * 8 + 8, k * LANES : (k + 1) * LANES]
+                )
+        o_ref[m] = s_ref[...].astype(BF)
+
+    for k in range(MEMBERS):
+        build(0, k, pa)
+
+    def step(i, _):
+        group(2 * i, pa, 2 * i + 1, pb)
+        group(2 * i + 1, pb, jnp.minimum(2 * i + 2, 7), pa)
+        return 0
+
+    lax.fori_loop(0, 4, step, 0)
+
+
+def home_forecast(states, weights, mix):
+    cells = MEMBERS * LANES
+    return pl.pallas_call(
+        home_body,
+        out_shape=jax.ShapeDtypeStruct((8, 256, LANES), BF),
+        in_specs=[WHOLE] * 3,
+        out_specs=WHOLE,
+        scratch_shapes=[VM((cells, HOME_DEPTH), BF)] * 2
+        + [VM((cells, TILE), BF)] * 4
+        + [VM((256, LANES), F32)],
+        cost_estimate=pl.CostEstimate(
+            flops=10_000_000_000, bytes_accessed=4_000_000, transcendentals=0
+        ),
+        compiler_params=LIMIT,
+        name="home",
+    )(held(states), stored(weights), stored(mix))
+
+
 def analysis_body(count, slots, a_ref, *refs):
     o_ref = refs[-1]
     for n in range(count):
         f_ref, slot = refs[n], slots[n]
         for q in range(4):
             spans = [slice((q * 8 + 2 * i) * 8, (q * 8 + 2 * i) * 8 + 16) for i in range(4)]
-            got = [[f_ref[m, slot, span, :].astype(F32) for m in range(8)] for span in spans]
+            got = [
+                [f_ref[m, slot * 256 + span.start : slot * 256 + span.stop, :] for m in range(8)]
+                for span in spans
+            ]
+            got = [[v.astype(F32) for v in vs] for vs in got]
             rows = [
                 jnp.concatenate([v[h * 8 : h * 8 + 8] for v in got[i]], axis=0)
                 for i in range(4)
@@ -258,38 +407,22 @@
     for j in range(16):
         place = index_ref[j]
         p = lax.div(place, 4)
-        rows = pl.ds(pl.multiple_of(lax.div(p, 2) * 16, 16), 16)
         odd = lax.rem(p, 2) == 1
         for c, (ref, slot) in chunks.items():
 
             @pl.when(lax.rem(place, 4) == c)
             def _():
+                rows = pl.ds(pl.multiple_of(slot * 256 + lax.div(p, 2) * 16, 16), 16)
                 for m in range(8):
-                    two = ref[m, slot, rows, :].astype(F32)
+                    two = ref[m, rows, :].astype(F32)
                     g_ref[m * 8 : m * 8 + 8, j * LANES : (j + 1) * LANES] = jnp.where(
                         odd, two[8:], two[:8]
                     )
 
 
-def gather_body(where, index_ref, *refs):
-    o_ref = refs[-1]
-    observed_rows(index_ref, {c: (refs[i], slot) for c, i, slot in where}, o_ref)
-
-
-def gather_part(index, where, sources):
-    return pl.pallas_call(
-        functools.partial(gather_body, where),
-        out_shape=jax.ShapeDtypeStruct((64, 2048), F32),
-        in_specs=[pl.BlockSpec(memory_space=pltpu.SMEM)] + [WHOLE] * len(sources),
-        out_specs=WHOLE,
-        compiler_params=LIMIT,
-        name="gather",
-    )(index, *[held(s) for s in sources])
-
-
-def gram_body(where, index_ref, values_ref, precision_ref, so_far_ref, f_ref, o_ref, g_ref):
-    g_ref[...] = so_far_ref[...]
-    observed_rows(index_ref, {c: (f_ref, slot) for c, slot in where}, g_ref)
+def gram_body(where, index_ref, values_ref, precision_ref, *refs):
+    o_ref, g_ref = refs[-2:]
+    observed_rows(index_ref, {c: (refs[i], slot) for c, i, slot in where}, g_ref)
     observed = g_ref[...]
     mean = jnp.sum(observed, axis=0, keepdims=True) * (1.0 / 64)
     spread = observed - mean
@@ -303,22 +436,23 @@
     )
     gram = dot(spread * weight, spread)
     proj = dot(jnp.broadcast_to(weight * (value - mean), (8, 2048)), spread)
-    o_ref[0:32, 0:64] = gram[:32]
-    o_ref[0:32, 64:128] = gram[32:]
-    o_ref[32:40, 0:64] = proj
-    o_ref[32:40, 64:128] = proj
-
-
-def gram_part(index, values, precision, so_far, where, states):
+    for n in range(8):
+        o_ref[n, 0:32, 0:64] = gram[:32]
+        o_ref[n, 0:32, 64:128] = gram[32:]
+        o_ref[n, 32:40, 0:64] = proj
+        o_ref[n, 32:40, 64:128] = proj
+
+
+def gram_part(index, values, precision, where, sources):
     return pl.pallas_call(
         functools.partial(gram_body, where),
-        out_shape=jax.ShapeDtypeStruct((40, LANES), F32),
-        in_specs=[pl.BlockSpec(memory_space=pltpu.SMEM)] + [WHOLE] * 4,
+        out_shape=jax.ShapeDtypeStruct((8, 40, LANES), F32),
+        in_specs=[pl.BlockSpec(memory_space=pltpu.SMEM)] + [WHOLE] * (2 + len(sources)),
         out_specs=WHOLE,
         scratch_shapes=[VM((64, 2048), F32)],
         compiler_params=LIMIT,
         name="gram",
-    )(index, values, precision, so_far, held(states))
+    )(index, values, precision, *[held(s) for s in sources])
 
 
 def place_body(slots, *refs):
@@ -381,36 +515,34 @@
     high = lax.ppermute(prior_realizations[:, :, 0, :], "state", backward)
     edges = jnp.concatenate([low, high], axis=1).astype(F32)
 
-    weights, mix = product_weights(latent_stencil_weights, latent_offset, output_mixing_matrix)
-    combined = transform + mean_weights[:, None]
-    update = (combined + (1.0 - jnp.sum(combined, axis=0)) / 64).T
-    coarse = lax.reduce_precision(update, 8, 7)
-    update = jnp.concatenate([coarse, update - coarse], axis=0).astype(BF)
+    weights, mix, home_weights, home_mix, update = all_weights(
+        latent_stencil_weights, latent_offset, output_mixing_matrix, transform, mean_weights
+    )
     index = obs_index[0, 0]
 
     exchange = functools.partial(
         lax.all_to_all, axis_name="mem", split_axis=0, concat_axis=0, tiled=True
     )
 
-    def forecast(chunks, edges):
-        return forecast_chunks(chunks, prior_realizations, edges, weights, mix)
-
-    x0 = exchange(forecast((0,), edges))
-    x1 = exchange(forecast((1, 2), edges))
-    x2 = exchange(forecast((3,), edges))
-    held4 = analysis_chunks(update, [x0], [0], None, 0, 4)
-    held4 = analysis_chunks(update, [x1], [0], held4, 1, 4)
-    held4 = analysis_chunks(update, [x1], [1], held4, 2, 4)
-    seen = gather_part(index, [(0, 0, 0), (1, 1, 0), (2, 1, 1)], [x0, x1])
-    part = gram_part(index, obs_values[0, 0], obs_precision[0, 0], seen, [(3, 0)], x2)
-    held4 = analysis_chunks(update, [x2], [0], held4, 3, 4)
-    held4, total = lax.optimization_barrier((held4, part))
+    def forecast(chunks, raw):
+        return forecast_chunks(chunks, raw, prior_realizations, edges, weights, mix)
+
+    x0 = exchange(forecast((0,), True))
+    x1 = exchange(forecast((1, 2), False))
+    x2 = home_forecast(x0, home_weights, home_mix)
+    part = gram_part(
+        index,
+        obs_values[0, 0],
+        obs_precision[0, 0],
+        [(0, 0, 0), (1, 1, 0), (2, 1, 1), (3, 2, 0)],
+        [x0, x1, x2],
+    )
+    total = jnp.sum(exchange(part), axis=0)
+    held4 = analysis_chunks(update, [x0, x1, x1, x2], [0, 0, 1, 0], None, 0, 4)
+    held4, total = lax.optimization_barrier((held4, total))
     x4 = exchange(held4)
-    for n in (1, 2, 4):
-        total = sum_over(total, "state", [lambda i: i ^ n])
-    total = sum_over(total, "state", [lambda i, n=n: (i + 8 * n) % 32 for n in range(1, 4)])
-    x4, total = lax.optimization_barrier((x4, total))
-    total = jnp.sum(exchange(jnp.broadcast_to(total[None], (8, *total.shape))), axis=0)
+    for n in (1, 2, 4, 8, 16):
+        total = sum_over(total, "state", [lambda i, n=n: i ^ n])
     analysis = place_chunks(0, [x4], [(0, 0), (0, 1), (0, 2), (0, 3)], None)
     gram = jnp.concatenate([total[:32, :64], total[:32, 64:]], axis=0) / 524288
     proj = total[32, :64] / math.sqrt(524288)

time: 140 us -> 126 us (0.900)
  waiting for transfers between devices: 32.3 us -> 27.1 us
  starting transfers between devices: 36.7 us -> 32.4 us
  Pallas kernels: 62.6 us -> 59.9 us
  other arithmetic: 3.44 us -> 1.21 us
    all_to_all x4 -> x3, waiting for transfers between devices: 12.4 us -> 7.64 us  [the longest x1 3.83 us: shards(): total = jnp.sum(exchange(part), axis=0)]
    all_to_all x1, waiting for transfers between devices: 4.78 us -> 0.57 us  [shards(): x4 = exchange(held4)]
    ppermute x6 -> x5, waiting for transfers between devices: 15.1 us -> 18.9 us  [sum_over(): lax.ppermute(part, axis, [(i, step(i)) for i in range(size)])]
    pallas_call x4 -> x1, Pallas kernels: 4.84 us -> 1.23 us  [analysis_chunks(): pl.pallas_call(functools.partial(analysis_body, count, slots), grid=(1,),...]
    all_to_all x4 -> x3, starting transfers between devices: 16 us -> 12.5 us  [the longest x1 4.8 us: shards(): x1 = exchange(forecast((1, 2), False))]
    unnamed x11 -> x13, local copies, waits for them, and re-layouts: 0.88 us -> 2.8 us
    ppermute x1, starting transfers between devices: 1.92 us -> 3.83 us  [shards(): low = lax.ppermute(prior_realizations[:, :, ROWS - 1, :], 'state', forward)]
    ppermute x1, starting transfers between devices: 7.94 us -> 6.04 us  [shards(): high = lax.ppermute(prior_realizations[:, :, 0, :], 'state', backward)]
  transfers between devices with their start and end apart: 13 -> 11, of which waited for: 10 -> 8; matrix products, arithmetic and copies ran while one was open for 3% -> 2% of each run, Pallas kernels for 33% -> 33%
where the time goes in v3:
time: 126 us; the launch traced here: 125 us
  Pallas kernels  59.9 us (48%)
  starting transfers between devices  32.4 us (26%)
  waiting for transfers between devices  27.1 us (22%)
  local copies, waits for them, and re-layouts  4.01 us (3%)
    pallas_call x2, Pallas kernels, forecast_chunks(): pl.pallas_call(functools.partial(forecast_body, chunks, columns, raw), gr...  38.1 us
    ppermute x5, waiting for transfers between devices, sum_over(): lax.ppermute(part, axis, [(i, step(i)) for i in range(size)])  18.9 us
    pallas_call x1, Pallas kernels, home_forecast(): pl.pallas_call(home_body, out_shape=jax.ShapeDtypeStruct((8, 256, LANES),...  12.1 us
    ppermute x5, starting transfers between devices, sum_over(): lax.ppermute(part, axis, [(i, step(i)) for i in range(size)])  6.45 us
    ppermute x1, starting transfers between devices, shards(): high = lax.ppermute(prior_realizations[:, :, 0, :], 'state', backward)  6.04 us
    all_to_all x1, starting transfers between devices, shards(): x1 = exchange(forecast((1, 2), False))  4.8 us
    all_to_all x1, starting transfers between devices, shards(): x0 = exchange(forecast((0,), True))  4.31 us
    all_to_all x1, waiting for transfers between devices, shards(): total = jnp.sum(exchange(part), axis=0)  3.83 us
  transfers between devices with their start and end apart: 11, of which 8 were waited for; matrix products, arithmetic and copies ran while one was open for 2% of the time, Pallas kernels for 33%

profile of v3, /device:TPU:24, one launch (start us, length us, event | category | flops | bytes accessed | tf_op | source)
XLA Modules:
  0.0 125.4 jit_solution(17283153350563018371)
XLA Ops:
  0.6 1.1 fusion.1
  1.8 3.8 %collective-permute-start = (bf16[8,4,512]{2,1,0:T(4,128)(2,1)S(1)}, bf16[8,4,512]{2,1,0:T(4,128)(2,1)S(1)}, u32[]{:S(2)}, u32[]{:S(2)}) collective-permute-start(bf16[8,4,512]{2,1,0:T(4,128)(2,1)S(1)} %bitcast.16), channel_id=1, source_target_pairs={{0,1},{1,2},{2,3},{3,4},{4,5},{5,6},{6,7},{7,8},{8,9},{9,10},{10,1... | collective-permute-start | bytes 98312 | tf_op jit(solution)/shard_map/ppermute | solution.py:514
  5.7 6.0 %collective-permute-start.1 = (bf16[8,4,512]{2,1,0:T(4,128)(2,1)S(1)}, bf16[8,4,512]{2,1,0:T(4,128)(2,1)S(1)}, u32[]{:S(2)}, u32[]{:S(2)}) collective-permute-start(bf16[8,4,512]{2,1,0:T(4,128)(2,1)S(1)} %bitcast.17), channel_id=1, source_target_pairs={{1,0},{2,1},{3,2},{4,3},{5,4},{6,5},{7,6},{8,7},{9,8},{10,9},{11,1... | collective-permute-start | bytes 98312 | tf_op jit(solution)/shard_map/ppermute | solution.py:515
  11.7 1.4 %copy.12.stencil_ref = bf16[128,36]{1,0:T(8,128)(2,1)} copy(bf16[128,36]{0,1:T(8,128)(2,1)} %param.10) | data formatting | bytes 18432 | tf_op args[1]
  13.1 3.3 %weights.1 = (bf16[224,2176]{1,0:T(8,128)(2,1)}, bf16[2048,64]{1,0:T(8,128)(2,1)}, bf16[128,1152]{1,0:T(8,128)(2,1)}, bf16[1024,32]{1,0:T(8,128)(2,1)}, bf16[128,64]{1,0:T(8,128)(2,1)}) custom-call(bf16[128,36]{1,0:T(8,128)(2,1)} %copy.12.stencil_ref, f32[1,128]{1,0:T(1,128)} %bitcast.18, bf16[4,128]{1,0:T(4,128)(2,1)} %mixing_ref.1, ...), custom_call_target="tpu_custom_call" | custom-call | tf_op jit(solution)/shard_map/weights/pallas_call | solution.py:98
  16.5 13.7 %forecast_0.1 = bf16[8,640,128]{2,1,0:T(8,128)(2,1)} custom-call(f32[8,8,512]{2,1,0:T(8,128)S(1)} %maximum_convert_fusion.edge_ref, bf16[224,2176]{1,0:T(8,128)(2,1)} %get-tuple-element.11.w_ref, bf16[2048,64]{1,0:T(8,128)(2,1)} %get-tuple-element.12.mix_ref, bf16[8,4,64,512]{3,2,1,0:T(8,128)(2,1)} %refs_3_.3, bf16[8,4,64,512]{3,2,1,0:T(8,128)(2,1)} %refs_3_.3, ...), custom_call_target="tpu_custom_call" | custom-call | flops 10000000000 | bytes 4000000 | tf_op jit(solution)/shard_map/forecast_0/pallas_call | solution.py:250
  30.2 4.3 %all-to-all-start = ((bf16[8,640,128]{2,1,0:T(8,128)(2,1)}), bf16[8,640,128]{2,1,0:T(8,128)(2,1)S(1)}, u32[]{:S(2)}, u32[]{:S(2)}) async-start(bf16[8,640,128]{2,1,0:T(8,128)(2,1)} %forecast_0.1), calls=%async_computation | async-start | bytes 2621440 | tf_op jit(solution)/shard_map/all_to_all | solution.py:530
  34.5 24.3 %forecast_1.1 = bf16[8,512,128]{2,1,0:T(8,128)(2,1)} custom-call(f32[8,8,512]{2,1,0:T(8,128)S(1)} %maximum_convert_fusion.edge_ref, bf16[224,2176]{1,0:T(8,128)(2,1)} %get-tuple-element.11.w_ref, bf16[2048,64]{1,0:T(8,128)(2,1)} %get-tuple-element.12.mix_ref, bf16[8,4,64,512]{3,2,1,0:T(8,128)(2,1)} %refs_3_.3, bf16[8,4,64,512]{3,2,1,0:T(8,128)(2,1)} %refs_3_.3, ...), custom_call_target="tpu_custom_call" | custom-call | flops 20000000000 | bytes 4000000 | tf_op jit(solution)/shard_map/forecast_1/pallas_call | solution.py:250
  58.9 4.8 %all-to-all-start.1 = ((bf16[8,512,128]{2,1,0:T(8,128)(2,1)}), bf16[8,512,128]{2,1,0:T(8,128)(2,1)S(1)}, u32[]{:S(2)}, u32[]{:S(2)}) async-start(bf16[8,512,128]{2,1,0:T(8,128)(2,1)} %forecast_1.1), calls=%async_computation.1 | async-start | bytes 2097152 | tf_op jit(solution)/shard_map/all_to_all | solution.py:531
  63.7 12.1 %home.1.refs_3_.refs_2_ = bf16[8,256,128]{2,1,0:T(8,128)(2,1)S(1)} custom-call(bf16[8,640,128]{2,1,0:T(8,128)(2,1)S(1)} %all-to-all-done.x_ref.refs_0_, bf16[128,1152]{1,0:T(8,128)(2,1)} %get-tuple-element.13.w_ref, bf16[1024,32]{1,0:T(8,128)(2,1)} %get-tuple-element.14.mix_ref), custom_call_target="tpu_custom_call" | custom-call | flops 10000000000 | bytes 4000000 | tf_op jit(solution)/shard_map/home/pallas_call | solution.py:343
  75.8 3.8 %all-to-all-done.1.refs_1_.refs_2_ = bf16[8,512,128]{2,1,0:T(8,128)(2,1)S(1)} async-done(((bf16[8,512,128]{2,1,0:T(8,128)(2,1)}), bf16[8,512,128]{2,1,0:T(8,128)(2,1)S(1)}, u32[]{:S(2)}, u32[]{:S(2)}) %all-to-all-start.1) | async-done | bytes 1048608 | tf_op jit(solution)/shard_map/all_to_all | solution.py:531
  79.6 2.8 %gram.1 = f32[8,40,128]{2,1,0:T(8,128)} custom-call(s32[16]{0:T(128)S(1)} %bitcast.15, f32[16,128]{1,0:T(8,128)S(1)} %bitcast.13, f32[16,128]{1,0:T(8,128)S(1)} %bitcast.14, bf16[8,640,128]{2,1,0:T(8,128)(2,1)S(1)} %all-to-all-done.x_ref.refs_0_, bf16[8,512,128]{2,1,0:T(8,128)(2,1)S(1)} %all-to-all-done.1.refs_1_.refs_2_, ...), custom_call_target="tpu_custom_call" | custom-call | tf_op jit(solution)/shard_map/gram/pallas_call | solution.py:447
  82.4 3.4 %all-to-all-start.2 = ((f32[8,40,128]{2,1,0:T(8,128)}), f32[8,40,128]{2,1,0:T(8,128)S(1)}, u32[]{:S(2)}, u32[]{:S(2)}) async-start(f32[8,40,128]{2,1,0:T(8,128)} %gram.1), calls=%async_computation.2 | async-start | bytes 327680 | tf_op jit(solution)/shard_map/all_to_all | solution.py:540
  85.8 1.2 analysis_0.1
  87.1 1.3 %copy-done = bf16[8,4,256,128]{3,2,1,0:T(8,128)(2,1)} copy-done((bf16[8,4,256,128]{3,2,1,0:T(8,128)(2,1)}, bf16[8,4,256,128]{3,2,1,0:T(8,128)(2,1)S(1)}, u32[]{:S(2)}) %copy-start) | copy-done | bytes 2097176
  88.4 3.8 %all-to-all-done.2 = f32[8,40,128]{2,1,0:T(8,128)S(1)} async-done(((f32[8,40,128]{2,1,0:T(8,128)}), f32[8,40,128]{2,1,0:T(8,128)S(1)}, u32[]{:S(2)}, u32[]{:S(2)}) %all-to-all-start.2) | async-done | bytes 163872 | tf_op jit(solution)/shard_map/all_to_all | solution.py:540
  92.2 3.6 %all-to-all-start.3 = ((bf16[8,4,256,128]{3,2,1,0:T(8,128)(2,1)}), bf16[8,4,256,128]{3,2,1,0:T(8,128)(2,1)S(1)}, u32[]{:S(2)}, u32[]{:S(2)}) async-start(bf16[8,4,256,128]{3,2,1,0:T(8,128)(2,1)} %copy-done), calls=%async_computation.3 | async-start | bytes 4194304 | tf_op jit(solution)/shard_map/all_to_all | solution.py:543
  95.9 0.1 collective-permute-start.2
  96.0 3.8 %collective-permute-done.2 = f32[40,128]{1,0:T(8,128)S(1)} collective-permute-done((f32[40,128]{1,0:T(8,128)S(1)}, f32[40,128]{1,0:T(8,128)S(1)}, u32[]{:S(2)}, u32[]{:S(2)}) %collective-permute-start.2) | collective-permute-done | bytes 20512 | tf_op jit(solution)/shard_map/ppermute | solution.py:496
  99.7 0.6 collective-permute-start.3
  100.3 4.1 %collective-permute-done.3 = f32[40,128]{1,0:T(8,128)S(1)} collective-permute-done((f32[40,128]{1,0:T(8,128)S(1)}, f32[40,128]{1,0:T(8,128)S(1)}, u32[]{:S(2)}, u32[]{:S(2)}) %collective-permute-start.3) | collective-permute-done | bytes 20512 | tf_op jit(solution)/shard_map/ppermute | solution.py:496
  104.4 4.4 %collective-permute-start.4 = (f32[40,128]{1,0:T(8,128)S(1)}, f32[40,128]{1,0:T(8,128)S(1)}, u32[]{:S(2)}, u32[]{:S(2)}) collective-permute-start(f32[40,128]{1,0:T(8,128)S(1)} %add.16), channel_id=1, source_target_pairs={{0,4},{1,5},{2,6},{3,7},{4,0},{5,1},{6,2},{7,3},{8,12},{9,13},{10,... | collective-permute-start | bytes 61448 | tf_op jit(solution)/shard_map/ppermute | solution.py:496
  108.8 3.3 %collective-permute-done.4 = f32[40,128]{1,0:T(8,128)S(1)} collective-permute-done((f32[40,128]{1,0:T(8,128)S(1)}, f32[40,128]{1,0:T(8,128)S(1)}, u32[]{:S(2)}, u32[]{:S(2)}) %collective-permute-start.4) | collective-permute-done | bytes 20512 | tf_op jit(solution)/shard_map/ppermute | solution.py:496
  112.1 0.4 collective-permute-start.5
  112.6 3.3 %collective-permute-done.5 = f32[40,128]{1,0:T(8,128)S(1)} collective-permute-done((f32[40,128]{1,0:T(8,128)S(1)}, f32[40,128]{1,0:T(8,128)S(1)}, u32[]{:S(2)}, u32[]{:S(2)}) %collective-permute-start.5) | collective-permute-done | bytes 20512 | tf_op jit(solution)/shard_map/ppermute | solution.py:496
  115.9 0.9 collective-permute-start.6
  116.9 4.3 %collective-permute-done.6 = f32[40,128]{1,0:T(8,128)S(1)} collective-permute-done((f32[40,128]{1,0:T(8,128)S(1)}, f32[40,128]{1,0:T(8,128)S(1)}, u32[]{:S(2)}, u32[]{:S(2)}) %collective-permute-start.6) | collective-permute-done | bytes 20512 | tf_op jit(solution)/shard_map/ppermute | solution.py:496
  121.2 0.1 fusion.2
  121.3 0.6 maximum_multiply_fusion
  121.9 0.5 fusion
  122.4 0.6 all-to-all-done.3.refs_0_
  123.0 2.4 %place_0.1 = bf16[8,4,64,512]{3,2,1,0:T(8,128)(2,1)} custom-call(bf16[8,4,256,128]{3,2,1,0:T(8,128)(2,1)S(1)} %all-to-all-done.3.refs_0_), custom_call_target="tpu_custom_call" | custom-call | tf_op jit(solution)/shard_map/place_0/pallas_call | solution.py:481
  (21 shorter events, 0.1 us)
Async XLA Ops:
  1.8 14.6 %collective-permute-start = (bf16[8,4,512]{2,1,0:T(4,128)(2,1)S(1)}, bf16[8,4,512]{2,1,0:T(4,128)(2,1)S(1)}, u32[]{:S(2)}, u32[]{:S(2)}) collective-permute-start(bf16[8,4,512]{2,1,0:T(4,128)(2,1)S(1)} %bitcast.16), channel_id=1, source_target_pairs={{0,1},{1,2},{2,3},{3,4},{4,5},{5,6},{6,7},{7,8},{8,9},{9,10},{10,1... | collective-permute-start | bytes 98312 | tf_op jit(solution)/shard_map/ppermute | solution.py:514
  5.7 10.8 %collective-permute-start.1 = (bf16[8,4,512]{2,1,0:T(4,128)(2,1)S(1)}, bf16[8,4,512]{2,1,0:T(4,128)(2,1)S(1)}, u32[]{:S(2)}, u32[]{:S(2)}) collective-permute-start(bf16[8,4,512]{2,1,0:T(4,128)(2,1)S(1)} %bitcast.17), channel_id=1, source_target_pairs={{1,0},{2,1},{3,2},{4,3},{5,4},{6,5},{7,6},{8,7},{9,8},{10,9},{11,1... | collective-permute-start | bytes 98312 | tf_op jit(solution)/shard_map/ppermute | solution.py:515
  30.2 28.6 %all-to-all-start = ((bf16[8,640,128]{2,1,0:T(8,128)(2,1)}), bf16[8,640,128]{2,1,0:T(8,128)(2,1)S(1)}, u32[]{:S(2)}, u32[]{:S(2)}) async-start(bf16[8,640,128]{2,1,0:T(8,128)(2,1)} %forecast_0.1), calls=%async_computation | async-start | bytes 2621440 | tf_op jit(solution)/shard_map/all_to_all | solution.py:530
  58.9 20.8 %all-to-all-start.1 = ((bf16[8,512,128]{2,1,0:T(8,128)(2,1)}), bf16[8,512,128]{2,1,0:T(8,128)(2,1)S(1)}, u32[]{:S(2)}, u32[]{:S(2)}) async-start(bf16[8,512,128]{2,1,0:T(8,128)(2,1)} %forecast_1.1), calls=%async_computation.1 | async-start | bytes 2097152 | tf_op jit(solution)/shard_map/all_to_all | solution.py:531
  63.7 16.0 %copy-start.2 = (f32[1,1,16,128]{3,2,1,0:T(8,128)S(1)}, f32[1,1,16,128]{3,2,1,0:T(8,128)}, u32[]{:S(2)}) copy-start(f32[1,1,16,128]{3,2,1,0:T(8,128)} %param.16) | copy-start | bytes 24580
  63.7 16.0 %copy-start.3 = (f32[1,1,16,128]{3,2,1,0:T(8,128)S(1)}, f32[1,1,16,128]{3,2,1,0:T(8,128)}, u32[]{:S(2)}) copy-start(f32[1,1,16,128]{3,2,1,0:T(8,128)} %param.17) | copy-start | bytes 24580
  63.7 16.0 %copy-start.4 = (s32[1,1,16]{2,1,0:T(1,128)S(1)}, s32[1,1,16]{2,1,0:T(1,128)}, u32[]{:S(2)}) copy-start(s32[1,1,16]{2,1,0:T(1,128)} %param.15) | copy-start | bytes 196
  75.8 10.0 %copy-start.1 = (bf16[128,64]{1,0:T(8,128)(2,1)S(1)}, bf16[128,64]{1,0:T(8,128)(2,1)}, u32[]{:S(2)}) copy-start(bf16[128,64]{1,0:T(8,128)(2,1)} %get-tuple-element.10.a_ref) | copy-start | bytes 49156
  82.4 9.8 %all-to-all-start.2 = ((f32[8,40,128]{2,1,0:T(8,128)}), f32[8,40,128]{2,1,0:T(8,128)S(1)}, u32[]{:S(2)}, u32[]{:S(2)}) async-start(f32[8,40,128]{2,1,0:T(8,128)} %gram.1), calls=%async_computation.2 | async-start | bytes 327680 | tf_op jit(solution)/shard_map/all_to_all | solution.py:540
  87.1 1.3 %copy-start = (bf16[8,4,256,128]{3,2,1,0:T(8,128)(2,1)}, bf16[8,4,256,128]{3,2,1,0:T(8,128)(2,1)S(1)}, u32[]{:S(2)}) copy-start(bf16[8,4,256,128]{3,2,1,0:T(8,128)(2,1)S(1)} %analysis_0.1) | copy-start | bytes 6291460
  92.2 30.7 %all-to-all-start.3 = ((bf16[8,4,256,128]{3,2,1,0:T(8,128)(2,1)}), bf16[8,4,256,128]{3,2,1,0:T(8,128)(2,1)S(1)}, u32[]{:S(2)}, u32[]{:S(2)}) async-start(bf16[8,4,256,128]{3,2,1,0:T(8,128)(2,1)} %copy-done), calls=%async_computation.3 | async-start | bytes 4194304 | tf_op jit(solution)/shard_map/all_to_all | solution.py:543
  95.9 3.9 %collective-permute-start.2 = (f32[40,128]{1,0:T(8,128)S(1)}, f32[40,128]{1,0:T(8,128)S(1)}, u32[]{:S(2)}, u32[]{:S(2)}) collective-permute-start(f32[40,128]{1,0:T(8,128)S(1)} %reduce_sum.9), channel_id=1, source_target_pairs={{0,1},{1,0},{2,3},{3,2},{4,5},{5,4},{6,7},{7,6},{8,9},{9,8},{10,11... | collective-permute-start | bytes 61448 | tf_op jit(solution)/shard_map/ppermute | solution.py:496
  99.7 4.7 %collective-permute-start.3 = (f32[40,128]{1,0:T(8,128)S(1)}, f32[40,128]{1,0:T(8,128)S(1)}, u32[]{:S(2)}, u32[]{:S(2)}) collective-permute-start(f32[40,128]{1,0:T(8,128)S(1)} %add.15), channel_id=1, source_target_pairs={{0,2},{1,3},{2,0},{3,1},{4,6},{5,7},{6,4},{7,5},{8,10},{9,11},{10,... | collective-permute-start | bytes 61448 | tf_op jit(solution)/shard_map/ppermute | solution.py:496
  104.4 7.7 %collective-permute-start.4 = (f32[40,128]{1,0:T(8,128)S(1)}, f32[40,128]{1,0:T(8,128)S(1)}, u32[]{:S(2)}, u32[]{:S(2)}) collective-permute-start(f32[40,128]{1,0:T(8,128)S(1)} %add.16), channel_id=1, source_target_pairs={{0,4},{1,5},{2,6},{3,7},{4,0},{5,1},{6,2},{7,3},{8,12},{9,13},{10,... | collective-permute-start | bytes 61448 | tf_op jit(solution)/shard_map/ppermute | solution.py:496
  112.1 3.8 %collective-permute-start.5 = (f32[40,128]{1,0:T(8,128)S(1)}, f32[40,128]{1,0:T(8,128)S(1)}, u32[]{:S(2)}, u32[]{:S(2)}) collective-permute-start(f32[40,128]{1,0:T(8,128)S(1)} %add.17), channel_id=1, source_target_pairs={{0,8},{1,9},{2,10},{3,11},{4,12},{5,13},{6,14},{7,15},{8,0},{9,1},... | collective-permute-start | bytes 61448 | tf_op jit(solution)/shard_map/ppermute | solution.py:496
  115.9 5.3 %collective-permute-start.6 = (f32[40,128]{1,0:T(8,128)S(1)}, f32[40,128]{1,0:T(8,128)S(1)}, u32[]{:S(2)}, u32[]{:S(2)}) collective-permute-start(f32[40,128]{1,0:T(8,128)S(1)} %add.18), channel_id=1, source_target_pairs={{0,16},{1,17},{2,18},{3,19},{4,20},{5,21},{6,22},{7,23},{8,24},{9,... | collective-permute-start | bytes 61448 | tf_op jit(solution)/shard_map/ppermute | solution.py:496

commit v4 on v3

--- a/solution.py
+++ b/solution.py
@@ -45,9 +45,10 @@
     inner, depth = 12 * height, 12 * height + 32
     k = lax.broadcasted_iota(jnp.int32, (depth, LANES), 0)
     j = lax.broadcasted_iota(jnp.int32, (depth, LANES), 1)
-    b, f, row = k // (4 * height), (k // height) % 4, k % height
+    bits = height.bit_length() - 1
+    b, f, row = k >> (bits + 2), (k >> bits) & 3, k & (height - 1)
     edge = k - inner
-    edge_b, below, edge_f = edge // 8, (edge // 4) % 2, edge % 4
+    edge_b, below, edge_f = edge >> 3, (edge >> 2) & 1, edge & 3
     lanes = lax.broadcasted_iota(jnp.int32, (HID, LANES), 1)
     linear = jnp.zeros((depth, LANES), F32)
     width = FIELDS * height
@@ -72,10 +73,21 @@
 
 
 def weights_body(
-    stencil_ref, offset_ref, mixing_ref, transform_ref, mean_ref, w_ref, m_ref, hw_ref, hm_ref, u_ref
+    stencil_ref,
+    offset_ref,
+    mixing_ref,
+    transform_ref,
+    mean_ref,
+    w_ref,
+    m_ref,
+    hw_ref,
+    hm_ref,
+    u_ref,
+    rows_ref,
 ):
-    stencil = 0.5 * stencil_ref[...].astype(F32)
-    rows = jnp.concatenate([stencil, jnp.zeros((HID, LANES - 36), F32)], axis=1).T
+    rows_ref[...] = jnp.zeros_like(rows_ref)
+    rows_ref[:36, :] = 0.5 * stencil_ref[...].astype(F32)
+    rows = rows_ref[...]
     rest = 0.5 * offset_ref[...]
     for i in range(3):
         cut = rest.astype(BF).astype(F32)
@@ -106,22 +118,71 @@
         ),
         in_specs=[WHOLE] * 5,
         out_specs=(WHOLE,) * 5,
+        scratch_shapes=[VM((LANES, HID), F32)],
         compiler_params=LIMIT,
         name="weights",
-    )(*map(stored, (stencil, offset[None], mixing, transform, mean_weights[None])))
-
-
-def forecast_body(chunks, columns, raw, edge_ref, w_ref, mix_ref, *refs):
-    windows, (o_ref, pa, pb, va, vb, ha, hb, s_ref) = refs[: len(columns)], refs[len(columns) :]
-    windows = dict(zip(columns, windows))
+    )(*map(stored, (stencil.T, offset[None], mixing, transform, mean_weights[None])))
+
+
+def forecast_body(chunks, columns, raw, edge_ref, w_ref, mix_ref, x_ref, *refs):
+    o_ref, pa, pb, va, vb, ha, hb, s_ref, window_ref, w_held, mix_held, sems = refs
+    copies = [
+        pltpu.make_async_copy(
+            x_ref.at[:, :, :, c * LANES : (c + 1) * LANES], window_ref.at[i], sems.at[i]
+        )
+        for i, c in enumerate(columns)
+    ]
+    late = weight_copies(w_ref, mix_ref, w_held, mix_held, sems, len(columns))
+    for copy in copies + late:
+        copy.start()
+    for copy in copies:
+        copy.wait()
+    windows = {c: window_ref.at[i] for i, c in enumerate(columns)}
     for slot, c in enumerate(chunks):
         forecast_block(
-            c, slot, windows, raw, edge_ref, w_ref, mix_ref, o_ref, pa, pb, va, vb, ha, hb, s_ref
+            c,
+            slot,
+            windows,
+            raw,
+            late if slot == 0 else [],
+            edge_ref,
+            w_held,
+            mix_held,
+            o_ref,
+            pa,
+            pb,
+            va,
+            vb,
+            ha,
+            hb,
+            s_ref,
         )
 
 
+def weight_copies(w_ref, mix_ref, w_held, mix_held, sems, at):
+    return [
+        pltpu.make_async_copy(w_ref, w_held, sems.at[at]),
+        pltpu.make_async_copy(mix_ref, mix_held, sems.at[at + 1]),
+    ]
+
+
 def forecast_block(
-    c, slot, windows, raw, edge_ref, w_ref, mix_ref, o_ref, pa, pb, va, vb, ha, hb, s_ref
+    c,
+    slot,
+    windows,
+    raw,
+    late,
+    edge_ref,
+    w_ref,
+    mix_ref,
+    o_ref,
+    pa,
+    pb,
+    va,
+    vb,
+    ha,
+    hb,
+    s_ref,
 ):
     lane = lax.broadcasted_iota(jnp.int32, (1, LANES), 1)
     row8 = lax.broadcasted_iota(jnp.int32, (8, LANES), 0)
@@ -133,9 +194,9 @@
         right = read(c + 1) if c < CHUNKS - 1 else jnp.zeros_like(mid)
         last = LANES - 1
         return (
-            jnp.where(lane == 0, pltpu.roll(left, 1, 1), pltpu.roll(mid, 1, 1)),
+            pltpu.roll(jnp.where(lane == last, left, mid), 1, 1),
             mid,
-            jnp.where(lane == last, pltpu.roll(right, last, 1), pltpu.roll(mid, last, 1)),
+            pltpu.roll(jnp.where(lane == 0, right, mid), last, 1),
         )
 
     def block(k, f, g, cc):
@@ -231,6 +292,8 @@
 
     for k in range(MEMBERS):
         build(0, k, pa)
+    for copy in late:
+        copy.wait()
 
     def step(i, _):
         group(2 * i, pa, 2 * i + 1, pb)
@@ -245,26 +308,33 @@
     count = len(chunks)
     low, high = chunks[0] - 1, CHUNKS - 1 if raw else chunks[-1] + 1
     columns = [c for c in range(CHUNKS) if low <= c <= high]
-    window = (MEMBERS, FIELDS, ROWS, LANES)
+    window = (len(columns), MEMBERS, FIELDS, ROWS, LANES)
     shape = (8, count * 256 + raw * MEMBERS * RAW, LANES)
     return pl.pallas_call(
         functools.partial(forecast_body, chunks, columns, raw),
         grid=(1,),
         out_shape=jax.ShapeDtypeStruct(shape, BF),
-        in_specs=[WHOLE] * 3 + [pl.BlockSpec(window, lambda i, c=c: (0, 0, 0, c)) for c in columns],
+        in_specs=[WHOLE] + [pl.BlockSpec(memory_space=pl.ANY)] * 3,
         out_specs=pl.BlockSpec(shape, lambda i: (0, 0, 0)),
         scratch_shapes=[VM((cells, DEPTH), BF)] * 2
         + [VM((cells, TILE), BF)] * 4
-        + [VM((2, 256, LANES), F32)],
+        + [VM((2, 256, LANES), F32), VM(window, BF)]
+        + [VM(weights.shape, BF), VM(mix.shape, BF)]
+        + [pltpu.SemaphoreType.DMA((len(columns) + 2,))],
         cost_estimate=pl.CostEstimate(
             flops=count * 10_000_000_000, bytes_accessed=4_000_000, transcendentals=0
         ),
         compiler_params=LIMIT,
         name=f"forecast_{chunks[0]}",
-    )(edges, stored(weights), stored(mix), *[stored(x)] * len(columns))
-
-
-def home_body(x_ref, w_ref, mix_ref, o_ref, pa, pb, va, vb, ha, hb, s_ref):
+    )(edges, stored(weights), stored(mix), stored(x))
+
+
+def home_body(
+    x_ref, w_given, mix_given, o_ref, pa, pb, va, vb, ha, hb, s_ref, w_ref, mix_ref, sems
+):
+    late = weight_copies(w_given, mix_given, w_ref, mix_ref, sems, 0)
+    for copy in late:
+        copy.start()
     lane = lax.broadcasted_iota(jnp.int32, (1, LANES), 1)
     row8 = lax.broadcasted_iota(jnp.int32, (8, LANES), 0)
     ones = jnp.where(row8 < 3, 1.0, 0.0).astype(F32)
@@ -329,6 +399,8 @@
 
     for k in range(MEMBERS):
         build(0, k, pa)
+    for copy in late:
+        copy.wait()
 
     def step(i, _):
         group(2 * i, pa, 2 * i + 1, pb)
@@ -343,11 +415,12 @@
     return pl.pallas_call(
         home_body,
         out_shape=jax.ShapeDtypeStruct((8, 256, LANES), BF),
-        in_specs=[WHOLE] * 3,
+        in_specs=[WHOLE] + [pl.BlockSpec(memory_space=pl.ANY)] * 2,
         out_specs=WHOLE,
         scratch_shapes=[VM((cells, HOME_DEPTH), BF)] * 2
         + [VM((cells, TILE), BF)] * 4
-        + [VM((256, LANES), F32)],
+        + [VM((256, LANES), F32), VM(weights.shape, BF), VM(mix.shape, BF)]
+        + [pltpu.SemaphoreType.DMA((2,))],
         cost_estimate=pl.CostEstimate(
             flops=10_000_000_000, bytes_accessed=4_000_000, transcendentals=0
         ),
@@ -420,6 +493,11 @@
                     )
 
 
+def in_two(v):
+    coarse = v.astype(BF)
+    return coarse, (v - coarse.astype(F32)).astype(BF)
+
+
 def gram_body(where, index_ref, values_ref, precision_ref, *refs):
     o_ref, g_ref = refs[-2:]
     observed_rows(index_ref, {c: (refs[i], slot) for c, i, slot in where}, g_ref)
@@ -428,14 +506,17 @@
     spread = observed - mean
     weight = jnp.concatenate([precision_ref[j : j + 1, :] for j in range(16)], axis=1)
     value = jnp.concatenate([values_ref[j : j + 1, :] for j in range(16)], axis=1)
-    dot = functools.partial(
-        lax.dot_general,
-        dimension_numbers=(((1,), (1,)), ((), ())),
-        precision=lax.Precision.HIGHEST,
+    left = jnp.broadcast_to(weight * (value - mean), (8, 2048))
+    left = jnp.concatenate([spread * weight, left], axis=0)
+    left, left_rest = in_two(left)
+    right, right_rest = in_two(spread)
+    both = lax.dot_general(
+        jnp.concatenate([left, left, left_rest], axis=1),
+        jnp.concatenate([right, right_rest, right], axis=1),
+        (((1,), (1,)), ((), ())),
         preferred_element_type=F32,
     )
-    gram = dot(spread * weight, spread)
-    proj = dot(jnp.broadcast_to(weight * (value - mean), (8, 2048)), spread)
+    gram, proj = both[:64], both[64:]
     for n in range(8):
         o_ref[n, 0:32, 0:64] = gram[:32]
         o_ref[n, 0:32, 64:128] = gram[32:]

time: 126 us -> 123 us (0.976)
  starting transfers between devices: 32.4 us -> 34 us
  local copies, waits for them, and re-layouts: 4.01 us -> 2.59 us
  waiting for transfers between devices: 27.1 us -> 25.7 us
    ppermute x5, starting transfers between devices: 6.45 us -> 7.95 us  [sum_over(): lax.ppermute(part, axis, [(i, step(i)) for i in range(size)])]
    ppermute x5, waiting for transfers between devices: 18.9 us -> 17.4 us  [sum_over(): lax.ppermute(part, axis, [(i, step(i)) for i in range(size)])]
    unnamed x13 -> x12, local copies, waits for them, and re-layouts: 2.8 us -> 1.37 us
  transfers between devices with their start and end apart: 11 -> 11, of which waited for: 8 -> 8; matrix products, arithmetic and copies ran while one was open for 2% -> 1% of each run, Pallas kernels for 33% -> 33%
where the time goes in v4:
time: 123 us
  Pallas kernels  58.7 us (48%)
  starting transfers between devices  34 us (28%)
  waiting for transfers between devices  25.7 us (21%)
  local copies, waits for them, and re-layouts  2.59 us (2%)
    pallas_call x2, Pallas kernels, forecast_chunks(): pl.pallas_call(functools.partial(forecast_body, chunks, columns, raw), gr...  37.6 us
    ppermute x5, waiting for transfers between devices, sum_over(): lax.ppermute(part, axis, [(i, step(i)) for i in range(size)])  17.4 us
    pallas_call x1, Pallas kernels, home_forecast(): pl.pallas_call(home_body, out_shape=jax.ShapeDtypeStruct((8, 256, LANES),...  12 us
    ppermute x5, starting transfers between devices, sum_over(): lax.ppermute(part, axis, [(i, step(i)) for i in range(size)])  7.95 us
    ppermute x1, starting transfers between devices, shards(): high = lax.ppermute(prior_realizations[:, :, 0, :], 'state', backward)  6.04 us
    all_to_all x1, starting transfers between devices, shards(): x1 = exchange(forecast((1, 2), False))  4.82 us
    all_to_all x1, starting transfers between devices, shards(): x0 = exchange(forecast((0,), True))  4.32 us
    all_to_all x1, waiting for transfers between devices, shards(): x1 = exchange(forecast((1, 2), False))  3.92 us
  transfers between devices with their start and end apart: 11, of which 8 were waited for; matrix products, arithmetic and copies ran while one was open for 1% of the time, Pallas kernels for 33%

profile of v4, /device:TPU:24, one launch (start us, length us, event | category | flops | bytes accessed | tf_op | source)
XLA Modules:
  0.0 122.9 jit_solution(1726404728434467279)
XLA Ops:
  0.6 1.1 fusion.1
  1.8 3.8 %collective-permute-start = (bf16[8,4,512]{2,1,0:T(4,128)(2,1)S(1)}, bf16[8,4,512]{2,1,0:T(4,128)(2,1)S(1)}, u32[]{:S(2)}, u32[]{:S(2)}) collective-permute-start(bf16[8,4,512]{2,1,0:T(4,128)(2,1)S(1)} %bitcast.17), channel_id=1, source_target_pairs={{0,1},{1,2},{2,3},{3,4},{4,5},{5,6},{6,7},{7,8},{8,9},{9,10},{10,1... | collective-permute-start | bytes 98312 | tf_op jit(solution)/shard_map/ppermute | solution.py:595
  5.7 6.0 %collective-permute-start.1 = (bf16[8,4,512]{2,1,0:T(4,128)(2,1)S(1)}, bf16[8,4,512]{2,1,0:T(4,128)(2,1)S(1)}, u32[]{:S(2)}, u32[]{:S(2)}) collective-permute-start(bf16[8,4,512]{2,1,0:T(4,128)(2,1)S(1)} %bitcast.18), channel_id=1, source_target_pairs={{1,0},{2,1},{3,2},{4,3},{5,4},{6,5},{7,6},{8,7},{9,8},{10,9},{11,1... | collective-permute-start | bytes 98312 | tf_op jit(solution)/shard_map/ppermute | solution.py:596
  11.7 3.1 %weights.1 = (bf16[224,2176]{1,0:T(8,128)(2,1)}, bf16[2048,64]{1,0:T(8,128)(2,1)}, bf16[128,1152]{1,0:T(8,128)(2,1)}, bf16[1024,32]{1,0:T(8,128)(2,1)}, bf16[128,64]{1,0:T(8,128)(2,1)}) custom-call(bf16[36,128]{1,0:T(8,128)(2,1)} %bitcast.19, f32[1,128]{1,0:T(1,128)} %bitcast.20, bf16[4,128]{1,0:T(4,128)(2,1)} %mixing_ref.1, f32[64,64]{1,0:T(8,128)} %transform_ref.1, ...), custom_call_target="tpu_custom_call" | custom-call | tf_op jit(solution)/shard_map/weights/pallas_call | solution.py:110
  14.9 13.5 %forecast_0.1 = bf16[8,640,128]{2,1,0:T(8,128)(2,1)} custom-call(f32[8,8,512]{2,1,0:T(8,128)S(1)} %maximum_convert_fusion.edge_ref, bf16[224,2176]{1,0:T(8,128)(2,1)} %get-tuple-element.11.w_ref, bf16[2048,64]{1,0:T(8,128)(2,1)} %get-tuple-element.12.mix_ref, bf16[8,4,64,512]{3,2,1,0:T(8,128)(2,1)} %x_ref.3), custom_call_target="tpu_custom_call" | custom-call | flops 10000000000 | bytes 4000000 | tf_op jit(solution)/shard_map/forecast_0/pallas_call | solution.py:313
  28.4 4.3 %all-to-all-start = ((bf16[8,640,128]{2,1,0:T(8,128)(2,1)}), bf16[8,640,128]{2,1,0:T(8,128)(2,1)S(1)}, u32[]{:S(2)}, u32[]{:S(2)}) async-start(bf16[8,640,128]{2,1,0:T(8,128)(2,1)} %forecast_0.1), calls=%async_computation | async-start | bytes 2621440 | tf_op jit(solution)/shard_map/all_to_all | solution.py:611
  32.7 24.1 %forecast_1.1 = bf16[8,512,128]{2,1,0:T(8,128)(2,1)} custom-call(f32[8,8,512]{2,1,0:T(8,128)S(1)} %maximum_convert_fusion.edge_ref, bf16[224,2176]{1,0:T(8,128)(2,1)} %get-tuple-element.11.w_ref, bf16[2048,64]{1,0:T(8,128)(2,1)} %get-tuple-element.12.mix_ref, bf16[8,4,64,512]{3,2,1,0:T(8,128)(2,1)} %x_ref.3), custom_call_target="tpu_custom_call" | custom-call | flops 20000000000 | bytes 4000000 | tf_op jit(solution)/shard_map/forecast_1/pallas_call | solution.py:313
  56.9 4.8 %all-to-all-start.1 = ((bf16[8,512,128]{2,1,0:T(8,128)(2,1)}), bf16[8,512,128]{2,1,0:T(8,128)(2,1)S(1)}, u32[]{:S(2)}, u32[]{:S(2)}) async-start(bf16[8,512,128]{2,1,0:T(8,128)(2,1)} %forecast_1.1), calls=%async_computation.1 | async-start | bytes 2097152 | tf_op jit(solution)/shard_map/all_to_all | solution.py:612
  61.7 0.0 copy-start.3
  61.7 12.0 %home.1.refs_3_.refs_2_ = bf16[8,256,128]{2,1,0:T(8,128)(2,1)S(1)} custom-call(bf16[8,640,128]{2,1,0:T(8,128)(2,1)S(1)} %all-to-all-done.x_ref.refs_0_, bf16[128,1152]{1,0:T(8,128)(2,1)} %get-tuple-element.13.w_given, bf16[1024,32]{1,0:T(8,128)(2,1)} %get-tuple-element.14.mix_given), custom_call_target="tpu_custom_call" | custom-call | flops 10000000000 | bytes 4000000 | tf_op jit(solution)/shard_map/home/pallas_call | solution.py:415
  73.7 3.9 %all-to-all-done.1.refs_1_.refs_2_ = bf16[8,512,128]{2,1,0:T(8,128)(2,1)S(1)} async-done(((bf16[8,512,128]{2,1,0:T(8,128)(2,1)}), bf16[8,512,128]{2,1,0:T(8,128)(2,1)S(1)}, u32[]{:S(2)}, u32[]{:S(2)}) %all-to-all-start.1) | async-done | bytes 1048608 | tf_op jit(solution)/shard_map/all_to_all | solution.py:612
  77.7 2.3 %gram.1 = f32[8,40,128]{2,1,0:T(8,128)} custom-call(s32[16]{0:T(128)S(1)} %bitcast.16, f32[16,128]{1,0:T(8,128)S(1)} %bitcast.14, f32[16,128]{1,0:T(8,128)S(1)} %bitcast.15, bf16[8,640,128]{2,1,0:T(8,128)(2,1)S(1)} %all-to-all-done.x_ref.refs_0_, bf16[8,512,128]{2,1,0:T(8,128)(2,1)S(1)} %all-to-all-done.1.refs_1_.refs_2_, ...), custom_call_target="tpu_custom_call" | custom-call | tf_op jit(solution)/shard_map/gram/pallas_call | solution.py:528
  80.0 3.4 %all-to-all-start.2 = ((f32[8,40,128]{2,1,0:T(8,128)}), f32[8,40,128]{2,1,0:T(8,128)S(1)}, u32[]{:S(2)}, u32[]{:S(2)}) async-start(f32[8,40,128]{2,1,0:T(8,128)} %gram.1), calls=%async_computation.2 | async-start | bytes 327680 | tf_op jit(solution)/shard_map/all_to_all | solution.py:621
  83.4 1.2 %analysis_0.1 = bf16[8,4,256,128]{3,2,1,0:T(8,128)(2,1)S(1)} custom-call(bf16[128,64]{1,0:T(8,128)(2,1)S(1)} %copy-done.1, bf16[8,640,128]{2,1,0:T(8,128)(2,1)S(1)} %all-to-all-done.x_ref.refs_0_, bf16[8,512,128]{2,1,0:T(8,128)(2,1)S(1)} %all-to-all-done.1.refs_1_.refs_2_, bf16[8,512,128]{2,1,0:T(8,128)(2,1)S(1)} %all-to-all-done.1.refs_1_.refs_2_, ...), custom_call_target="tpu_custom_call" | custom-call | tf_op jit(solution)/shard_map/analysis_0/pallas_call | solution.py:467
  84.6 1.3 %copy-done = bf16[8,4,256,128]{3,2,1,0:T(8,128)(2,1)} copy-done((bf16[8,4,256,128]{3,2,1,0:T(8,128)(2,1)}, bf16[8,4,256,128]{3,2,1,0:T(8,128)(2,1)S(1)}, u32[]{:S(2)}) %copy-start) | copy-done | bytes 2097176
  85.9 3.8 %all-to-all-done.2 = f32[8,40,128]{2,1,0:T(8,128)S(1)} async-done(((f32[8,40,128]{2,1,0:T(8,128)}), f32[8,40,128]{2,1,0:T(8,128)S(1)}, u32[]{:S(2)}, u32[]{:S(2)}) %all-to-all-start.2) | async-done | bytes 163872 | tf_op jit(solution)/shard_map/all_to_all | solution.py:621
  89.8 3.6 %all-to-all-start.3 = ((bf16[8,4,256,128]{3,2,1,0:T(8,128)(2,1)}), bf16[8,4,256,128]{3,2,1,0:T(8,128)(2,1)S(1)}, u32[]{:S(2)}, u32[]{:S(2)}) async-start(bf16[8,4,256,128]{3,2,1,0:T(8,128)(2,1)} %copy-done), calls=%async_computation.3 | async-start | bytes 4194304 | tf_op jit(solution)/shard_map/all_to_all | solution.py:624
  93.4 0.1 collective-permute-start.2
  93.5 3.8 %collective-permute-done.2 = f32[40,128]{1,0:T(8,128)S(1)} collective-permute-done((f32[40,128]{1,0:T(8,128)S(1)}, f32[40,128]{1,0:T(8,128)S(1)}, u32[]{:S(2)}, u32[]{:S(2)}) %collective-permute-start.2) | collective-permute-done | bytes 20512 | tf_op jit(solution)/shard_map/ppermute | solution.py:577
  97.3 2.2 %collective-permute-start.3 = (f32[40,128]{1,0:T(8,128)S(1)}, f32[40,128]{1,0:T(8,128)S(1)}, u32[]{:S(2)}, u32[]{:S(2)}) collective-permute-start(f32[40,128]{1,0:T(8,128)S(1)} %add.15), channel_id=1, source_target_pairs={{0,2},{1,3},{2,0},{3,1},{4,6},{5,7},{6,4},{7,5},{8,10},{9,11},{10,... | collective-permute-start | bytes 61448 | tf_op jit(solution)/shard_map/ppermute | solution.py:577
  99.4 2.5 %collective-permute-done.3 = f32[40,128]{1,0:T(8,128)S(1)} collective-permute-done((f32[40,128]{1,0:T(8,128)S(1)}, f32[40,128]{1,0:T(8,128)S(1)}, u32[]{:S(2)}, u32[]{:S(2)}) %collective-permute-start.3) | collective-permute-done | bytes 20512 | tf_op jit(solution)/shard_map/ppermute | solution.py:577
  102.0 4.4 %collective-permute-start.4 = (f32[40,128]{1,0:T(8,128)S(1)}, f32[40,128]{1,0:T(8,128)S(1)}, u32[]{:S(2)}, u32[]{:S(2)}) collective-permute-start(f32[40,128]{1,0:T(8,128)S(1)} %add.16), channel_id=1, source_target_pairs={{0,4},{1,5},{2,6},{3,7},{4,0},{5,1},{6,2},{7,3},{8,12},{9,13},{10,... | collective-permute-start | bytes 61448 | tf_op jit(solution)/shard_map/ppermute | solution.py:577
  106.3 3.4 %collective-permute-done.4 = f32[40,128]{1,0:T(8,128)S(1)} collective-permute-done((f32[40,128]{1,0:T(8,128)S(1)}, f32[40,128]{1,0:T(8,128)S(1)}, u32[]{:S(2)}, u32[]{:S(2)}) %collective-permute-start.4) | collective-permute-done | bytes 20512 | tf_op jit(solution)/shard_map/ppermute | solution.py:577
  109.7 0.4 collective-permute-start.5
  110.1 3.4 %collective-permute-done.5 = f32[40,128]{1,0:T(8,128)S(1)} collective-permute-done((f32[40,128]{1,0:T(8,128)S(1)}, f32[40,128]{1,0:T(8,128)S(1)}, u32[]{:S(2)}, u32[]{:S(2)}) %collective-permute-start.5) | collective-permute-done | bytes 20512 | tf_op jit(solution)/shard_map/ppermute | solution.py:577
  113.5 0.9 collective-permute-start.6
  114.4 4.4 %collective-permute-done.6 = f32[40,128]{1,0:T(8,128)S(1)} collective-permute-done((f32[40,128]{1,0:T(8,128)S(1)}, f32[40,128]{1,0:T(8,128)S(1)}, u32[]{:S(2)}, u32[]{:S(2)}) %collective-permute-start.6) | collective-permute-done | bytes 20512 | tf_op jit(solution)/shard_map/ppermute | solution.py:577
  118.8 0.1 fusion.2
  118.8 0.6 maximum_multiply_fusion
  119.5 0.5 fusion
  120.0 0.5 all-to-all-done.3.refs_0_
  120.5 2.4 %place_0.1 = bf16[8,4,64,512]{3,2,1,0:T(8,128)(2,1)} custom-call(bf16[8,4,256,128]{3,2,1,0:T(8,128)(2,1)S(1)} %all-to-all-done.3.refs_0_), custom_call_target="tpu_custom_call" | custom-call | tf_op jit(solution)/shard_map/place_0/pallas_call | solution.py:562
  (20 shorter events, 0.1 us)
Async XLA Ops:
  1.8 13.1 %collective-permute-start = (bf16[8,4,512]{2,1,0:T(4,128)(2,1)S(1)}, bf16[8,4,512]{2,1,0:T(4,128)(2,1)S(1)}, u32[]{:S(2)}, u32[]{:S(2)}) collective-permute-start(bf16[8,4,512]{2,1,0:T(4,128)(2,1)S(1)} %bitcast.17), channel_id=1, source_target_pairs={{0,1},{1,2},{2,3},{3,4},{4,5},{5,6},{6,7},{7,8},{8,9},{9,10},{10,1... | collective-permute-start | bytes 98312 | tf_op jit(solution)/shard_map/ppermute | solution.py:595
  5.7 9.2 %collective-permute-start.1 = (bf16[8,4,512]{2,1,0:T(4,128)(2,1)S(1)}, bf16[8,4,512]{2,1,0:T(4,128)(2,1)S(1)}, u32[]{:S(2)}, u32[]{:S(2)}) collective-permute-start(bf16[8,4,512]{2,1,0:T(4,128)(2,1)S(1)} %bitcast.18), channel_id=1, source_target_pairs={{1,0},{2,1},{3,2},{4,3},{5,4},{6,5},{7,6},{8,7},{9,8},{10,9},{11,1... | collective-permute-start | bytes 98312 | tf_op jit(solution)/shard_map/ppermute | solution.py:596
  28.4 28.5 %all-to-all-start = ((bf16[8,640,128]{2,1,0:T(8,128)(2,1)}), bf16[8,640,128]{2,1,0:T(8,128)(2,1)S(1)}, u32[]{:S(2)}, u32[]{:S(2)}) async-start(bf16[8,640,128]{2,1,0:T(8,128)(2,1)} %forecast_0.1), calls=%async_computation | async-start | bytes 2621440 | tf_op jit(solution)/shard_map/all_to_all | solution.py:611
  56.9 20.8 %all-to-all-start.1 = ((bf16[8,512,128]{2,1,0:T(8,128)(2,1)}), bf16[8,512,128]{2,1,0:T(8,128)(2,1)S(1)}, u32[]{:S(2)}, u32[]{:S(2)}) async-start(bf16[8,512,128]{2,1,0:T(8,128)(2,1)} %forecast_1.1), calls=%async_computation.1 | async-start | bytes 2097152 | tf_op jit(solution)/shard_map/all_to_all | solution.py:612
  61.7 16.0 %copy-start.2 = (f32[1,1,16,128]{3,2,1,0:T(8,128)S(1)}, f32[1,1,16,128]{3,2,1,0:T(8,128)}, u32[]{:S(2)}) copy-start(f32[1,1,16,128]{3,2,1,0:T(8,128)} %param.16) | copy-start | bytes 24580
  61.7 16.0 %copy-start.3 = (f32[1,1,16,128]{3,2,1,0:T(8,128)S(1)}, f32[1,1,16,128]{3,2,1,0:T(8,128)}, u32[]{:S(2)}) copy-start(f32[1,1,16,128]{3,2,1,0:T(8,128)} %param.17) | copy-start | bytes 24580
  61.7 16.0 %copy-start.4 = (s32[1,1,16]{2,1,0:T(1,128)S(1)}, s32[1,1,16]{2,1,0:T(1,128)}, u32[]{:S(2)}) copy-start(s32[1,1,16]{2,1,0:T(1,128)} %param.15) | copy-start | bytes 196
  73.7 9.6 %copy-start.1 = (bf16[128,64]{1,0:T(8,128)(2,1)S(1)}, bf16[128,64]{1,0:T(8,128)(2,1)}, u32[]{:S(2)}) copy-start(bf16[128,64]{1,0:T(8,128)(2,1)} %get-tuple-element.10.a_ref) | copy-start | bytes 49156
  80.0 9.8 %all-to-all-start.2 = ((f32[8,40,128]{2,1,0:T(8,128)}), f32[8,40,128]{2,1,0:T(8,128)S(1)}, u32[]{:S(2)}, u32[]{:S(2)}) async-start(f32[8,40,128]{2,1,0:T(8,128)} %gram.1), calls=%async_computation.2 | async-start | bytes 327680 | tf_op jit(solution)/shard_map/all_to_all | solution.py:621
  84.6 1.3 %copy-start = (bf16[8,4,256,128]{3,2,1,0:T(8,128)(2,1)}, bf16[8,4,256,128]{3,2,1,0:T(8,128)(2,1)S(1)}, u32[]{:S(2)}) copy-start(bf16[8,4,256,128]{3,2,1,0:T(8,128)(2,1)S(1)} %analysis_0.1) | copy-start | bytes 6291460
  89.8 30.7 %all-to-all-start.3 = ((bf16[8,4,256,128]{3,2,1,0:T(8,128)(2,1)}), bf16[8,4,256,128]{3,2,1,0:T(8,128)(2,1)S(1)}, u32[]{:S(2)}, u32[]{:S(2)}) async-start(bf16[8,4,256,128]{3,2,1,0:T(8,128)(2,1)} %copy-done), calls=%async_computation.3 | async-start | bytes 4194304 | tf_op jit(solution)/shard_map/all_to_all | solution.py:624
  93.4 3.9 %collective-permute-start.2 = (f32[40,128]{1,0:T(8,128)S(1)}, f32[40,128]{1,0:T(8,128)S(1)}, u32[]{:S(2)}, u32[]{:S(2)}) collective-permute-start(f32[40,128]{1,0:T(8,128)S(1)} %reduce_sum.9), channel_id=1, source_target_pairs={{0,1},{1,0},{2,3},{3,2},{4,5},{5,4},{6,7},{7,6},{8,9},{9,8},{10,11... | collective-permute-start | bytes 61448 | tf_op jit(solution)/shard_map/ppermute | solution.py:577
  97.3 4.7 %collective-permute-start.3 = (f32[40,128]{1,0:T(8,128)S(1)}, f32[40,128]{1,0:T(8,128)S(1)}, u32[]{:S(2)}, u32[]{:S(2)}) collective-permute-start(f32[40,128]{1,0:T(8,128)S(1)} %add.15), channel_id=1, source_target_pairs={{0,2},{1,3},{2,0},{3,1},{4,6},{5,7},{6,4},{7,5},{8,10},{9,11},{10,... | collective-permute-start | bytes 61448 | tf_op jit(solution)/shard_map/ppermute | solution.py:577
  102.0 7.7 %collective-permute-start.4 = (f32[40,128]{1,0:T(8,128)S(1)}, f32[40,128]{1,0:T(8,128)S(1)}, u32[]{:S(2)}, u32[]{:S(2)}) collective-permute-start(f32[40,128]{1,0:T(8,128)S(1)} %add.16), channel_id=1, source_target_pairs={{0,4},{1,5},{2,6},{3,7},{4,0},{5,1},{6,2},{7,3},{8,12},{9,13},{10,... | collective-permute-start | bytes 61448 | tf_op jit(solution)/shard_map/ppermute | solution.py:577
  109.7 3.8 %collective-permute-start.5 = (f32[40,128]{1,0:T(8,128)S(1)}, f32[40,128]{1,0:T(8,128)S(1)}, u32[]{:S(2)}, u32[]{:S(2)}) collective-permute-start(f32[40,128]{1,0:T(8,128)S(1)} %add.17), channel_id=1, source_target_pairs={{0,8},{1,9},{2,10},{3,11},{4,12},{5,13},{6,14},{7,15},{8,0},{9,1},... | collective-permute-start | bytes 61448 | tf_op jit(solution)/shard_map/ppermute | solution.py:577
  113.5 5.3 %collective-permute-start.6 = (f32[40,128]{1,0:T(8,128)S(1)}, f32[40,128]{1,0:T(8,128)S(1)}, u32[]{:S(2)}, u32[]{:S(2)}) collective-permute-start(f32[40,128]{1,0:T(8,128)S(1)} %add.18), channel_id=1, source_target_pairs={{0,16},{1,17},{2,18},{3,19},{4,20},{5,21},{6,22},{7,23},{8,24},{9,... | collective-permute-start | bytes 61448 | tf_op jit(solution)/shard_map/ppermute | solution.py:577

commit v5 on v4

--- a/solution.py
+++ b/solution.py
@@ -23,6 +23,7 @@
 DEPTH = 224
 HOME_DEPTH = 128
 CHUNKS = 4
+OBSERVED = 32 * 8 * 16 * 128
 RAW = 48
 LANES = 128
 TILE = 256
@@ -467,7 +468,7 @@
     return pl.pallas_call(
         functools.partial(analysis_body, count, slots),
         grid=(1,),
-        out_shape=jax.ShapeDtypeStruct((8, total, 256, LANES), BF),
+        out_shape=pltpu.HBM((8, total, 256, LANES), BF),
         in_specs=[WHOLE] * (1 + count) + [pl.BlockSpec(memory_space=pl.ANY)] * len(alias),
         out_specs=pl.BlockSpec((8, count, 256, LANES), lambda i: (0, to // count, 0, 0)),
         input_output_aliases=alias,
@@ -536,40 +537,38 @@
     )(index, values, precision, *[held(s) for s in sources])
 
 
-def place_body(slots, *refs):
-    o_ref, s_ref = refs[-2:]
-    for i, (which, slot) in enumerate(slots):
+def place_body(b_ref, near_ref, far_ref, o_ref, gram_ref, proj_ref, s_ref):
+    for c in range(CHUNKS):
         for m in range(8):
-            s_ref[m] = refs[which][m, slot].astype(F32)
+            s_ref[m] = b_ref[m, c].astype(F32)
         for k in range(MEMBERS):
             for f in range(FIELDS):
                 at = pl.ds(f * 64 + k, 8, stride=8)
                 for half in range(4):
+                    both = [s_ref[2 * half, at, :], s_ref[2 * half + 1, at, :]]
                     o_ref[
-                        k, f, half * 16 : half * 16 + 16, i * LANES : (i + 1) * LANES
-                    ] = jnp.concatenate(
-                        [s_ref[2 * half, at, :], s_ref[2 * half + 1, at, :]], axis=0
-                    ).astype(BF)
-
-
-def place_chunks(at, sources, slots, so_far):
-    given = [held(s) for s in sources]
-    alias = {}
-    if so_far is not None:
-        alias[len(given)] = 0
-        given.append(so_far)
-    wide = len(slots) * LANES
+                        k, f, half * 16 : half * 16 + 16, c * LANES : (c + 1) * LANES
+                    ] = jnp.concatenate(both, axis=0).astype(BF)
+    total = near_ref[...] + far_ref[...]
+    gram_ref[:32, :] = total[:32, :64] * (1.0 / OBSERVED)
+    gram_ref[32:, :] = total[:32, 64:] * (1.0 / OBSERVED)
+    proj_ref[...] = total[32:33, :64] * (1.0 / math.sqrt(OBSERVED))
+
+
+def place(back, near, far):
     return pl.pallas_call(
-        functools.partial(place_body, slots),
-        grid=(1,),
-        out_shape=jax.ShapeDtypeStruct((MEMBERS, FIELDS, ROWS, COLS), BF),
-        in_specs=[WHOLE] * len(sources) + [pl.BlockSpec(memory_space=pl.ANY)] * len(alias),
-        out_specs=pl.BlockSpec((MEMBERS, FIELDS, ROWS, wide), lambda i: (0, 0, 0, at)),
+        place_body,
+        out_shape=(
+            jax.ShapeDtypeStruct((MEMBERS, FIELDS, ROWS, COLS), BF),
+            jax.ShapeDtypeStruct((64, 64), F32),
+            jax.ShapeDtypeStruct((1, 64), F32),
+        ),
+        in_specs=[WHOLE] * 3,
+        out_specs=(WHOLE,) * 3,
         scratch_shapes=[VM((8, 256, LANES), F32)],
-        input_output_aliases=alias,
         compiler_params=LIMIT,
-        name=f"place_{at}",
-    )(*given)
+        name="place",
+    )(held(back), near, far)
 
 
 def sum_over(part, axis, steps):
@@ -622,12 +621,11 @@
     held4 = analysis_chunks(update, [x0, x1, x1, x2], [0, 0, 1, 0], None, 0, 4)
     held4, total = lax.optimization_barrier((held4, total))
     x4 = exchange(held4)
-    for n in (1, 2, 4, 8, 16):
+    for n in (1, 2, 4, 8):
         total = sum_over(total, "state", [lambda i, n=n: i ^ n])
-    analysis = place_chunks(0, [x4], [(0, 0), (0, 1), (0, 2), (0, 3)], None)
-    gram = jnp.concatenate([total[:32, :64], total[:32, 64:]], axis=0) / 524288
-    proj = total[32, :64] / math.sqrt(524288)
-    return (analysis, gram, proj)
+    far = lax.ppermute(total, "state", [(i, i ^ 16) for i in range(count)])
+    analysis, gram, proj = place(x4, total, far)
+    return (analysis, gram, proj.reshape(64))
 
 
 def solution(mesh):

time: 123 us -> 123 us (level)
    ppermute x0 -> x1, waiting for transfers between devices: none -> 4.41 us  [shards(): far = lax.ppermute(total, 'state', [(i, i ^ 16) for i in range(count)])]
    ppermute x5 -> x4, waiting for transfers between devices: 17.4 us -> 13 us  [sum_over(): lax.ppermute(part, axis, [(i, step(i)) for i in range(size)])]
    pallas_call x1, Pallas kernels: 1.23 us -> 2.55 us  [analysis_chunks(): pl.pallas_call(functools.partial(analysis_body, count, slots), grid=(1,),...]
    ppermute x5 -> x4, starting transfers between devices: 7.95 us -> 7.08 us  [sum_over(): lax.ppermute(part, axis, [(i, step(i)) for i in range(size)])]
  transfers between devices with their start and end apart: 11 -> 11, of which waited for: 8 -> 8; matrix products, arithmetic and copies ran while one was open for 1% -> 0% of each run, Pallas kernels for 33% -> 33%
where the time goes in v5:
time: 123 us
  Pallas kernels  59 us (48%)
  starting transfers between devices  33.9 us (28%)
  waiting for transfers between devices  26.9 us (22%)
  local copies, waits for them, and re-layouts  2.19 us (2%)
    pallas_call x2, Pallas kernels, forecast_chunks(): pl.pallas_call(functools.partial(forecast_body, chunks, columns, raw), gr...  36.6 us
    ppermute x4, waiting for transfers between devices, sum_over(): lax.ppermute(part, axis, [(i, step(i)) for i in range(size)])  13 us
    pallas_call x1, Pallas kernels, home_forecast(): pl.pallas_call(home_body, out_shape=jax.ShapeDtypeStruct((8, 256, LANES),...  12 us
    ppermute x4, starting transfers between devices, sum_over(): lax.ppermute(part, axis, [(i, step(i)) for i in range(size)])  7.08 us
    ppermute x1, starting transfers between devices, shards(): high = lax.ppermute(prior_realizations[:, :, 0, :], 'state', backward)  6.04 us
    all_to_all x1, starting transfers between devices, shards(): x1 = exchange(forecast((1, 2), False))  4.79 us
    ppermute x1, waiting for transfers between devices, shards(): far = lax.ppermute(total, 'state', [(i, i ^ 16) for i in range(count)])  4.41 us
    all_to_all x1, starting transfers between devices, shards(): x0 = exchange(forecast((0,), True))  4.32 us
  transfers between devices with their start and end apart: 11, of which 8 were waited for; matrix products, arithmetic and copies ran while one was open for 0% of the time, Pallas kernels for 33%

profile of v5, /device:TPU:24, one launch (start us, length us, event | category | flops | bytes accessed | tf_op | source)
XLA Modules:
  0.0 122.9 jit_solution(2794531103383283377)
XLA Ops:
  0.6 1.1 fusion
  1.8 3.8 %collective-permute-start = (bf16[8,4,512]{2,1,0:T(4,128)(2,1)S(1)}, bf16[8,4,512]{2,1,0:T(4,128)(2,1)S(1)}, u32[]{:S(2)}, u32[]{:S(2)}) collective-permute-start(bf16[8,4,512]{2,1,0:T(4,128)(2,1)S(1)} %bitcast.16), channel_id=1, source_target_pairs={{0,1},{1,2},{2,3},{3,4},{4,5},{5,6},{6,7},{7,8},{8,9},{9,10},{10,1... | collective-permute-start | bytes 98312 | tf_op jit(solution)/shard_map/ppermute | solution.py:594
  5.7 6.0 %collective-permute-start.1 = (bf16[8,4,512]{2,1,0:T(4,128)(2,1)S(1)}, bf16[8,4,512]{2,1,0:T(4,128)(2,1)S(1)}, u32[]{:S(2)}, u32[]{:S(2)}) collective-permute-start(bf16[8,4,512]{2,1,0:T(4,128)(2,1)S(1)} %bitcast.17), channel_id=1, source_target_pairs={{1,0},{2,1},{3,2},{4,3},{5,4},{6,5},{7,6},{8,7},{9,8},{10,9},{11,1... | collective-permute-start | bytes 98312 | tf_op jit(solution)/shard_map/ppermute | solution.py:595
  11.7 3.1 %weights.1 = (bf16[224,2176]{1,0:T(8,128)(2,1)}, bf16[2048,64]{1,0:T(8,128)(2,1)}, bf16[128,1152]{1,0:T(8,128)(2,1)}, bf16[1024,32]{1,0:T(8,128)(2,1)}, bf16[128,64]{1,0:T(8,128)(2,1)}) custom-call(bf16[36,128]{1,0:T(8,128)(2,1)} %bitcast.18, f32[1,128]{1,0:T(1,128)} %bitcast.19, bf16[4,128]{1,0:T(4,128)(2,1)} %mixing_ref.1, f32[64,64]{1,0:T(8,128)} %transform_ref.1, ...), custom_call_target="tpu_custom_call" | custom-call | tf_op jit(solution)/shard_map/weights/pallas_call | solution.py:111
  14.8 0.0 collective-permute-done.1
  14.9 13.5 %forecast_0.1 = bf16[8,640,128]{2,1,0:T(8,128)(2,1)} custom-call(f32[8,8,512]{2,1,0:T(8,128)S(1)} %maximum_convert_fusion.edge_ref, bf16[224,2176]{1,0:T(8,128)(2,1)} %get-tuple-element.14.w_ref, bf16[2048,64]{1,0:T(8,128)(2,1)} %get-tuple-element.15.mix_ref, bf16[8,4,64,512]{3,2,1,0:T(8,128)(2,1)} %x_ref.3), custom_call_target="tpu_custom_call" | custom-call | flops 10000000000 | bytes 4000000 | tf_op jit(solution)/shard_map/forecast_0/pallas_call | solution.py:314
  28.4 4.3 %all-to-all-start = ((bf16[8,640,128]{2,1,0:T(8,128)(2,1)}), bf16[8,640,128]{2,1,0:T(8,128)(2,1)S(1)}, u32[]{:S(2)}, u32[]{:S(2)}) async-start(bf16[8,640,128]{2,1,0:T(8,128)(2,1)} %forecast_0.1), calls=%async_computation | async-start | bytes 2621440 | tf_op jit(solution)/shard_map/all_to_all | solution.py:610
  32.7 23.1 %forecast_1.1 = bf16[8,512,128]{2,1,0:T(8,128)(2,1)S(1)} custom-call(f32[8,8,512]{2,1,0:T(8,128)S(1)} %maximum_convert_fusion.edge_ref, bf16[224,2176]{1,0:T(8,128)(2,1)} %get-tuple-element.14.w_ref, bf16[2048,64]{1,0:T(8,128)(2,1)} %get-tuple-element.15.mix_ref, bf16[8,4,64,512]{3,2,1,0:T(8,128)(2,1)} %x_ref.3), custom_call_target="tpu_custom_call" | custom-call | flops 20000000000 | bytes 4000000 | tf_op jit(solution)/shard_map/forecast_1/pallas_call | solution.py:314
  55.8 1.0 copy-done
  56.8 4.8 %all-to-all-start.1 = ((bf16[8,512,128]{2,1,0:T(8,128)(2,1)}), bf16[8,512,128]{2,1,0:T(8,128)(2,1)S(1)}, u32[]{:S(2)}, u32[]{:S(2)}) async-start(bf16[8,512,128]{2,1,0:T(8,128)(2,1)} %copy-done), calls=%async_computation.1 | async-start | bytes 2097152 | tf_op jit(solution)/shard_map/all_to_all | solution.py:611
  61.6 0.0 copy-start.3
  61.6 0.0 copy-start.4
  61.6 12.0 %home.1.refs_3_.refs_2_ = bf16[8,256,128]{2,1,0:T(8,128)(2,1)S(1)} custom-call(bf16[8,640,128]{2,1,0:T(8,128)(2,1)S(1)} %all-to-all-done.x_ref.refs_0_, bf16[128,1152]{1,0:T(8,128)(2,1)} %get-tuple-element.16.w_given, bf16[1024,32]{1,0:T(8,128)(2,1)} %get-tuple-element.17.mix_given), custom_call_target="tpu_custom_call" | custom-call | flops 10000000000 | bytes 4000000 | tf_op jit(solution)/shard_map/home/pallas_call | solution.py:416
  73.6 0.0 copy-start.1
  73.7 3.9 %all-to-all-done.1.refs_1_.refs_2_ = bf16[8,512,128]{2,1,0:T(8,128)(2,1)S(1)} async-done(((bf16[8,512,128]{2,1,0:T(8,128)(2,1)}), bf16[8,512,128]{2,1,0:T(8,128)(2,1)S(1)}, u32[]{:S(2)}, u32[]{:S(2)}) %all-to-all-start.1) | async-done | bytes 1048608 | tf_op jit(solution)/shard_map/all_to_all | solution.py:611
  77.6 2.3 %gram.1 = f32[8,40,128]{2,1,0:T(8,128)} custom-call(s32[16]{0:T(128)S(1)} %bitcast.15, f32[16,128]{1,0:T(8,128)S(1)} %bitcast.13, f32[16,128]{1,0:T(8,128)S(1)} %bitcast.14, bf16[8,640,128]{2,1,0:T(8,128)(2,1)S(1)} %all-to-all-done.x_ref.refs_0_, bf16[8,512,128]{2,1,0:T(8,128)(2,1)S(1)} %all-to-all-done.1.refs_1_.refs_2_, ...), custom_call_target="tpu_custom_call" | custom-call | tf_op jit(solution)/shard_map/gram/pallas_call | solution.py:529
  79.9 3.4 %all-to-all-start.2 = ((f32[8,40,128]{2,1,0:T(8,128)}), f32[8,40,128]{2,1,0:T(8,128)S(1)}, u32[]{:S(2)}, u32[]{:S(2)}) async-start(f32[8,40,128]{2,1,0:T(8,128)} %gram.1), calls=%async_computation.2 | async-start | bytes 327680 | tf_op jit(solution)/shard_map/all_to_all | solution.py:620
  83.3 2.6 %analysis_0.1 = bf16[8,4,256,128]{3,2,1,0:T(8,128)(2,1)} custom-call(bf16[128,64]{1,0:T(8,128)(2,1)S(1)} %copy-done.1, bf16[8,640,128]{2,1,0:T(8,128)(2,1)S(1)} %all-to-all-done.x_ref.refs_0_, bf16[8,512,128]{2,1,0:T(8,128)(2,1)S(1)} %all-to-all-done.1.refs_1_.refs_2_, bf16[8,512,128]{2,1,0:T(8,128)(2,1)S(1)} %all-to-all-done.1.refs_1_.refs_2_, ...), custom_call_target="tpu_custom_call" | custom-call | tf_op jit(solution)/shard_map/analysis_0/pallas_call | solution.py:468
  85.8 3.8 %all-to-all-done.2 = f32[8,40,128]{2,1,0:T(8,128)S(1)} async-done(((f32[8,40,128]{2,1,0:T(8,128)}), f32[8,40,128]{2,1,0:T(8,128)S(1)}, u32[]{:S(2)}, u32[]{:S(2)}) %all-to-all-start.2) | async-done | bytes 163872 | tf_op jit(solution)/shard_map/all_to_all | solution.py:620
  89.7 3.6 %all-to-all-start.3 = ((bf16[8,4,256,128]{3,2,1,0:T(8,128)(2,1)}), bf16[8,4,256,128]{3,2,1,0:T(8,128)(2,1)S(1)}, u32[]{:S(2)}, u32[]{:S(2)}) async-start(bf16[8,4,256,128]{3,2,1,0:T(8,128)(2,1)} %analysis_0.1), calls=%async_computation.3 | async-start | bytes 4194304 | tf_op jit(solution)/shard_map/all_to_all | solution.py:623
  93.3 0.1 collective-permute-start.2
  93.4 3.8 %collective-permute-done.2 = f32[40,128]{1,0:T(8,128)S(1)} collective-permute-done((f32[40,128]{1,0:T(8,128)S(1)}, f32[40,128]{1,0:T(8,128)S(1)}, u32[]{:S(2)}, u32[]{:S(2)}) %collective-permute-start.2) | collective-permute-done | bytes 20512 | tf_op jit(solution)/shard_map/ppermute | solution.py:576
  97.2 2.2 %collective-permute-start.3 = (f32[40,128]{1,0:T(8,128)S(1)}, f32[40,128]{1,0:T(8,128)S(1)}, u32[]{:S(2)}, u32[]{:S(2)}) collective-permute-start(f32[40,128]{1,0:T(8,128)S(1)} %add.12), channel_id=1, source_target_pairs={{0,2},{1,3},{2,0},{3,1},{4,6},{5,7},{6,4},{7,5},{8,10},{9,11},{10,... | collective-permute-start | bytes 61448 | tf_op jit(solution)/shard_map/ppermute | solution.py:576
  99.4 2.5 %collective-permute-done.3 = f32[40,128]{1,0:T(8,128)S(1)} collective-permute-done((f32[40,128]{1,0:T(8,128)S(1)}, f32[40,128]{1,0:T(8,128)S(1)}, u32[]{:S(2)}, u32[]{:S(2)}) %collective-permute-start.3) | collective-permute-done | bytes 20512 | tf_op jit(solution)/shard_map/ppermute | solution.py:576
  101.9 4.4 %collective-permute-start.4 = (f32[40,128]{1,0:T(8,128)S(1)}, f32[40,128]{1,0:T(8,128)S(1)}, u32[]{:S(2)}, u32[]{:S(2)}) collective-permute-start(f32[40,128]{1,0:T(8,128)S(1)} %add.13), channel_id=1, source_target_pairs={{0,4},{1,5},{2,6},{3,7},{4,0},{5,1},{6,2},{7,3},{8,12},{9,13},{10,... | collective-permute-start | bytes 61448 | tf_op jit(solution)/shard_map/ppermute | solution.py:576
  106.3 3.4 %collective-permute-done.4 = f32[40,128]{1,0:T(8,128)S(1)} collective-permute-done((f32[40,128]{1,0:T(8,128)S(1)}, f32[40,128]{1,0:T(8,128)S(1)}, u32[]{:S(2)}, u32[]{:S(2)}) %collective-permute-start.4) | collective-permute-done | bytes 20512 | tf_op jit(solution)/shard_map/ppermute | solution.py:576
  109.7 0.4 collective-permute-start.5
  110.0 3.4 %collective-permute-done.5 = f32[40,128]{1,0:T(8,128)S(1)} collective-permute-done((f32[40,128]{1,0:T(8,128)S(1)}, f32[40,128]{1,0:T(8,128)S(1)}, u32[]{:S(2)}, u32[]{:S(2)}) %collective-permute-start.5) | collective-permute-done | bytes 20512 | tf_op jit(solution)/shard_map/ppermute | solution.py:576
  113.5 0.9 collective-permute-start.6
  114.3 4.4 %collective-permute-done.6.far_ref = f32[40,128]{1,0:T(8,128)S(1)} collective-permute-done((f32[40,128]{1,0:T(8,128)S(1)}, f32[40,128]{1,0:T(8,128)S(1)}, u32[]{:S(2)}, u32[]{:S(2)}) %collective-permute-start.6) | collective-permute-done | bytes 20512 | tf_op jit(solution)/shard_map/ppermute | solution.py:626
  118.7 1.7 %all-to-all-done.3.b_ref = bf16[8,4,256,128]{3,2,1,0:T(8,128)(2,1)S(1)} async-done(((bf16[8,4,256,128]{3,2,1,0:T(8,128)(2,1)}), bf16[8,4,256,128]{3,2,1,0:T(8,128)(2,1)S(1)}, u32[]{:S(2)}, u32[]{:S(2)}) %all-to-all-start.3) | async-done | bytes 2097184 | tf_op jit(solution)/shard_map/all_to_all | solution.py:623
  120.4 2.4 %place.1 = (bf16[8,4,64,512]{3,2,1,0:T(8,128)(2,1)}, f32[64,64]{1,0:T(8,128)}, f32[1,64]{1,0:T(1,128)}) custom-call(bf16[8,4,256,128]{3,2,1,0:T(8,128)(2,1)S(1)} %all-to-all-done.3.b_ref, f32[40,128]{1,0:T(8,128)S(1)} %add.15.near_ref, f32[40,128]{1,0:T(8,128)S(1)} %collective-permute-done.6.far_ref), custom_call_target="tpu_custom_call" | custom-call | tf_op jit(solution)/shard_map/place/pallas_call | solution.py:559
  (16 shorter events, 0.1 us)
Async XLA Ops:
  1.8 13.0 %collective-permute-start = (bf16[8,4,512]{2,1,0:T(4,128)(2,1)S(1)}, bf16[8,4,512]{2,1,0:T(4,128)(2,1)S(1)}, u32[]{:S(2)}, u32[]{:S(2)}) collective-permute-start(bf16[8,4,512]{2,1,0:T(4,128)(2,1)S(1)} %bitcast.16), channel_id=1, source_target_pairs={{0,1},{1,2},{2,3},{3,4},{4,5},{5,6},{6,7},{7,8},{8,9},{9,10},{10,1... | collective-permute-start | bytes 98312 | tf_op jit(solution)/shard_map/ppermute | solution.py:594
  5.7 9.2 %collective-permute-start.1 = (bf16[8,4,512]{2,1,0:T(4,128)(2,1)S(1)}, bf16[8,4,512]{2,1,0:T(4,128)(2,1)S(1)}, u32[]{:S(2)}, u32[]{:S(2)}) collective-permute-start(bf16[8,4,512]{2,1,0:T(4,128)(2,1)S(1)} %bitcast.17), channel_id=1, source_target_pairs={{1,0},{2,1},{3,2},{4,3},{5,4},{6,5},{7,6},{8,7},{9,8},{10,9},{11,1... | collective-permute-start | bytes 98312 | tf_op jit(solution)/shard_map/ppermute | solution.py:595
  28.4 28.5 %all-to-all-start = ((bf16[8,640,128]{2,1,0:T(8,128)(2,1)}), bf16[8,640,128]{2,1,0:T(8,128)(2,1)S(1)}, u32[]{:S(2)}, u32[]{:S(2)}) async-start(bf16[8,640,128]{2,1,0:T(8,128)(2,1)} %forecast_0.1), calls=%async_computation | async-start | bytes 2621440 | tf_op jit(solution)/shard_map/all_to_all | solution.py:610
  55.8 1.0 copy-start
  56.8 20.8 %all-to-all-start.1 = ((bf16[8,512,128]{2,1,0:T(8,128)(2,1)}), bf16[8,512,128]{2,1,0:T(8,128)(2,1)S(1)}, u32[]{:S(2)}, u32[]{:S(2)}) async-start(bf16[8,512,128]{2,1,0:T(8,128)(2,1)} %copy-done), calls=%async_computation.1 | async-start | bytes 2097152 | tf_op jit(solution)/shard_map/all_to_all | solution.py:611
  61.6 16.0 %copy-start.2 = (f32[1,1,16,128]{3,2,1,0:T(8,128)S(1)}, f32[1,1,16,128]{3,2,1,0:T(8,128)}, u32[]{:S(2)}) copy-start(f32[1,1,16,128]{3,2,1,0:T(8,128)} %param.16) | copy-start | bytes 24580
  61.6 16.0 %copy-start.3 = (f32[1,1,16,128]{3,2,1,0:T(8,128)S(1)}, f32[1,1,16,128]{3,2,1,0:T(8,128)}, u32[]{:S(2)}) copy-start(f32[1,1,16,128]{3,2,1,0:T(8,128)} %param.17) | copy-start | bytes 24580
  61.6 16.0 %copy-start.4 = (s32[1,1,16]{2,1,0:T(1,128)S(1)}, s32[1,1,16]{2,1,0:T(1,128)}, u32[]{:S(2)}) copy-start(s32[1,1,16]{2,1,0:T(1,128)} %param.15) | copy-start | bytes 196
  73.6 9.6 %copy-start.1 = (bf16[128,64]{1,0:T(8,128)(2,1)S(1)}, bf16[128,64]{1,0:T(8,128)(2,1)}, u32[]{:S(2)}) copy-start(bf16[128,64]{1,0:T(8,128)(2,1)} %get-tuple-element.13.a_ref) | copy-start | bytes 49156
  79.9 9.8 %all-to-all-start.2 = ((f32[8,40,128]{2,1,0:T(8,128)}), f32[8,40,128]{2,1,0:T(8,128)S(1)}, u32[]{:S(2)}, u32[]{:S(2)}) async-start(f32[8,40,128]{2,1,0:T(8,128)} %gram.1), calls=%async_computation.2 | async-start | bytes 327680 | tf_op jit(solution)/shard_map/all_to_all | solution.py:620
  89.7 30.7 %all-to-all-start.3 = ((bf16[8,4,256,128]{3,2,1,0:T(8,128)(2,1)}), bf16[8,4,256,128]{3,2,1,0:T(8,128)(2,1)S(1)}, u32[]{:S(2)}, u32[]{:S(2)}) async-start(bf16[8,4,256,128]{3,2,1,0:T(8,128)(2,1)} %analysis_0.1), calls=%async_computation.3 | async-start | bytes 4194304 | tf_op jit(solution)/shard_map/all_to_all | solution.py:623
  93.3 3.9 %collective-permute-start.2 = (f32[40,128]{1,0:T(8,128)S(1)}, f32[40,128]{1,0:T(8,128)S(1)}, u32[]{:S(2)}, u32[]{:S(2)}) collective-permute-start(f32[40,128]{1,0:T(8,128)S(1)} %reduce_sum.9), channel_id=1, source_target_pairs={{0,1},{1,0},{2,3},{3,2},{4,5},{5,4},{6,7},{7,6},{8,9},{9,8},{10,11... | collective-permute-start | bytes 61448 | tf_op jit(solution)/shard_map/ppermute | solution.py:576
  97.2 4.7 %collective-permute-start.3 = (f32[40,128]{1,0:T(8,128)S(1)}, f32[40,128]{1,0:T(8,128)S(1)}, u32[]{:S(2)}, u32[]{:S(2)}) collective-permute-start(f32[40,128]{1,0:T(8,128)S(1)} %add.12), channel_id=1, source_target_pairs={{0,2},{1,3},{2,0},{3,1},{4,6},{5,7},{6,4},{7,5},{8,10},{9,11},{10,... | collective-permute-start | bytes 61448 | tf_op jit(solution)/shard_map/ppermute | solution.py:576
  101.9 7.8 %collective-permute-start.4 = (f32[40,128]{1,0:T(8,128)S(1)}, f32[40,128]{1,0:T(8,128)S(1)}, u32[]{:S(2)}, u32[]{:S(2)}) collective-permute-start(f32[40,128]{1,0:T(8,128)S(1)} %add.13), channel_id=1, source_target_pairs={{0,4},{1,5},{2,6},{3,7},{4,0},{5,1},{6,2},{7,3},{8,12},{9,13},{10,... | collective-permute-start | bytes 61448 | tf_op jit(solution)/shard_map/ppermute | solution.py:576
  109.7 3.8 %collective-permute-start.5 = (f32[40,128]{1,0:T(8,128)S(1)}, f32[40,128]{1,0:T(8,128)S(1)}, u32[]{:S(2)}, u32[]{:S(2)}) collective-permute-start(f32[40,128]{1,0:T(8,128)S(1)} %add.14), channel_id=1, source_target_pairs={{0,8},{1,9},{2,10},{3,11},{4,12},{5,13},{6,14},{7,15},{8,0},{9,1},... | collective-permute-start | bytes 61448 | tf_op jit(solution)/shard_map/ppermute | solution.py:576
  113.5 5.3 %collective-permute-start.6 = (f32[40,128]{1,0:T(8,128)S(1)}, f32[40,128]{1,0:T(8,128)S(1)}, u32[]{:S(2)}, u32[]{:S(2)}) collective-permute-start(f32[40,128]{1,0:T(8,128)S(1)} %add.15.near_ref), channel_id=1, source_target_pairs={{0,16},{1,17},{2,18},{3,19},{4,20},{5,21},{6,22},{7,23},{8,24},{9,... | collective-permute-start | bytes 61448 | tf_op jit(solution)/shard_map/ppermute | solution.py:626
